TPU v7x, 32 devices: a whole 2x2x4 slice. The times are simulated.
32 devices in a mesh: section: 2 (over core), grp: 4 (over y, x), dp: 4 (over z).
Axes of the slice: x: 2, y: 2, z: 4, core: 2. Of those that a mesh axis runs over, the one named last changes fastest.
Arguments:
- boundary: bfloat16 [2, 2, 16, 128, 2048], P('section', None, ('grp', 'dp')), may hold values from -6 to 6
- doc_lengths: int32 [2, 16, 3], P(None, ('grp', 'dp')), may hold values from 1 to 64, as said below
- norm_gain: bfloat16 [2, 2048], P('section', 'dp'), may hold values from 0.5 to 1.5
- in_weight: bfloat16 [2, 2048, 8192], P('section', 'dp'), may hold values from -0.125 to 0.125
- conv_weight: bfloat16 [2, 4, 4096], P('section', None, 'dp'), may hold values from -3 to 3
- conv_bias: bfloat16 [2, 4096], P('section', 'dp'), may hold values from -3 to 3
- down_weight: bfloat16 [2, 4096, 128], P('section', 'dp'), may hold values from -0.09375 to 0.09375
- kq_weight: bfloat16 [2, 32, 4096], P('section', None, 'dp'), may hold values from -0.09375 to 0.09375
- dt_weight: bfloat16 [2, 128, 4096], P('section', None, 'dp'), may hold values from -0.5 to 0.5
- dt_bias: bfloat16 [2, 4096], P('section', 'dp'), may hold values from -3 to 1
- skip_weight: bfloat16 [2, 4096], P('section', 'dp'), may hold values from 0.5 to 1.5
- out_weight: bfloat16 [2, 4096, 2048], P('section', 'dp'), may hold values from -0.25 to 0.25
Outputs:
- result: float32 [2, 2, 16, 128, 2048], P('section', None, ('grp', 'dp'))
- grad_norm_gain: float32 [2, 2048], P('section', 'dp')
- grad_in_weight: float32 [2, 2048, 8192], P('section', 'dp')
- grad_conv_weight: float32 [2, 4, 4096], P('section', None, 'dp')
- grad_conv_bias: float32 [2, 4096], P('section', 'dp')
- grad_down_weight: float32 [2, 4096, 128], P('section', 'dp')
- grad_kq_weight: float32 [2, 32, 4096], P('section', None, 'dp')
- grad_dt_weight: float32 [2, 128, 4096], P('section', None, 'dp')
- grad_dt_bias: float32 [2, 4096], P('section', 'dp')
- grad_skip_weight: float32 [2, 4096], P('section', 'dp')
- grad_out_weight: float32 [2, 4096, 2048], P('section', 'dp')
Inputs may be any that keep to these rules, and one draw needn't show every extreme that they name: `doc_lengths`: in every slot one document, at a place drawn from the seed, has exactly 64 positions and the others 1 to 32, so a slot never overflows.
All inputs are finite; a program needn't handle non-finite values.
Results may differ from a plain program's by a relative error of at most 0.02.
Values may be sent and summed in bfloat16 or wider, within the bound.
No kernel may reach another device: no remote copies, remote signals or barrier semaphores. Data moves between devices by JAX's collectives and lax.ppermute only.
A program may use at most 448 MiB of HBM per device.

v0:
```python
from functools import partial

import jax
import jax.numpy as jnp
from jax import lax
from jax.sharding import PartitionSpec as P

BLOCK = 16


EPSILON = 1e-05


def shifted(value, axis, steps):
    count = lax.axis_size(axis)
    leading, last = (max(0, -steps), min(count, count - steps))
    return lax.ppermute(value, axis, [(source, source + steps) for source in range(leading, last)])


def matrix_dot(left_op, right_op, left_axis, right_axis):
    return lax.dot_general(
        left_op,
        right_op,
        (((left_axis,), (right_axis,)), ((), ())),
        preferred_element_type=jnp.float32,
    )


def doc_layout(lengths, length):
    doc_ends = jnp.cumsum(lengths)
    position = jnp.arange(length, dtype=jnp.int32)
    segment = jnp.sum((position[:, None] >= doc_ends[None, :]).astype(jnp.int32), axis=1)
    row_valid = (position < doc_ends[-1]).astype(jnp.float32)
    previous = jnp.concatenate([jnp.full((1,), -1, jnp.int32), segment[:-1]])
    carry_on = (previous == segment).astype(jnp.float32)
    return (segment, row_valid, carry_on)


def conv_piece(segment, source, conv_taps, conv_bias):
    summed = conv_bias[None, :] + conv_taps[0][None, :] * source
    for offset in range(1, conv_taps.shape[0]):
        earlier = jnp.concatenate(
            [jnp.zeros((offset, source.shape[1]), source.dtype), source[:-offset]], axis=0
        )
        before = jnp.concatenate([jnp.full((offset,), -1, jnp.int32), segment[:-offset]])
        same_doc = (before == segment).astype(source.dtype)
        summed = summed + conv_taps[offset][None, :] * earlier * same_doc[:, None]
    return jax.nn.silu(summed)


def norm_piece(hidden, norm_gain):
    inv_rms = lax.rsqrt(jnp.mean(hidden * hidden, axis=1, keepdims=True) + EPSILON)
    return hidden * inv_rms * norm_gain[None, :]


def block_scan(carried, pieces):
    step_size, key_vec, queries, values, carry_on = pieces
    key_sq = key_vec * key_vec
    state = carried
    readouts = []
    for position in range(step_size.shape[0]):
        decay = carry_on[position] * (
            1.0 - key_sq[position][:, None] * step_size[position][None, :]
        )
        drive = key_vec[position][:, None] * (step_size[position] * values[position])[None, :]
        state = decay * state + drive
        readouts.append(jnp.sum(state * queries[position][:, None], axis=0))
    return (state, jnp.stack(readouts))


def recurrence(step_size, key_vec, queries, values, carry_on):
    length, channels = values.shape
    blocks = length // BLOCK

    def blocked(array):
        return array.reshape((blocks, BLOCK) + array.shape[1:])

    initial = jnp.zeros((key_vec.shape[1], channels), jnp.float32)
    final_state, readout = lax.scan(
        jax.checkpoint(block_scan),
        initial,
        (
            blocked(step_size),
            blocked(key_vec),
            blocked(queries),
            blocked(values),
            blocked(carry_on),
        ),
    )
    return readout.reshape(length, channels)


def mixer(carry_on, rate_in, kq_rows, values, gate_rows, rate_bias, skip_gain):
    state_dim = kq_rows.shape[1] // 2
    key_vec, queries = (kq_rows[:, :state_dim], kq_rows[:, state_dim:])
    strength = jax.nn.sigmoid(rate_in + rate_bias[None, :])
    step_size = strength / (1.0 + strength * jnp.sum(key_vec * key_vec, axis=1, keepdims=True))
    combined = (
        recurrence(step_size, key_vec, queries, values, carry_on) + skip_gain[None, :] * values
    )
    return combined * jax.nn.silu(gate_rows)


def run_layer(hidden, layout, weights):
    segment, row_valid, carry_on = layout
    norm_gain, w_in, conv_taps, conv_bias, w_down, w_kq, w_rate, rate_bias, skip_gain, w_out = (
        weights
    )
    channels = w_kq.shape[1]
    normed_full, norm_pull = jax.vjp(norm_piece, hidden, norm_gain.astype(jnp.float32))
    normed = normed_full.astype(jnp.bfloat16)
    projected = matrix_dot(normed, w_in, 1, 0)
    inner_full, conv_pull = jax.vjp(
        partial(conv_piece, segment),
        projected[:, :channels],
        conv_taps.astype(jnp.float32),
        conv_bias.astype(jnp.float32),
    )
    inner_act = inner_full.astype(jnp.bfloat16)
    low_rank = matrix_dot(inner_act, w_down, 1, 0).astype(jnp.bfloat16)
    kq_rows = matrix_dot(inner_act, w_kq, 1, 1)
    rate_pre = matrix_dot(low_rank, w_rate, 1, 0)
    gated_full, mix_pull = jax.vjp(
        partial(mixer, carry_on),
        rate_pre,
        kq_rows,
        inner_act.astype(jnp.float32),
        projected[:, channels:],
        rate_bias.astype(jnp.float32),
        skip_gain.astype(jnp.float32),
    )
    gated_out = gated_full.astype(jnp.bfloat16)
    branch = matrix_dot(gated_out, w_out, 1, 0)
    layer_out = hidden + row_valid[:, None] * branch
    return (layer_out, (normed, inner_act, low_rank, gated_out, norm_pull, conv_pull, mix_pull))


def back_layer(hidden, upstream, layout, weights, totals):
    layer_out, saved = run_layer(hidden, layout, weights)
    normed, inner_act, low_rank, gated_out, norm_pull, conv_pull, mix_pull = saved
    norm_gain, w_in, conv_taps, conv_bias, w_down, w_kq, w_rate, rate_bias, skip_gain, w_out = (
        weights
    )
    (
        sum_gain,
        sum_in,
        sum_taps,
        sum_conv_bias,
        sum_down,
        sum_kq,
        sum_rate,
        sum_rate_bias,
        sum_skip,
        sum_out,
    ) = totals
    dbranch = (layout[1][:, None] * upstream).astype(jnp.bfloat16)
    sum_out = sum_out + matrix_dot(gated_out, dbranch, 0, 0)
    dgated = matrix_dot(dbranch, w_out, 1, 1)
    drate, dkq_rows, dvalues, dgate, grad_rate_bias, grad_skip = mix_pull(dgated)
    sum_rate_bias = sum_rate_bias + grad_rate_bias
    sum_skip = sum_skip + grad_skip
    drate_low = drate.astype(jnp.bfloat16)
    sum_rate = sum_rate + matrix_dot(low_rank, drate_low, 0, 0)
    dlow_rank = matrix_dot(drate_low, w_rate, 1, 1).astype(jnp.bfloat16)
    dkq_low = dkq_rows.astype(jnp.bfloat16)
    sum_down = sum_down + matrix_dot(inner_act, dlow_rank, 0, 0)
    sum_kq = sum_kq + matrix_dot(dkq_low, inner_act, 0, 0)
    dinner = dvalues + matrix_dot(dlow_rank, w_down, 1, 1) + matrix_dot(dkq_low, w_kq, 1, 0)
    dsource, grad_taps, grad_conv_bias = conv_pull(dinner)
    sum_taps = sum_taps + grad_taps
    sum_conv_bias = sum_conv_bias + grad_conv_bias
    dprojected = jnp.concatenate([dsource, dgate], axis=1).astype(jnp.bfloat16)
    sum_in = sum_in + matrix_dot(normed, dprojected, 0, 0)
    dhidden, grad_gain = norm_pull(matrix_dot(dprojected, w_in, 1, 1))
    sum_gain = sum_gain + grad_gain
    return (
        upstream + dhidden,
        (
            sum_gain,
            sum_in,
            sum_taps,
            sum_conv_bias,
            sum_down,
            sum_kq,
            sum_rate,
            sum_rate_bias,
            sum_skip,
            sum_out,
        ),
    )


def on_device(
    boundary,
    doc_lengths,
    norm_gain,
    in_weight,
    conv_weight,
    conv_bias,
    down_weight,
    kq_weight,
    dt_weight,
    dt_bias,
    skip_weight,
    out_weight,
):
    section_idx = lax.axis_index("section")
    micro_count = boundary.shape[1]
    length = boundary.shape[3]
    width_model = boundary.shape[4]
    row_part = (
        norm_gain[0],
        in_weight[0],
        down_weight[0],
        out_weight[0],
        conv_bias[0],
        dt_bias[0],
        skip_weight[0],
    )
    col_part = (conv_weight[0], kq_weight[0], dt_weight[0])
    gain_full, in_full, down_full, out_full, conv_bias_full, rate_bias_full, skip_full = (
        lax.all_gather(row_part[0], "dp", axis=0, tiled=True),
        lax.all_gather(row_part[1], "dp", axis=0, tiled=True),
        lax.all_gather(row_part[2], "dp", axis=0, tiled=True),
        lax.all_gather(row_part[3], "dp", axis=0, tiled=True),
        lax.all_gather(row_part[4], "dp", axis=0, tiled=True),
        lax.all_gather(row_part[5], "dp", axis=0, tiled=True),
        lax.all_gather(row_part[6], "dp", axis=0, tiled=True),
    )
    taps_full, kq_full, rate_full = (
        lax.all_gather(col_part[0], "dp", axis=1, tiled=True),
        lax.all_gather(col_part[1], "dp", axis=1, tiled=True),
        lax.all_gather(col_part[2], "dp", axis=1, tiled=True),
    )
    weights = (
        gain_full,
        in_full,
        taps_full,
        conv_bias_full,
        down_full,
        kq_full,
        rate_full,
        rate_bias_full,
        skip_full,
        out_full,
    )
    boundary_rows = boundary[0, :, 0]
    lengths = doc_lengths[:, 0]

    def layout_of(micro_idx):
        slot_idx = jnp.clip(micro_idx, 0, micro_count - 1)
        return doc_layout(lax.dynamic_index_in_dim(lengths, slot_idx, 0, keepdims=False), length)

    received = jnp.zeros((length, width_model), jnp.bfloat16)
    kept_inputs = []
    forward_outs = []
    for tick_num in range(micro_count + 1):
        micro_idx = tick_num - section_idx
        active = (micro_idx >= 0) & (micro_idx < micro_count)
        own_input = boundary_rows[min(tick_num, micro_count - 1)]
        layer_input = jnp.where(section_idx == 0, own_input, received)
        kept_inputs.append(layer_input)
        layout = layout_of(micro_idx)
        layer_out = lax.cond(
            active,
            lambda: run_layer(layer_input.astype(jnp.float32), layout, weights)[0],
            lambda: jnp.zeros((length, width_model), jnp.float32),
        )
        forward_outs.append(layer_out)
        if tick_num < micro_count:
            received = shifted(layer_out.astype(jnp.bfloat16), "section", 1)
    kept_stack = jnp.stack(kept_inputs)
    grad_received = jnp.zeros((length, width_model), jnp.bfloat16)
    totals = tuple((jnp.zeros(weight.shape, jnp.float32) for weight in weights))
    input_grads = []
    for tick_num in range(micro_count + 1):
        micro_idx = tick_num - (1 - section_idx)
        active = (micro_idx >= 0) & (micro_idx < micro_count)
        slot_idx = jnp.clip(micro_idx, 0, micro_count - 1)
        layer_input = lax.dynamic_index_in_dim(
            kept_stack, slot_idx + section_idx, 0, keepdims=False
        ).astype(jnp.float32)
        upstream = jnp.where(
            section_idx == 1, boundary_rows[min(tick_num, micro_count - 1)], grad_received
        ).astype(jnp.float32)
        layout = layout_of(micro_idx)
        current = totals
        dhidden, totals = lax.cond(
            active,
            lambda: back_layer(layer_input, upstream, layout, weights, current),
            lambda: (jnp.zeros((length, width_model), jnp.float32), current),
        )
        input_grads.append(dhidden)
        if tick_num < micro_count:
            grad_received = shifted(dhidden.astype(jnp.bfloat16), "section", -1)
    result_rows = jnp.stack(
        [
            jnp.where(section_idx == 0, input_grads[micro + 1], forward_outs[micro + 1])
            for micro in range(micro_count)
        ]
    )
    result = result_rows.reshape(1, micro_count, 1, length, width_model)
    (
        grad_gain,
        grad_in,
        grad_taps,
        grad_conv_bias,
        grad_down,
        grad_kq,
        grad_rate,
        grad_rate_bias,
        grad_skip,
        grad_out,
    ) = totals
    row_grads = (grad_gain, grad_in, grad_down, grad_out, grad_conv_bias, grad_rate_bias, grad_skip)
    col_grads = (grad_taps, grad_kq, grad_rate)
    row_sums = (
        lax.psum_scatter(
            row_grads[0].astype(jnp.bfloat16), "dp", scatter_dimension=0, tiled=True
        ).astype(jnp.float32),
        lax.psum_scatter(
            row_grads[1].astype(jnp.bfloat16), "dp", scatter_dimension=0, tiled=True
        ).astype(jnp.float32),
        lax.psum_scatter(
            row_grads[2].astype(jnp.bfloat16), "dp", scatter_dimension=0, tiled=True
        ).astype(jnp.float32),
        lax.psum_scatter(
            row_grads[3].astype(jnp.bfloat16), "dp", scatter_dimension=0, tiled=True
        ).astype(jnp.float32),
        lax.psum_scatter(
            row_grads[4].astype(jnp.bfloat16), "dp", scatter_dimension=0, tiled=True
        ).astype(jnp.float32),
        lax.psum_scatter(
            row_grads[5].astype(jnp.bfloat16), "dp", scatter_dimension=0, tiled=True
        ).astype(jnp.float32),
        lax.psum_scatter(
            row_grads[6].astype(jnp.bfloat16), "dp", scatter_dimension=0, tiled=True
        ).astype(jnp.float32),
    )
    col_sums = (
        lax.psum_scatter(
            col_grads[0].astype(jnp.bfloat16), "dp", scatter_dimension=1, tiled=True
        ).astype(jnp.float32),
        lax.psum_scatter(
            col_grads[1].astype(jnp.bfloat16), "dp", scatter_dimension=1, tiled=True
        ).astype(jnp.float32),
        lax.psum_scatter(
            col_grads[2].astype(jnp.bfloat16), "dp", scatter_dimension=1, tiled=True
        ).astype(jnp.float32),
    )
    summed = (
        lax.psum(row_sums[0].astype(jnp.bfloat16), "grp").astype(jnp.float32),
        lax.psum(row_sums[1].astype(jnp.bfloat16), "grp").astype(jnp.float32),
        lax.psum(row_sums[2].astype(jnp.bfloat16), "grp").astype(jnp.float32),
        lax.psum(row_sums[3].astype(jnp.bfloat16), "grp").astype(jnp.float32),
        lax.psum(row_sums[4].astype(jnp.bfloat16), "grp").astype(jnp.float32),
        lax.psum(row_sums[5].astype(jnp.bfloat16), "grp").astype(jnp.float32),
        lax.psum(row_sums[6].astype(jnp.bfloat16), "grp").astype(jnp.float32),
        lax.psum(col_sums[0].astype(jnp.bfloat16), "grp").astype(jnp.float32),
        lax.psum(col_sums[1].astype(jnp.bfloat16), "grp").astype(jnp.float32),
        lax.psum(col_sums[2].astype(jnp.bfloat16), "grp").astype(jnp.float32),
    )
    (
        sum_gain,
        sum_in,
        sum_down,
        sum_out,
        sum_conv_bias,
        sum_rate_bias,
        sum_skip,
        sum_taps,
        sum_kq,
        sum_rate,
    ) = summed
    return (
        result,
        sum_gain[None],
        sum_in[None],
        sum_taps[None],
        sum_conv_bias[None],
        sum_down[None],
        sum_kq[None],
        sum_rate[None],
        sum_rate_bias[None],
        sum_skip[None],
        sum_out[None],
    )


def solution(mesh):
    return jax.shard_map(
        on_device,
        mesh=mesh,
        in_specs=(
            P("section", None, ("grp", "dp"), None, None),
            P(None, ("grp", "dp"), None),
            P("section", "dp"),
            P("section", "dp", None),
            P("section", None, "dp"),
            P("section", "dp"),
            P("section", "dp", None),
            P("section", None, "dp"),
            P("section", None, "dp"),
            P("section", "dp"),
            P("section", "dp"),
            P("section", "dp", None),
        ),
        out_specs=(
            P("section", None, ("grp", "dp"), None, None),
            P("section", "dp"),
            P("section", "dp", None),
            P("section", None, "dp"),
            P("section", "dp"),
            P("section", "dp", None),
            P("section", None, "dp"),
            P("section", None, "dp"),
            P("section", "dp"),
            P("section", "dp"),
            P("section", "dp", None),
        ),
        check_vma=False,
    )
```

profile of v0, /device:TPU:0, one launch (start us, length us, event | category | flops | bytes accessed | tf_op | source)
XLA Modules:
  0.0 5447.6 jit_solution(542309771765837108)
XLA Ops:
  78.1 15.1 all-gather.9
  95.4 264.6 %all-gather.15.cloned.1.call-done = bf16[1,4096,2048]{2,1,0:T(8,128)(2,1)} async-done(((bf16[1,1024,2048]{2,1,0:T(8,128)(2,1)}), bf16[1,4096,2048]{2,1,0:T(8,128)(2,1)}) %all-gather.15.cloned.1.call-update) | async-done | bytes 16777232 | tf_op jit(solution)/shard_map/all_gather | solution.py:225
  360.0 561.0 %all-gather.17.cloned.1.call-done = bf16[1,2048,8192]{2,1,0:T(8,128)(2,1)} async-done(((bf16[1,512,8192]{2,1,0:T(8,128)(2,1)}), bf16[1,2048,8192]{2,1,0:T(8,128)(2,1)}) %all-gather.17.cloned.1.call-update) | async-done | bytes 33554448 | tf_op jit(solution)/shard_map/all_gather | solution.py:223
  921.0 228.9 %conditional.6 = (bf16[128,2048]{1,0:T(8,128)(2,1)S(1)}) conditional(s32[]{:T(128)} %convert_element_type.574, () %tuple.166, (pred[]{:T(512)}, bf16[128,2048]{1,0:T(8,128)(2,1)S(1)}, bf16[128,2048]{1,0:T(8,128)(2,1)S(1)}, f32[128]{0:T(128)}, bf16[4096]{0:T(1024)(128)(2,1)S(1)}, /*index=5*/bf16[4,4096]{1,0:T(4,128)(2,1)S(1)}, ...), branch_computations={%region_2.3_spmd, %region_3.24_spmd} | conditional | flops 6777114112 | bytes 126246080 | solution.py:264
  944.5 194.1 %while.196 = (s32[]{:T(128)}, f32[16,4096]{1,0:T(8,128)S(1)}, f32[8,16,4096]{2,1,0:T(8,128)}, f32[8,16]{1,0:T(8,128)S(1)}, f32[8,16,16]{2,1,0:T(8,128)S(1)}, /*i...) while((s32[]{:T(128)}, f32[16,4096]{1,0:T(8,128)S(1)}, ...), condition=%wide.region_23.23_spmd.clone, body=%wide.region_6.22_spmd.clone.sunk | while | flops 11665682 | bytes 8402308 | solution.py:79
  1156.9 230.4 %conditional.7 = (f32[128,2048]{1,0:T(8,128)}) conditional(s32[]{:T(128)} %convert_element_type.579, () %tuple.168, (bf16[128,2048]{1,0:T(8,128)(2,1)S(1)}, f32[128]{0:T(128)S(1)}, bf16[4096]{0:T(1024)(128)(2,1)S(1)}, bf16[4,4096]{1,0:T(4,128)(2,1)S(1)}, bf16[2048]{0:T(1024)(128)(2,1)S(1)}, /*index=5*/bf16[2048,8192]{1,0:T(8,128)(2,1)}, ...), branch_computations={%region_26.27_spmd, %region_27.48_spmd} | conditional | flops 6776589824 | bytes 125717632 | solution.py:264
  1180.2 195.0 %while.197 = (s32[]{:T(128)}, f32[16,4096]{1,0:T(8,128)S(1)}, f32[8,16,4096]{2,1,0:T(8,128)}, f32[8,16]{1,0:T(8,128)S(1)}, f32[8,16,16]{2,1,0:T(8,128)S(1)}, /*i...) while((s32[]{:T(128)}, f32[16,4096]{1,0:T(8,128)S(1)}, ...), condition=%wide.region_47.47_spmd.clone, body=%wide.region_30.46_spmd.clone.sunk | while | flops 11665682 | bytes 8402308 | solution.py:79
  1395.3 45.7 conditional.8
  1395.3 21.1 broadcast_in_dim.2417
  1445.4 752.3 %collective-permute-done.2 = bf16[128,2048]{1,0:T(8,128)(2,1)S(1)} collective-permute-done((bf16[128,2048]{1,0:T(8,128)(2,1)}, bf16[128,2048]{1,0:T(8,128)(2,1)S(1)}, u32[]{:S(2)}, u32[]{:S(2)}) %collective-permute-start.2) | collective-permute-done | bytes 524320 | tf_op jit(solution)/shard_map/ppermute | solution.py:17
  2199.9 997.4 %conditional.9 = (f32[128,2048]{1,0:T(8,128)}, f32[2048]{0:T(1024)}, f32[2048,8192]{1,0:T(8,128)}, f32[4,4096]{1,0:T(4,128)}, f32[4096]{0:T(1024)}, /*index=5*/f...) conditional(s32[]{:T(128)} %convert_element_type.570, ...), branch_computations={%region_166.167_spmd, %region_167.280_spmd} | conditional | flops 18229213184 | bytes 569313344 | solution.py:288
  2218.3 15.1 multiply_reduce_fusion.233
  2247.3 393.2 %while.199 = (s32[]{:T(128)}, f32[16,4096]{1,0:T(8,128)S(1)}, f32[8,16,4096]{2,1,0:T(8,128)}, f32[8,16,4096]{2,1,0:T(8,128)}, f32[8,16]{1,0:T(8,128)}, /*index=5...) while((s32[]{:T(128)}, f32[16,4096]{1,0:T(8,128)S(1)}, ...), condition=%wide.region_187.187_spmd.clone, body=%wide.region_170.186_spmd.clone.sunk | while | flops 11731218 | bytes 10312157 | solution.py:79
  2644.3 421.9 %while.200 = (s32[]{:T(128)}, f32[16,4096]{1,0:T(8,128)}, f32[8,16,4096]{2,1,0:T(8,128)}, f32[8,16,16]{2,1,0:T(8,128)S(1)}, f32[8,16,16]{2,1,0:T(8,128)}, /*inde...) while((s32[]{:T(128)}, f32[16,4096]{1,0:T(8,128)}, ...), condition=%wide.region_269.269_spmd.clone, body=%wide.region_188.268_spmd.clone.sunk | while | flops 34680324 | bytes 23446268 | solution.py:79
  3092.0 43.3 convolution_add_fusion.5
  3137.6 25.6 convolution_add_fusion.6
  3163.2 19.1 fusion.234
  3206.8 1014.9 %conditional.10 = (f32[128,2048]{1,0:T(8,128)}, f32[2048]{0:T(1024)}, f32[2048,8192]{1,0:T(8,128)}, f32[4,4096]{1,0:T(4,128)}, f32[4096]{0:T(1024)}, /*index=5*/...) conditional(s32[]{:T(128)} %convert_element_type.591, ...), branch_computations={%region_282.283_spmd, %region_283.396_spmd} | conditional | flops 18229213184 | bytes 568231872 | solution.py:288
  3225.5 15.0 multiply_reduce_fusion.336
  3253.9 399.2 %while.194 = (s32[]{:T(128)}, f32[16,4096]{1,0:T(8,128)S(1)}, f32[8,16,4096]{2,1,0:T(8,128)}, f32[8,16,4096]{2,1,0:T(8,128)}, f32[8,16]{1,0:T(8,128)}, /*index=5...) while((s32[]{:T(128)}, f32[16,4096]{1,0:T(8,128)S(1)}, ...), condition=%wide.region_303.303_spmd.clone, body=%wide.region_286.302_spmd.clone.sunk | while | flops 11731218 | bytes 10312157 | solution.py:79
  3656.8 433.1 %while.195 = (s32[]{:T(128)}, f32[16,4096]{1,0:T(8,128)}, f32[8,16,4096]{2,1,0:T(8,128)}, f32[8,16,16]{2,1,0:T(8,128)S(1)}, f32[8,16,16]{2,1,0:T(8,128)}, /*inde...) while((s32[]{:T(128)}, f32[16,4096]{1,0:T(8,128)}, ...), condition=%wide.region_385.385_spmd.clone, body=%wide.region_304.384_spmd.clone.sunk | while | flops 34680324 | bytes 23446268 | solution.py:79
  4115.7 43.3 convolution_add_fusion.13
  4161.6 25.5 convolution_add_fusion.14
  4187.1 19.3 fusion.308
  4229.1 17.5 convert_element_type.610
  4246.7 32.9 convert_element_type.602
  4282.0 16.4 reduce-scatter.15.cloned.1.call-done
  4298.4 282.0 %reduce-scatter.17.cloned.1.call-done = bf16[1024,2048]{1,0:T(8,128)(2,1)} async-done(((bf16[4096,2048]{1,0:T(8,128)(2,1)}), bf16[1024,2048]{1,0:T(8,128)(2,1)}) %reduce-scatter.17.cloned.1.call-update) | async-done | bytes 4194320 | tf_op jit(solution)/shard_map/reduce_scatter | solution.py:327
  4580.5 555.2 %reduce-scatter.21.cloned.1.call-done = bf16[512,8192]{1,0:T(8,128)(2,1)} async-done(((bf16[2048,8192]{1,0:T(8,128)(2,1)}), bf16[512,8192]{1,0:T(8,128)(2,1)}) %reduce-scatter.21.cloned.1.call-update) | async-done | bytes 8388624
  5145.9 19.8 all-reduce.350
  5169.8 17.2 all-reduce.351
  5189.9 232.2 %all-reduce.355.cloned.1.call-done = (bf16[1,512,8192]{2,1,0:T(8,128)(2,1)}, bf16[1,1024,128]{2,1,0:T(8,128)(2,1)}, bf16[1,32,1024]{2,1,0:T(8,128)(2,1)}, bf16[1...) async-done(((bf16[1,512,8192]{2,1,0:T(8,128)(2,1)}, bf16[1,1024,128]{2,1,0:T(8,128)(2,1)}, bf16[1,32,1024]{2,1,0:T(8,128)(2,1)}, bf16[1,128,1024]{2,1,0:T(8,128)(2,1)}, ...) | async-done | bytes 13172752 | tf_op jit(solution)/shard_map/psum | solution.py:353
  (3707 shorter events, 2412.9 us)
Async XLA Ops:
  7.2 88.2 %all-gather.19.cloned.1.call-start = ((), (), s32[]{:S(2)}) async-start(), calls=%async_computation.12 | async-start | bytes 1310720 | tf_op jit(solution)/shard_map/all_gather | solution.py:224
  7.9 87.5 %all-gather.21.cloned.1.call-start = ((), (), s32[]{:S(2)}) async-start(), calls=%async_computation.13 | async-start | bytes 1310720 | tf_op jit(solution)/shard_map/all_gather | solution.py:233
  8.7 351.3 %all-gather.15.cloned.1.call-start = ((), (), s32[]{:S(2)}) async-start(), calls=%async_computation.10 | async-start | bytes 20971520 | tf_op jit(solution)/shard_map/all_gather | solution.py:225
  9.4 30.2 copy-start.262
  9.4 43.4 copy-start.291
  9.4 55.4 %copy-start.259 = (bf16[1,4,1024]{2,1,0:T(4,128)(2,1)S(1)}, bf16[1,4,1024]{2,1,0:T(4,128)(2,1)}, u32[]{:S(2)}) copy-start(bf16[1,4,1024]{2,1,0:T(4,128)(2,1)} %param.46) | copy-start | bytes 24580
  9.5 68.6 %copy-start.195 = (bf16[1,32,1024]{2,1,0:T(8,128)(2,1)S(1)}, bf16[1,32,1024]{2,1,0:T(8,128)(2,1)}, u32[]{:S(2)}) copy-start(bf16[1,32,1024]{2,1,0:T(8,128)(2,1)} %param.49) | copy-start | bytes 196612
  9.5 85.0 %copy-start.39 = (bf16[1,2,1,128,2048]{4,3,2,1,0:T(8,128)(2,1)S(1)}, bf16[1,2,1,128,2048]{4,3,2,1,0:T(8,128)(2,1)}, u32[]{:S(2)}) copy-start(bf16[1,2,1,128,2048]{4,3,2,1,0:T(8,128)(2,1)} %param.42) | copy-start | bytes 3145732
  9.5 911.5 %all-gather.17.cloned.1.call-start = ((), (), s32[]{:S(2)}) async-start(), calls=%async_computation.11 | async-start | bytes 41943040 | tf_op jit(solution)/shard_map/all_gather | solution.py:223
  10.1 4271.9 %reduce-scatter.13.cloned.1.call-start = ((), (), s32[]{:S(2)}) async-start(), calls=%async_computation.7 | async-start | bytes 327680 | tf_op jit(solution)/shard_map/reduce_scatter | solution.py:344
  26.4 2173.4 %copy-start.96 = (bf16[4096]{0:T(1024)(128)(2,1)}, bf16[4096]{0:T(1024)(128)(2,1)S(1)}, u32[]{:S(2)}) copy-start(bf16[4096]{0:T(1024)(128)(2,1)S(1)} %reduce) | copy-start | bytes 24580
  39.6 2160.2 %copy-start.101 = (bf16[4096]{0:T(1024)(128)(2,1)}, bf16[4096]{0:T(1024)(128)(2,1)S(1)}, u32[]{:S(2)}) copy-start(bf16[4096]{0:T(1024)(128)(2,1)S(1)} %reduce.1) | copy-start | bytes 24580
  52.8 2147.0 %copy-start.104 = (bf16[4096]{0:T(1024)(128)(2,1)}, bf16[4096]{0:T(1024)(128)(2,1)S(1)}, u32[]{:S(2)}) copy-start(bf16[4096]{0:T(1024)(128)(2,1)S(1)} %reduce.3) | copy-start | bytes 24580
  64.9 1329.7 %copy-start.113 = (bf16[2048]{0:T(1024)(128)(2,1)}, bf16[2048]{0:T(1024)(128)(2,1)S(1)}, u32[]{:S(2)}) copy-start(bf16[2048]{0:T(1024)(128)(2,1)S(1)} %reduce.2) | copy-start | bytes 12292
  78.1 2121.8 %copy-start.56 = (bf16[1,4,4096]{2,1,0:T(4,128)(2,1)}, bf16[1,4,4096]{2,1,0:T(4,128)(2,1)S(1)}, u32[]{:S(2)}) copy-start(bf16[1,4,4096]{2,1,0:T(4,128)(2,1)S(1)} %all-gather) | copy-start | bytes 98308
  93.2 2106.7 %copy-start.25 = (bf16[1,32,4096]{2,1,0:T(8,128)(2,1)}, bf16[1,32,4096]{2,1,0:T(8,128)(2,1)S(1)}, u32[]{:S(2)}) copy-start(bf16[1,32,4096]{2,1,0:T(8,128)(2,1)S(1)} %all-gather.9) | copy-start | bytes 786436
  1150.0 5.8 collective-permute-start
  1153.5 237.7 %copy-start.305 = (s32[3,1]{0,1:T(1,128)}, s32[3,1]{0,1:T(1,128)S(1)}, u32[]{:S(2)}) copy-start(s32[3,1]{0,1:T(1,128)S(1)} %reduce-window.29) | copy-start | bytes 40
  1388.7 3.3 collective-permute-start.1
  1441.8 758.0 %copy-start.10 = (bf16[3,128,2048]{2,1,0:T(8,128)(2,1)S(1)}, bf16[3,128,2048]{2,1,0:T(8,128)(2,1)}, u32[]{:S(2)}) copy-start(bf16[3,128,2048]{2,1,0:T(8,128)(2,1)} %copy-done.9) | copy-start | bytes 4718596
  1441.8 758.0 %copy-start.114 = (bf16[2048]{0:T(1024)(128)(2,1)S(1)}, bf16[2048]{0:T(1024)(128)(2,1)}, u32[]{:S(2)}) copy-start(bf16[2048]{0:T(1024)(128)(2,1)} %copy-done.113) | copy-start | bytes 12292
  1441.8 755.9 %collective-permute-start.2 = (bf16[128,2048]{1,0:T(8,128)(2,1)}, bf16[128,2048]{1,0:T(8,128)(2,1)S(1)}, u32[]{:S(2)}, u32[]{:S(2)}) collective-permute-start(bf16[128,2048]{1,0:T(8,128)(2,1)} %copy-done.91), channel_id=1, source_target_pairs={{16,0},{17,1},{18,2},{19,3},{20,4},{21,5},{22,6},{23,7},{24,8},{25... | collective-permute-start | bytes 1572872 | tf_op jit(solution)/shard_map/ppermute | solution.py:17
  2644.3 421.9 %copy-start.269 = (f32[128]{0:T(128)S(1)}, f32[128]{0:T(128)}, u32[]{:S(2)}) copy-start(f32[128]{0:T(128)} %copy-done.268) | copy-start | bytes 1540 | tf_op jit(solution)/shard_map/cond
  3200.4 4.1 collective-permute-start.3
  3206.9 33.7 copy-start.31
  3656.8 433.1 %copy-start.271 = (f32[128]{0:T(128)S(1)}, f32[128]{0:T(128)}, u32[]{:S(2)}) copy-start(f32[128]{0:T(128)} %copy-done.270) | copy-start | bytes 1540 | tf_op jit(solution)/shard_map/cond
  4223.5 58.5 %reduce-scatter.11.cloned.1.call-start = ((), (), s32[]{:S(2)}) async-start(), calls=%async_computation.6 | async-start | bytes 1310720 | tf_op jit(solution)/shard_map/reduce_scatter | solution.py:324
  4226.3 72.2 %reduce-scatter.15.cloned.1.call-start = ((), (), s32[]{:S(2)}) async-start(), calls=%async_computation.8 | async-start | bytes 1310720 | tf_op jit(solution)/shard_map/reduce_scatter | solution.py:347
  4229.1 351.4 %reduce-scatter.17.cloned.1.call-start = ((), (), s32[]{:S(2)}) async-start(), calls=%async_computation.9 | async-start | bytes 20971520 | tf_op jit(solution)/shard_map/reduce_scatter | solution.py:327
  4246.6 889.0 %reduce-scatter.21.cloned.1.call-start = ((), (), s32[]{:S(2)}) async-start(), calls=%async_computation.15 | async-start | bytes 41943040
  4279.6 889.1 %reduce-scatter.19.cloned.1.call-start = ((), (), s32[]{:S(2)}) async-start(), calls=%async_computation.14 | async-start | bytes 1310720
  4281.9 1140.2 %all-reduce.355.cloned.1.call-start = ((), (), s32[]{:S(2)}) async-start(), calls=%async_computation.16 | async-start | bytes 26345472 | tf_op jit(solution)/shard_map/psum | solution.py:353
  (846 other events, 14173.8 us)
Sparse Core Ops, SparseCore 0:
  9.6 31.0 all-gather.18
  42.3 28.8 all-gather.20
  72.8 287.1 all-gather.14
  361.4 559.5 all-gather.16
  4223.7 17.8 reduce-scatter.12
  4244.3 25.3 reduce-scatter.10
  4272.6 25.7 reduce-scatter.14
  4301.5 278.9 reduce-scatter.16
  4582.8 552.7 reduce-scatter.20
  5137.9 28.2 reduce-scatter.18
  5170.6 251.4 all-reduce.354
where the time goes:
time: 5490 us; the launch traced here: 5450 us
  waiting for transfers between devices  2670 us (49%)
  other arithmetic  1820 us (33%)
  local copies, waits for them, and re-layouts  461 us (8%)
  matrix products  334 us (6%)
  blocking collectives  118 us (2%)
    ppermute x4, waiting for transfers between devices, shifted(): lax.ppermute(value, axis, [(source, source + steps) for source in range(l...  754 us
    reduce_sum x288, other arithmetic, block_scan(): readouts.append(jnp.sum(state * queries[position][:, None], axis=0))  711 us
    all_gather x1, waiting for transfers between devices, on_device(): lax.all_gather(row_part[1], 'dp', axis=0, tiled=True)  561 us
    unnamed x13, waiting for transfers between devices  558 us
    reduce_sum x112, other arithmetic, block_scan(): key_vec[position][:, None]  347 us
    dot_general x36, matrix products, matrix_dot(): lax.dot_general(left_op, right_op, (((left_axis,), (right_axis,)), ((), (...  334 us
    reduce_sum x128, other arithmetic, block_scan(): key_sq[position][:, None] * step_size[position][None, :]  316 us
    reduce_scatter x1, waiting for transfers between devices, on_device(): lax.psum_scatter(row_grads[3].astype(jnp.bfloat16), 'dp', scatter_dimensi...  282 us
  transfers between devices with their start and end apart: 15, of which 8 were waited for; matrix products, arithmetic and copies ran while one was open for 2% of the time, Pallas kernels for 0%

commit v1 on v0

v1 whole, which is shorter than its diff:
```python
from functools import partial

import jax
import jax.numpy as jnp
from jax import lax
from jax.experimental import pallas as pl
from jax.experimental.pallas import tpu as pltpu
from jax.sharding import PartitionSpec as P

EPSILON = 1e-05
BF = jnp.bfloat16
F32 = jnp.float32
STATE = 16
RANK = 128
LANES = 128
ROWS = 8
MIB = 1024 * 1024


def dot(left, right, left_axis, right_axis, kind=F32):
    return lax.dot_general(
        left, right, (((left_axis,), (right_axis,)), ((), ())), preferred_element_type=kind
    )


def sig(value):
    return 1.0 / (1.0 + jnp.exp(-value))


def swap(value, axis, shift):
    return lax.ppermute(value, axis, [(i, i ^ shift) for i in range(lax.axis_size(axis))])


def peers(value):
    return [swap(value, "grp", d) for d in range(1, lax.axis_size("grp"))]


def call(body, out_shape, **kwargs):
    limit = kwargs.pop("vmem", 48)
    return pl.pallas_call(
        body,
        out_shape=out_shape,
        compiler_params=pltpu.CompilerParams(vmem_limit_bytes=limit * MIB),
        **kwargs,
    )


def shape(dims, kind):
    return jax.ShapeDtypeStruct(dims, kind)


def conv_of(x_ref, pad_ref, mask_ref, vec_ref, cols):
    length = x_ref.shape[0]
    pad_ref[0:ROWS, :] = jnp.zeros((ROWS, LANES), F32)
    pad_ref[ROWS : ROWS + length, :] = x_ref[:, cols]
    total = vec_ref[4:5, cols] + vec_ref[0:1, cols] * x_ref[:, cols]
    shifted = []
    for j in (1, 2, 3):
        earlier = pad_ref[ROWS - j : ROWS - j + length, :] * mask_ref[:, j * LANES : (j + 1) * LANES]
        shifted.append(earlier)
        total = total + vec_ref[j : j + 1, cols] * earlier
    return total, shifted


def conv_fwd_body(x_ref, mask_ref, vec_ref, wdk_ref, inner_ref, part_ref, pad_ref):
    channels = x_ref.shape[1]
    for b in range(channels // LANES):
        cols = slice(b * LANES, (b + 1) * LANES)
        c, _ = conv_of(x_ref, pad_ref, mask_ref, vec_ref, cols)
        inner_ref[:, cols] = (c * sig(c)).astype(BF)
    both = dot(inner_ref[...], wdk_ref[...], 1, 1)
    part_ref[...] = pack(both[:, :RANK], both[:, RANK:])


def pack(low_rank, kq):
    high = kq.astype(BF).astype(F32)
    rest = pltpu.roll(kq - high, 64, axis=1)
    return jnp.concatenate([low_rank, high + rest], axis=1).astype(BF)


def conv_fwd(x, masks, vec, wdk):
    rows, channels = x.shape
    length = 128
    return call(
        conv_fwd_body,
        (shape((rows, channels), BF), shape((rows, 2 * LANES), BF)),
        grid=(rows // length,),
        in_specs=[
            pl.BlockSpec((length, channels), lambda j: (j, 0)),
            pl.BlockSpec((length, 4 * LANES), lambda j: (j, 0)),
            pl.BlockSpec(vec.shape, lambda j: (0, 0)),
            pl.BlockSpec(wdk.shape, lambda j: (0, 0)),
        ],
        out_specs=(
            pl.BlockSpec((length, channels), lambda j: (j, 0)),
            pl.BlockSpec((length, 2 * LANES), lambda j: (j, 0)),
        ),
        scratch_shapes=[pltpu.VMEM((ROWS + length, LANES), F32)],
    )(x, masks, vec, wdk)


def summed_parts(parts, j, length):
    low_rank = jnp.zeros((length, RANK), F32)
    kq = jnp.zeros((length, LANES), F32)
    for d, part in enumerate(parts):
        rows = slice((j ^ d) * length, ((j ^ d) + 1) * length)
        low_rank = low_rank + part[rows, :RANK].astype(F32)
        kq = kq + part[rows, RANK:].astype(F32)
    kq = kq + pltpu.roll(kq, 64, axis=1)
    lane = lax.broadcasted_iota(jnp.int32, (1, LANES), 1)
    return low_rank, jnp.where(lane < 2 * STATE, kq, 0.0)


def rec_body(backward, n_slots, length, width, *refs):
    n_parts = n_slots
    parts, refs = refs[:n_parts], refs[n_parts:]
    if backward:
        (inner, gate, dgated, wdt, vec, mask, gated_out, lr_out, dgate_out, drate_out, dstate_out,
         dpart_out, ddt_out, dvec_out,
         kq_n, kq_i, c_i, lr_n, step_i, p_i, y_i, str_n, hist, dy_i, a_i, b_i, h_scr, dkq_i,
         dlr_n, corr_n) = refs
    else:
        (inner, gate, wdt, vec, mask, gated_out,
         kq_n, kq_i, c_i, lr_n, step_i, p_i, y_i, state) = refs
    nb = width // (2 * LANES)
    first = pl.program_id(0) == 0
    last = pl.program_id(0) == pl.num_programs(0) - 1
    lane = lax.broadcasted_iota(jnp.int32, (1, LANES), 1)
    pieces = [(hh, b, slice((hh * nb + b) * LANES, (hh * nb + b + 1) * LANES)) for hh in (0, 1) for b in range(nb)]

    def rows_of(j):
        return slice(j * length, (j + 1) * length)

    def spread(j, hh):
        return pl.ds(hh * n_slots + j, length, stride=ROWS)

    @pl.when(first)
    def _():
        for j in range(n_slots):
            low_rank, kq = summed_parts(parts, j, length)
            lr_n[rows_of(j), :] = low_rank.astype(BF)
            if backward:
                lr_out[rows_of(j), :] = low_rank.astype(BF)
            kq_n[rows_of(j), :] = kq
            for hh in (0, 1):
                kq_i[spread(j, hh), :] = kq
                c_i[spread(j, hh), :] = mask[rows_of(j), 0:LANES]
        if backward:
            dkq_i[...] = jnp.zeros(dkq_i.shape, F32)
            dlr_n[...] = jnp.zeros(dlr_n.shape, F32)
            corr_n[...] = jnp.zeros(corr_n.shape, F32)

    for j in range(n_slots):
        rows = rows_of(j)
        rate = dot(lr_n[rows, :], wdt[...], 1, 0)
        kq = kq_n[rows, :]
        ks = jnp.sum(jnp.where(lane < STATE, kq * kq, 0.0), axis=1, keepdims=True)
        for hh, b, cols in pieces:
            strength = sig(rate[:, cols] + vec[0:1, cols])
            step = strength / (1.0 + strength * ks)
            step_i[b, spread(j, hh), :] = step
            p_i[b, spread(j, hh), :] = step * inner[rows, cols].astype(F32)
            if backward:
                str_n[rows, cols] = strength
                g = gate[rows, cols]
                dy_i[b, spread(j, hh), :] = dgated[rows, cols] * (g * sig(g))

    def lanes_of(kq, n):
        return jnp.broadcast_to(kq[:, n : n + 1], (ROWS, LANES))

    if backward:
        hist[0] = jnp.zeros(hist.shape[1:], F32)
    else:
        state[...] = jnp.zeros(state.shape, F32)

    def forward_step(t, carry):
        now = pl.ds(pl.multiple_of(t * ROWS, ROWS), ROWS)
        kq, c = kq_i[now, :], c_i[now, :]
        steps = [step_i[b, now, :] for b in range(nb)]
        ps = [p_i[b, now, :] for b in range(nb)]
        ys = [jnp.zeros((ROWS, LANES), F32) for _ in range(nb)]
        for n in range(STATE):
            k, q = lanes_of(kq, n), lanes_of(kq, STATE + n)
            ck2 = c * k * k
            for b in range(nb):
                before = hist[t, n * nb + b] if backward else state[n * nb + b]
                after = (c - ck2 * steps[b]) * before + k * ps[b]
                if backward:
                    hist[t + 1, n * nb + b] = after
                else:
                    state[n * nb + b] = after
                ys[b] = ys[b] + q * after
        for b in range(nb):
            y_i[b, now, :] = ys[b]
        return carry

    lax.fori_loop(0, length, forward_step, 0)

    if not backward:
        for j in range(n_slots):
            rows = rows_of(j)
            for hh, b, cols in pieces:
                y = y_i[b, spread(j, hh), :] + vec[1:2, cols] * inner[rows, cols].astype(F32)
                g = gate[rows, cols]
                gated_out[rows, cols] = (y * (g * sig(g))).astype(BF)
        return

    h_scr[...] = jnp.zeros(h_scr.shape, F32)

    def backward_step(i, carry):
        t = length - 1 - i
        now = pl.ds(pl.multiple_of(t * ROWS, ROWS), ROWS)
        kq, c = kq_i[now, :], c_i[now, :]
        steps = [step_i[b, now, :] for b in range(nb)]
        ps = [p_i[b, now, :] for b in range(nb)]
        dys = [dy_i[b, now, :] for b in range(nb)]
        a_sum = [jnp.zeros((ROWS, LANES), F32) for _ in range(nb)]
        b_sum = [jnp.zeros((ROWS, LANES), F32) for _ in range(nb)]
        out = jnp.zeros((ROWS, LANES), F32)
        for n in range(STATE):
            k, q = lanes_of(kq, n), lanes_of(kq, STATE + n)
            ck = c * k
            ck2 = ck * k
            dk1 = dk2 = dq = None
            for b in range(nb):
                before, after = hist[t, n * nb + b], hist[t + 1, n * nb + b]
                grad = dys[b] * q + h_scr[n * nb + b]
                a_sum[b] = a_sum[b] + grad * k
                both = grad * before
                b_sum[b] = b_sum[b] + ck2 * both
                h_scr[n * nb + b] = (c - ck2 * steps[b]) * grad
                one, two, three = ps[b] * grad, steps[b] * both, dys[b] * after
                dk1 = one if dk1 is None else dk1 + one
                dk2 = two if dk2 is None else dk2 + two
                dq = three if dq is None else dq + three
            dk = dk1 - (2.0 * ck) * dk2
            out = jnp.where(lane == n, jnp.sum(dk, axis=1, keepdims=True), out)
            out = jnp.where(lane == STATE + n, jnp.sum(dq, axis=1, keepdims=True), out)
        for b in range(nb):
            a_i[b, now, :] = a_sum[b]
            b_i[b, now, :] = b_sum[b]
        dkq_i[now, :] = dkq_i[now, :] + out
        return carry

    lax.fori_loop(0, length, backward_step, 0)

    ddt = [jnp.zeros((1, LANES), F32) for _ in pieces]
    dskip = [jnp.zeros((1, LANES), F32) for _ in pieces]
    for j in range(n_slots):
        rows = rows_of(j)
        kq = kq_n[rows, :]
        ks = jnp.sum(jnp.where(lane < STATE, kq * kq, 0.0), axis=1, keepdims=True)
        corr = jnp.zeros((length, 1), F32)
        for i, (hh, b, cols) in enumerate(pieces):
            at = spread(j, hh)
            inn = inner[rows, cols].astype(F32)
            a, step, dy = a_i[b, at, :], step_i[b, at, :], dy_i[b, at, :]
            skip = vec[1:2, cols]
            dstep = inn * a - b_i[b, at, :]
            strength = str_n[rows, cols]
            inv = 1.0 / (1.0 + strength * ks)
            drate = (dstep * (inv * inv) * (strength * (1.0 - strength))).astype(BF)
            drate_out[rows, cols] = drate
            dstate_out[rows, cols] = step * a + skip * dy
            corr = corr + jnp.sum(dstep * (step * step), axis=1, keepdims=True)
            y = y_i[b, at, :] + skip * inn
            g = gate[rows, cols]
            s = sig(g)
            gated_out[rows, cols] = (y * (g * s)).astype(BF)
            dgate_out[rows, cols] = (dgated[rows, cols] * y * (s * (1.0 + g * (1.0 - s)))).astype(BF)
            ddt[i] = ddt[i] + jnp.sum(drate.astype(F32), axis=0, keepdims=True)
            dskip[i] = dskip[i] + jnp.sum(dy * inn, axis=0, keepdims=True)
        corr_n[rows, :] = corr_n[rows, :] + corr
        dlr_n[rows, :] = dlr_n[rows, :] + dot(drate_out[rows, :], wdt[...], 1, 1)
    ddt_out[...] = dot(lr_n[...], drate_out[...], 0, 0)
    dvec_out[...] = jnp.concatenate(
        [jnp.concatenate(ddt, axis=1), jnp.concatenate(dskip, axis=1), jnp.zeros((6, width), F32)], axis=0
    )

    @pl.when(last)
    def _():
        for j in range(n_slots):
            rows = rows_of(j)
            dkq = dkq_i[spread(j, 0), :] + dkq_i[spread(j, 1), :]
            dkq = dkq - jnp.where(lane < STATE, 2.0 * kq_n[rows, :] * corr_n[rows, :], 0.0)
            dpart_out[rows, :] = pack(dlr_n[rows, :], dkq)


def rec(backward, parts, inner, gate, dgated, wdt, vec, masks):
    rows, channels = inner.shape
    n_slots = len(parts)
    length = rows // n_slots
    width = channels // 2
    nb = width // (2 * LANES)

    def whole(a):
        return pl.BlockSpec(a.shape, lambda i: (0,) * a.ndim)

    def block(n):
        return pl.BlockSpec((n, width), lambda i: (0, i))

    wide = pltpu.VMEM((nb, ROWS * length, LANES), F32)
    row = pltpu.VMEM((rows, LANES), F32)
    spread = pltpu.VMEM((ROWS * length, LANES), F32)
    scratch = [row, spread, spread, pltpu.VMEM((rows, RANK), BF), wide, wide, wide]
    if not backward:
        scratch += [pltpu.VMEM((STATE * nb, ROWS, LANES), F32)]
        return call(
            partial(rec_body, False, n_slots, length, width),
            shape((rows, channels), BF),
            grid=(2,),
            in_specs=[whole(p) for p in parts] + [block(rows), block(rows), block(RANK), block(vec.shape[0]), whole(masks)],
            out_specs=block(rows),
            scratch_shapes=scratch,
        )(*parts, inner, gate, wdt, vec, masks)
    scratch += [
        pltpu.VMEM((rows, width), F32),
        pltpu.VMEM((length + 1, STATE * nb, ROWS, LANES), F32),
        wide,
        wide,
        wide,
        pltpu.VMEM((STATE * nb, ROWS, LANES), F32),
        spread,
        pltpu.VMEM((rows, RANK), F32),
        row,
    ]
    lr_like = shape((rows, RANK), BF)
    part_like = shape((rows, 2 * LANES), BF)
    return call(
        partial(rec_body, True, n_slots, length, width),
        (
            shape((rows, channels), BF),
            lr_like,
            shape((rows, channels), BF),
            shape((rows, channels), BF),
            shape((rows, channels), F32),
            part_like,
            shape((RANK, channels), F32),
            shape((ROWS, channels), F32),
        ),
        grid=(2,),
        in_specs=[whole(p) for p in parts]
        + [block(rows), block(rows), block(rows), block(RANK), block(vec.shape[0]), whole(masks)],
        out_specs=(block(rows), whole(lr_like), block(rows), block(rows), block(rows), whole(part_like), block(RANK), block(ROWS)),
        scratch_shapes=scratch,
        vmem=60,
    )(*parts, inner, gate, dgated, wdt, vec, masks)


def conv_bwd_body(n_slots, p0, p1, p2, p3, x_ref, inner, dstate, mask_ref, vec_ref, wdk_ref,
                  dx_out, dsmall_out, dvec_out, pad_ref, late_ref, dcat):
    j = pl.program_id(0)
    length, channels = x_ref.shape
    lane = lax.broadcasted_iota(jnp.int32, (1, LANES), 1)

    @pl.when(j == 0)
    def _():
        dsmall_out[...] = jnp.zeros(dsmall_out.shape, F32)
        dvec_out[...] = jnp.zeros(dvec_out.shape, F32)

    low_rank = jnp.zeros((length, RANK), F32)
    kq = jnp.zeros((length, LANES), F32)
    for d, part in enumerate((p0, p1, p2, p3)):
        rows = pl.ds(pl.multiple_of((j ^ d) * length, length), length)
        low_rank = low_rank + part[rows, :RANK].astype(F32)
        kq = kq + part[rows, RANK:].astype(F32)
    kq = kq + pltpu.roll(kq, 64, axis=1)
    dcat[:, :RANK] = low_rank.astype(BF)
    dcat[:, RANK:] = jnp.where(lane < 2 * STATE, kq, 0.0).astype(BF)
    dsmall_out[...] += dot(dcat[...], inner[...], 0, 0)
    late_ref[length : length + ROWS, :] = jnp.zeros((ROWS, LANES), F32)
    for b in range(channels // LANES):
        cols = slice(b * LANES, (b + 1) * LANES)
        c, earlier = conv_of(x_ref, pad_ref, mask_ref, vec_ref, cols)
        dinner = dstate[:, cols] + dot(dcat[...], wdk_ref[:, cols], 1, 0)
        s = sig(c)
        dc = dinner * (s * (1.0 + c * (1.0 - s)))
        dx = vec_ref[0:1, cols] * dc
        sums = [jnp.sum(dc * x_ref[:, cols], axis=0, keepdims=True)]
        for lag in (1, 2, 3):
            sums.append(jnp.sum(dc * earlier[lag - 1], axis=0, keepdims=True))
            late_ref[0:length, :] = dc * mask_ref[:, lag * LANES : (lag + 1) * LANES]
            dx = dx + vec_ref[lag : lag + 1, cols] * late_ref[lag : lag + length, :]
        sums.append(jnp.sum(dc, axis=0, keepdims=True))
        dx_out[:, cols] = dx.astype(BF)
        for i, value in enumerate(sums):
            dvec_out[i : i + 1, cols] += value


def conv_bwd(parts, x, inner, dstate, masks, vec, wdk):
    rows, channels = x.shape
    n_slots = len(parts)
    length = rows // n_slots

    def whole(a):
        return pl.BlockSpec(a.shape, lambda i: (0,) * a.ndim)

    slot = pl.BlockSpec((length, channels), lambda j: (j, 0))
    small = shape((2 * LANES, channels), F32)
    vecs = shape((ROWS, channels), F32)
    return call(
        partial(conv_bwd_body, n_slots),
        (shape((rows, channels), BF), small, vecs),
        grid=(n_slots,),
        in_specs=[whole(p) for p in parts]
        + [slot, slot, slot, pl.BlockSpec((length, 4 * LANES), lambda j: (j, 0)), whole(vec), whole(wdk)],
        out_specs=(slot, whole(small), whole(vecs)),
        scratch_shapes=[
            pltpu.VMEM((ROWS + length, LANES), F32),
            pltpu.VMEM((ROWS + length, LANES), F32),
            pltpu.VMEM((length, 2 * LANES), BF),
        ],
    )(*parts, x, inner, dstate, masks, vec, wdk)


def norm(hidden, gain):
    rms = lax.rsqrt(jnp.mean(hidden * hidden, axis=1, keepdims=True) + EPSILON)
    return (hidden * rms * gain[None, :]).astype(BF), rms


def norm_back(hidden, rms, gain, dnormed, dout):
    a = hidden * rms
    scaled = dnormed * gain[None, :]
    dh = dout + rms * (scaled - a * jnp.mean(scaled * a, axis=1, keepdims=True))
    return dh, jnp.sum(dnormed * a, axis=0)


def slot_masks(lengths, length):
    ends = jnp.cumsum(lengths, axis=1)
    position = jnp.arange(length, dtype=jnp.int32)
    segment = jnp.sum((position[None, :, None] >= ends[:, None, :]).astype(jnp.int32), axis=2)
    valid = (position[None, :] < ends[:, -1:]).astype(F32)
    same = []
    for lag in (1, 2, 3):
        before = jnp.concatenate([jnp.full((segment.shape[0], lag), -1, jnp.int32), segment[:, :-lag]], axis=1)
        same.append((before == segment).astype(F32))
    stack = jnp.stack([same[0]] + same, axis=2).reshape(-1, 4, 1)
    spread = jnp.broadcast_to(stack, stack.shape[:2] + (LANES,)).reshape(-1, 4 * LANES)
    return spread, valid


def on_device(boundary, doc_lengths, norm_gain, in_weight, conv_weight, conv_bias, down_weight, kq_weight,
              dt_weight, dt_bias, skip_weight, out_weight):
    s = lax.axis_index("section")
    g = lax.axis_index("grp")
    z = lax.axis_index("dp")
    n_grp = lax.axis_size("grp")
    n_dp = lax.axis_size("dp")
    length, width = boundary.shape[3], boundary.shape[4]
    inner = in_weight.shape[2] // 2
    block = inner // n_dp
    sub = block // (2 * n_grp)
    half = sub * n_dp
    mine_first = s == 0

    def pick(first, second):
        return jnp.where(mine_first, first, second)

    small = jnp.concatenate(
        [down_weight[0].T, kq_weight[0], jnp.zeros((2 * LANES - RANK - 2 * STATE, block), BF), dt_weight[0],
         conv_weight[0], conv_bias, dt_bias, skip_weight], axis=0)

    def columns(array, which):
        blocks = array.shape[1] // block
        view = array.reshape(array.shape[0], blocks, n_grp, 2, sub)
        view = lax.dynamic_index_in_dim(view, g, 2, keepdims=False)
        return lax.dynamic_index_in_dim(view, which, 2, keepdims=False).reshape(array.shape[0], blocks * sub)

    def out_rows(which):
        view = out_weight[0].reshape(n_grp, 2, sub, width)
        view = lax.dynamic_index_in_dim(view, g, 0, keepdims=False)
        return lax.dynamic_index_in_dim(view, which, 0, keepdims=False)

    def shards(which):
        w_x = columns(in_weight[0, :, :inner], which)
        w_g = columns(in_weight[0, :, inner:], which)
        return w_x, w_g, columns(small, which), out_rows(which)

    keep, send = shards(s), shards(1 - s)
    come = [swap(piece, "section", 1) for piece in send]
    layers = []
    gains = lax.all_gather(norm_gain[0], "dp", axis=0, tiled=True)
    gains_other = swap(gains, "section", 1)
    for l in (0, 1):
        w_x, w_g, w_s, w_o = [pick(a, b) if l == 0 else pick(b, a) for a, b in zip(keep, come)]
        w_x = lax.all_gather(w_x, "dp", axis=0, tiled=True)
        w_g = lax.all_gather(w_g, "dp", axis=0, tiled=True)
        w_s = lax.all_gather(w_s, "dp", axis=1, tiled=True)
        w_o = lax.all_gather(w_o, "dp", axis=0, tiled=True)
        w_x = jnp.concatenate([w_x, swap(w_x, "section", 1)], axis=1)
        w_g = jnp.concatenate([w_g, swap(w_g, "section", 1)], axis=1)
        w_s = jnp.concatenate([w_s, swap(w_s, "section", 1)], axis=1)
        w_o = jnp.concatenate([w_o, swap(w_o, "section", 1)], axis=0)
        gain = (pick(gains, gains_other) if l == 0 else pick(gains_other, gains)).astype(F32)
        cat = w_s[: 2 * LANES]
        wdt = w_s[2 * LANES : 2 * LANES + RANK]
        tail = w_s[2 * LANES + RANK :].astype(F32)
        conv_vec = jnp.concatenate([tail[:5], jnp.zeros((3, tail.shape[1]), F32)], axis=0)
        rate_vec = jnp.concatenate([tail[5:7], jnp.zeros((6, tail.shape[1]), F32)], axis=0)
        layers.append((gain, w_x, w_g, w_o, cat, wdt, conv_vec, rate_vec))

    rows = boundary[0, :, 0]
    traded = swap(pick(rows[1], rows[0]), "section", 1)
    hidden = pick(rows[0], traded)
    cotangent = pick(traded, rows[1])
    lengths = lax.dynamic_index_in_dim(doc_lengths[:, 0], s, 0, keepdims=True)
    all_lengths = jnp.concatenate([lengths] + peers(lengths), axis=0)
    masks, valid = slot_masks(all_lengths, length)
    valid = valid[0][:, None]

    def group(value):
        return jnp.concatenate([value] + peers(value), axis=0)

    def scatter(value):
        total = value[:length].astype(F32)
        for d in range(1, n_grp):
            total = total + swap(value[d * length : (d + 1) * length], "grp", d).astype(F32)
        return total

    def forward(h, layer):
        gain, w_x, w_g, w_o, cat, wdt, conv_vec, rate_vec = layer
        normed, rms = norm(h, gain)
        normed = group(normed)
        x = dot(normed, w_x, 1, 0)
        gate = dot(normed, w_g, 1, 0)
        act, part = conv_fwd(x, masks, conv_vec, cat)
        return rms, normed, x, gate, act, [part] + peers(part)

    def backward(h, dout, dbranch, layer, saved, dgated, rec_out):
        gain, w_x, w_g, w_o, cat, wdt, conv_vec, rate_vec = layer
        rms, normed, x, gate, act, parts = saved
        gated, lr, dgate, drate, dstate, dpart, ddt, dvec = rec_out
        dx, dsmall, dconv = conv_bwd([dpart] + peers(dpart), x, act, dstate, masks, conv_vec, cat)
        dnormed = (dot(dx, w_x, 1, 1) + dot(dgate, w_g, 1, 1)).astype(BF)
        dnormed = scatter(dnormed)
        dh, dgain = norm_back(h, rms, gain, dnormed, dout)

        def both(left, right, left_own, right_own):
            left_far = swap(left[:, half:] if left_own else left, "section", 1)
            right_far = swap(right[:, half:] if right_own else right, "section", 1)
            left_near = left[:, :half] if left_own else left
            right_near = right[:, :half] if right_own else right
            return (dot(left_near, right_near, 0, 0) + dot(left_far, right_far, 0, 0)).astype(BF)

        grad_x = both(normed, dx, False, True)
        grad_g = both(normed, dgate, False, True)
        grad_o = both(gated, dbranch, True, False)
        grad_s = jnp.concatenate([dsmall, ddt, dconv[:5], dvec[:2], jnp.zeros((1, ddt.shape[1]), F32)], axis=0)
        grad_s = (grad_s[:, :half] + swap(grad_s[:, half:].astype(BF), "section", 1).astype(F32)).astype(BF)
        return dh, dgain, (grad_x, grad_g, grad_o, grad_s)

    h0 = hidden.astype(F32)
    saved0 = forward(h0, layers[0])
    gated0 = rec(False, saved0[5], saved0[4], saved0[3], None, layers[0][5], layers[0][7], masks)
    branch0 = scatter(dot(gated0, layers[0][3], 1, 0, BF))
    h1 = (h0 + valid * branch0).astype(BF).astype(F32)
    saved1 = forward(h1, layers[1])
    dout1 = cotangent.astype(F32)
    dbranch1 = group((valid * dout1).astype(BF))
    dgated1 = dot(dbranch1, layers[1][3], 1, 1)
    rec1 = rec(True, saved1[5], saved1[4], saved1[3], dgated1, layers[1][5], layers[1][7], masks)
    branch1 = scatter(dot(rec1[0], layers[1][3], 1, 0, BF))
    out1 = h1 + valid * branch1
    dh1, dgain1, grads1 = backward(h1, dout1, dbranch1, layers[1], saved1, dgated1, rec1)
    dout0 = dh1.astype(BF).astype(F32)
    dbranch0 = group((valid * dout0).astype(BF))
    dgated0 = dot(dbranch0, layers[0][3], 1, 1)
    rec0 = rec(True, saved0[5], saved0[4], saved0[3], dgated0, layers[0][5], layers[0][7], masks)
    dh0, dgain0, grads0 = backward(h0, dout0, dbranch0, layers[0], saved0, dgated0, rec0)

    far = swap(pick(out1, dh0), "section", 1)
    result = pick(jnp.stack([dh0, far]), jnp.stack([far, out1]))
    result = result.reshape(1, 2, 1, length, width)

    def reduced(grads):
        grad_x, grad_g, grad_o, grad_s = grads
        return (
            lax.psum_scatter(grad_x, "dp", scatter_dimension=0, tiled=True),
            lax.psum_scatter(grad_g, "dp", scatter_dimension=0, tiled=True),
            lax.psum_scatter(grad_o, "dp", scatter_dimension=0, tiled=True),
            lax.psum_scatter(grad_s, "dp", scatter_dimension=1, tiled=True),
        )

    red0, red1 = reduced(grads0), reduced(grads1)
    collected = []
    for first, second in zip(red0, red1):
        near, away = pick(first, second), pick(second, first)
        far = swap(away, "section", 1)
        halves = pick(jnp.stack([near, far]), jnp.stack([far, near]))
        collected.append(lax.all_gather(halves, "grp", axis=0).astype(F32))
    g_x, g_g, g_o, g_s = collected
    rows_in = g_x.shape[2]

    def side(value):
        value = value.reshape(n_grp, 2, rows_in, n_dp, sub)
        return value.transpose(2, 3, 0, 1, 4).reshape(rows_in, inner)

    grad_in = jnp.concatenate([side(g_x), side(g_g)], axis=1)
    grad_out = g_o.reshape(block, width)
    grad_small = g_s.transpose(2, 0, 1, 3).reshape(g_s.shape[2], block)
    gain_sum = lax.psum(jnp.stack([dgain0, dgain1]), ("section", "grp", "dp"))
    gain_sum = lax.dynamic_index_in_dim(gain_sum, s, 0, keepdims=False)
    grad_gain = lax.dynamic_slice_in_dim(gain_sum, z * norm_gain.shape[1], norm_gain.shape[1], 0)
    base = 2 * LANES + RANK
    return (
        result,
        grad_gain[None],
        grad_in[None],
        grad_small[None, base : base + 4],
        grad_small[base + 4][None],
        grad_small[:RANK].T[None],
        grad_small[None, RANK : RANK + 2 * STATE],
        grad_small[None, 2 * LANES : base],
        grad_small[base + 5][None],
        grad_small[base + 6][None],
        grad_out[None],
    )


def solution(mesh):
    return jax.shard_map(
        on_device,
        mesh=mesh,
        in_specs=(
            P("section", None, ("grp", "dp"), None, None),
            P(None, ("grp", "dp"), None),
            P("section", "dp"),
            P("section", "dp", None),
            P("section", None, "dp"),
            P("section", "dp"),
            P("section", "dp", None),
            P("section", None, "dp"),
            P("section", None, "dp"),
            P("section", "dp"),
            P("section", "dp"),
            P("section", "dp", None),
        ),
        out_specs=(
            P("section", None, ("grp", "dp"), None, None),
            P("section", "dp"),
            P("section", "dp", None),
            P("section", None, "dp"),
            P("section", "dp"),
            P("section", "dp", None),
            P("section", None, "dp"),
            P("section", None, "dp"),
            P("section", "dp"),
            P("section", "dp"),
            P("section", "dp", None),
        ),
        check_vma=False,
    )
```

time: 5490 us -> 1730 us (0.32)
  waiting for transfers between devices: 2670 us -> 548 us
  other arithmetic: 1820 us -> 56.5 us
  Pallas kernels: 0 us -> 690 us
  local copies, waits for them, and re-layouts: 461 us -> 160 us
  matrix products: 334 us -> 89.4 us
    reduce_sum x542 -> x5, other arithmetic: 1390 us -> 5.41 us  [the longest x2 2.68 us: norm(): rms = lax.rsqrt(jnp.mean(hidden * hidden, axis=1, keepdims=True) + EPSILON)]
    pallas_call x0 -> x7, Pallas kernels: none -> 690 us  [the longest x2 632 us: rec(): call(partial(rec_body, True, n_slots, length, width), (shape((rows, chann...]
    all_gather x4 -> x9, waiting for transfers between devices: 826 us -> 182 us  [the longest x2 86 us: on_device(): w_o = lax.all_gather(w_o, 'dp', axis=0, tiled=True)]
    ppermute x4 -> x70, waiting for transfers between devices: 754 us -> 191 us  [swap(): lax.ppermute(value, axis, [(i, i ^ shift) for i in range(lax.axis_size(ax...]
    unnamed x13 -> x19, waiting for transfers between devices: 558 us -> 1.46 us
    dot_general x36 -> x24, matrix products: 334 us -> 89.4 us  [dot(): lax.dot_general(left, right, (((left_axis,), (right_axis,)), ((), ())), p...]
    psum x1 -> x0, waiting for transfers between devices: 232 us -> none  [on_device(): lax.psum(row_sums[1].astype(jnp.bfloat16), 'grp').astype(jnp.float32)]
    mul x678 -> x1, other arithmetic: 198 us -> 0.01 us  [on_device(): h1 = (h0 + valid * branch0).astype(BF).astype(F32)]
  transfers between devices with their start and end apart: 15 -> 87, of which waited for: 8 -> 47; matrix products, arithmetic and copies ran while one was open for 2% -> 15% of each run, Pallas kernels for 0% -> 21%
where the time goes in v1:
time: 1730 us; the launch traced here: 1720 us
  Pallas kernels  690 us (40%)
  waiting for transfers between devices  548 us (32%)
  local copies, waits for them, and re-layouts  160 us (9%)
  blocking collectives  107 us (6%)
  matrix products  89.4 us (5%)
  other arithmetic  56.5 us (3%)
  starting transfers between devices  56 us (3%)
    pallas_call x2, Pallas kernels, rec(): call(partial(rec_body, True, n_slots, length, width), (shape((rows, chann...  632 us
    ppermute x70, waiting for transfers between devices, swap(): lax.ppermute(value, axis, [(i, i ^ shift) for i in range(lax.axis_size(ax...  191 us
    dot_general x24, matrix products, dot(): lax.dot_general(left, right, (((left_axis,), (right_axis,)), ((), ())), p...  89.4 us
    reduce_scatter x2, waiting for transfers between devices, reduced(): lax.psum_scatter(grad_x, 'dp', scatter_dimension=0, tiled=True)  86.5 us
    reduce_scatter x2, waiting for transfers between devices, reduced(): lax.psum_scatter(grad_o, 'dp', scatter_dimension=0, tiled=True)  86.3 us
    all_gather x2, waiting for transfers between devices, on_device(): w_o = lax.all_gather(w_o, 'dp', axis=0, tiled=True)  86 us
    ppermute x70, starting transfers between devices, swap(): lax.ppermute(value, axis, [(i, i ^ shift) for i in range(lax.axis_size(ax...  54.7 us
    all_gather x2, waiting for transfers between devices, on_device(): w_g = lax.all_gather(w_g, 'dp', axis=0, tiled=True)  43.6 us
  transfers between devices with their start and end apart: 87, of which 47 were waited for; matrix products, arithmetic and copies ran while one was open for 15% of the time, Pallas kernels for 21%

profile of v1, /device:TPU:0, one launch (start us, length us, event | category | flops | bytes accessed | tf_op | source)
XLA Modules:
  0.0 1722.2 jit_solution(6261240540651476720)
XLA Ops:
  21.0 8.4 dynamic-slice_reduce_fusion.3
  40.6 8.4 dynamic-slice_reduce_fusion.1
  64.1 12.7 all-gather
  81.2 14.1 all_gather.45
  95.3 24.9 %all_gather.49 = bf16[391,512]{1,0:T(8,128)(2,1)S(1)} all-gather(bf16[391,128]{1,0:T(8,128)(2,1)S(1)} %get-tuple-element.160), channel_id=1, replica_groups=mesh['section'=2,'grp'=4,'dp'=4] {'dp'}, dimensions={1}, use_global_device_ids=true | all-gather | bytes 500480 | tf_op jit(solution)/shard_map/all_gather | solution.py:488
  140.4 42.2 %all-gather.17.cloned.1.call-done = bf16[2048,512]{1,0:T(8,128)(2,1)} async-done(((bf16[512,512]{1,0:T(8,128)(2,1)}), bf16[2048,512]{1,0:T(8,128)(2,1)}) %all-gather.17.cloned.1.call-update) | async-done | bytes 2097168 | tf_op jit(solution)/shard_map/all_gather | solution.py:486
  185.7 43.1 %all-gather.15.cloned.1.call-done = bf16[512,2048]{1,0:T(8,128)(2,1)} async-done(((bf16[128,2048]{1,0:T(8,128)(2,1)}), bf16[512,2048]{1,0:T(8,128)(2,1)}) %all-gather.15.cloned.1.call-update) | async-done | bytes 2097168 | tf_op jit(solution)/shard_map/all_gather | solution.py:489
  231.9 42.9 %all-gather.19.cloned.1.call-done = bf16[2048,512]{1,0:T(8,128)(2,1)} async-done(((bf16[512,512]{1,0:T(8,128)(2,1)}), bf16[2048,512]{1,0:T(8,128)(2,1)}) %all-gather.19.cloned.1.call-update) | async-done | bytes 2097168 | tf_op jit(solution)/shard_map/all_gather | solution.py:487
  278.0 43.0 %all-gather.21.cloned.1.call-done = bf16[512,2048]{1,0:T(8,128)(2,1)} async-done(((bf16[128,2048]{1,0:T(8,128)(2,1)}), bf16[512,2048]{1,0:T(8,128)(2,1)}) %all-gather.21.cloned.1.call-update) | async-done | bytes 2097168 | tf_op jit(solution)/shard_map/all_gather | solution.py:489
  355.6 17.0 collective-permute-done.13.refs_2_
  372.6 35.9 %shard_map.204 = bf16[512,1024]{1,0:T(8,128)(2,1)S(1)} custom-call(bf16[512,256]{1,0:T(8,128)(2,1)S(1)} %get-tuple-element.33.refs_0_, bf16[512,256]{1,0:T(8,128)(2,1)S(1)} %collective-permute-done.12.refs_1_, bf16[512,256]{1,0:T(8,128)(2,1)S(1)} %collective-permute-done.13.refs_2_, bf16[512,256]{1,0:T(8,128)(2,1)S(1)} %collective-permute-done.14.refs_3_, ...), custom_call_target="tpu_custom_call" | custom-call | tf_op jit(solution)/shard_map/pallas_call | solution.py:308
  420.7 8.7 collective-permute-done.21
  430.0 8.9 collective-permute-done.20
  463.1 9.4 collective-permute-done.23
  494.0 315.7 %shard_map.206 = (bf16[512,1024]{1,0:T(8,128)(2,1)}, bf16[512,128]{1,0:T(8,128)(2,1)}, bf16[512,1024]{1,0:T(8,128)(2,1)}, bf16[512,1024]{1,0:T(8,128)(2,1)}, f32...) custom-call(bf16[512,256]{1,0:T(8,128)(2,1)} %copy-done.30, ...), custom_call_target="tpu_custom_call" | custom-call | tf_op jit(solution)/shard_map/pallas_call | solution.py:329
  843.9 9.2 collective-permute-done.40
  867.0 12.3 collective-permute-done.43
  879.3 9.1 collective-permute-done.42
  892.1 316.1 %shard_map.208 = (bf16[512,1024]{1,0:T(8,128)(2,1)}, bf16[512,128]{1,0:T(8,128)(2,1)}, bf16[512,1024]{1,0:T(8,128)(2,1)}, bf16[512,1024]{1,0:T(8,128)(2,1)}, f32...) custom-call(bf16[512,256]{1,0:T(8,128)(2,1)} %copy-done.19, ...), custom_call_target="tpu_custom_call" | custom-call | tf_op jit(solution)/shard_map/pallas_call | solution.py:329
  1310.4 41.0 %reduce-scatter.15.cloned.1.call-done = bf16[512,512]{1,0:T(8,128)(2,1)} async-done(((bf16[2048,512]{1,0:T(8,128)(2,1)}), bf16[512,512]{1,0:T(8,128)(2,1)}) %reduce-scatter.15.cloned.1.call-update) | async-done | bytes 524304 | tf_op jit(solution)/shard_map/reduce_scatter | solution.py:578
  1351.4 45.5 %reduce-scatter.13.cloned.1.call-done = bf16[512,512]{1,0:T(8,128)(2,1)} async-done(((bf16[2048,512]{1,0:T(8,128)(2,1)}), bf16[512,512]{1,0:T(8,128)(2,1)}) %reduce-scatter.13.cloned.1.call-update) | async-done | bytes 524304 | tf_op jit(solution)/shard_map/reduce_scatter | solution.py:578
  1401.5 40.8 %reduce-scatter.23.cloned.1.call-done = bf16[128,2048]{1,0:T(8,128)(2,1)} async-done(((bf16[512,2048]{1,0:T(8,128)(2,1)}), bf16[128,2048]{1,0:T(8,128)(2,1)}) %reduce-scatter.23.cloned.1.call-update) | async-done | bytes 524304 | tf_op jit(solution)/shard_map/reduce_scatter | solution.py:580
  1442.4 45.5 %reduce-scatter.21.cloned.1.call-done = bf16[128,2048]{1,0:T(8,128)(2,1)} async-done(((bf16[512,2048]{1,0:T(8,128)(2,1)}), bf16[128,2048]{1,0:T(8,128)(2,1)}) %reduce-scatter.21.cloned.1.call-update) | async-done | bytes 524304 | tf_op jit(solution)/shard_map/reduce_scatter | solution.py:580
  1522.1 9.8 collective-permute-done.48
  1534.0 9.1 collective-permute-done.52
  1543.1 20.3 %collective-permute-done.51 = bf16[128,2048]{1,0:T(8,128)(2,1)} collective-permute-done((bf16[128,2048]{1,0:T(8,128)(2,1)}, bf16[128,2048]{1,0:T(8,128)(2,1)}, u32[]{:S(2)}, u32[]{:S(2)}) %collective-permute-start.51) | collective-permute-done | bytes 524320 | tf_op jit(solution)/shard_map/ppermute | solution.py:31
  1569.6 38.7 %psum.7 = f32[2,2048]{1,0:T(2,128)S(1)} all-reduce(f32[2,2048]{1,0:T(2,128)S(1)} %pad_maximum_fusion.4), channel_id=1, replica_groups=mesh['section'=2,'grp'=4,'dp'=4] {'section','grp','dp'}, use_global_device_ids=true, to_apply=%region_8.9 | all-reduce | flops 4096 | bytes 32768 | tf_op jit(solution)/shard_map/psum | solution.py:601
  1609.0 16.2 all_gather.54
  1642.2 10.7 copy.139
  1667.9 10.7 copy.138
  1686.4 11.8 fusion
  1698.3 10.2 all-gather.27.cloned.1.call-done
  (558 shorter events, 413.7 us)
Async XLA Ops:
  7.2 123.3 %all-gather.11.cloned.1.call-start = ((), (), s32[]{:S(2)}) async-start(), calls=%async_computation.8 | async-start | bytes 2621440 | tf_op jit(solution)/shard_map/all_gather | solution.py:486
  32.6 103.0 %all-gather.13.cloned.1.call-start = ((), (), s32[]{:S(2)}) async-start(), calls=%async_computation.9 | async-start | bytes 2621440 | tf_op jit(solution)/shard_map/all_gather | solution.py:487
  52.2 130.4 %all-gather.17.cloned.1.call-start = ((), (), s32[]{:S(2)}) async-start(), calls=%async_computation.11 | async-start | bytes 2621440 | tf_op jit(solution)/shard_map/all_gather | solution.py:486
  52.9 175.8 %all-gather.15.cloned.1.call-start = ((), (), s32[]{:S(2)}) async-start(), calls=%async_computation.10 | async-start | bytes 2621440 | tf_op jit(solution)/shard_map/all_gather | solution.py:489
  58.2 216.6 %all-gather.19.cloned.1.call-start = ((), (), s32[]{:S(2)}) async-start(), calls=%async_computation.12 | async-start | bytes 2621440 | tf_op jit(solution)/shard_map/all_gather | solution.py:487
  58.8 262.2 %all-gather.21.cloned.1.call-start = ((), (), s32[]{:S(2)}) async-start(), calls=%async_computation.13 | async-start | bytes 2621440 | tf_op jit(solution)/shard_map/all_gather | solution.py:489
  64.1 64.2 %collective-permute-start = (bf16[128,2048]{1,0:T(8,128)(2,1)}, bf16[128,2048]{1,0:T(8,128)(2,1)}, u32[]{:S(2)}, u32[]{:S(2)}) collective-permute-start(bf16[128,2048]{1,0:T(8,128)(2,1)} %bitcast_select_fusion.7), channel_id=1, source_target_pairs={{0,16},{16,0},{1,17},{17,1},{2,18},{18,2},{3,19},{19,3},{4,20},{20... | collective-permute-start | bytes 1572872 | tf_op jit(solution)/shard_map/ppermute | solution.py:31
  76.8 43.4 %collective-permute-start.4 = (bf16[2048]{0:T(1024)(128)(2,1)S(1)}, bf16[2048]{0:T(1024)(128)(2,1)S(1)}, u32[]{:S(2)}, u32[]{:S(2)}) collective-permute-start(bf16[2048]{0:T(1024)(128)(2,1)S(1)} %reduce.1), channel_id=1, source_target_pairs={{0,16},{16,0},{1,17},{17,1},{2,18},{18,2},{3,19},{19,3},{4,20},{20... | collective-permute-start | bytes 12296 | tf_op jit(solution)/shard_map/ppermute | solution.py:31
  121.1 1183.7 %reduce-scatter.17.cloned.1.call-start = ((), (), s32[]{:S(2)}) async-start(), calls=%async_computation.17 | async-start | bytes 2621440 | tf_op jit(solution)/shard_map/reduce_scatter | solution.py:579
  130.5 193.7 %collective-permute-start.9 = (bf16[2048,512]{1,0:T(8,128)(2,1)}, bf16[2048,512]{1,0:T(8,128)(2,1)}, u32[]{:S(2)}, u32[]{:S(2)}) collective-permute-start(bf16[2048,512]{1,0:T(8,128)(2,1)} %all-gather.11.cloned.1.call-done), channel_id=1, source_target_pairs={{0,16},{16,0},{1,17},{17,1},{2,18},{18,2},{3,19},{19,3},{4,20},{20... | collective-permute-start | bytes 6291464 | tf_op jit(solution)/shard_map/ppermute | solution.py:31
  131.3 146.7 %collective-permute-start.7 = (bf16[128,2048]{1,0:T(8,128)(2,1)S(1)}, bf16[128,2048]{1,0:T(8,128)(2,1)S(1)}, u32[]{:S(2)}, u32[]{:S(2)}) collective-permute-start(bf16[128,2048]{1,0:T(8,128)(2,1)S(1)} %fusion.12), channel_id=1, source_target_pairs={{0,12},{4,8},{8,4},{12,0},{1,13},{5,9},{9,5},{13,1},{2,14},{6,10},... | collective-permute-start | bytes 1572872 | tf_op jit(solution)/shard_map/ppermute | solution.py:31
  133.8 193.5 %collective-permute-start.6 = (bf16[128,2048]{1,0:T(8,128)(2,1)S(1)}, bf16[128,2048]{1,0:T(8,128)(2,1)}, u32[]{:S(2)}, u32[]{:S(2)}) collective-permute-start(bf16[128,2048]{1,0:T(8,128)(2,1)S(1)} %fusion.12), channel_id=1, source_target_pairs={{0,8},{4,12},{8,0},{12,4},{1,9},{5,13},{9,1},{13,5},{2,10},{6,14},... | collective-permute-start | bytes 1572872 | tf_op jit(solution)/shard_map/ppermute | solution.py:31
  134.5 193.3 %collective-permute-start.5 = (bf16[128,2048]{1,0:T(8,128)(2,1)S(1)}, bf16[128,2048]{1,0:T(8,128)(2,1)}, u32[]{:S(2)}, u32[]{:S(2)}) collective-permute-start(bf16[128,2048]{1,0:T(8,128)(2,1)S(1)} %fusion.12), channel_id=1, source_target_pairs={{0,4},{4,0},{8,12},{12,8},{1,5},{5,1},{9,13},{13,9},{2,6},{6,2},{1... | collective-permute-start | bytes 1572872 | tf_op jit(solution)/shard_map/ppermute | solution.py:31
  135.6 200.6 %collective-permute-start.16 = (bf16[2048,512]{1,0:T(8,128)(2,1)}, bf16[2048,512]{1,0:T(8,128)(2,1)}, u32[]{:S(2)}, u32[]{:S(2)}) collective-permute-start(bf16[2048,512]{1,0:T(8,128)(2,1)} %all-gather.13.cloned.1.call-done), channel_id=1, source_target_pairs={{0,16},{16,0},{1,17},{17,1},{2,18},{18,2},{3,19},{19,3},{4,20},{20... | collective-permute-start | bytes 6291464 | tf_op jit(solution)/shard_map/ppermute | solution.py:31
  278.0 69.3 %collective-permute-start.25 = (bf16[2048,512]{1,0:T(8,128)(2,1)}, bf16[2048,512]{1,0:T(8,128)(2,1)}, u32[]{:S(2)}, u32[]{:S(2)}) collective-permute-start(bf16[2048,512]{1,0:T(8,128)(2,1)} %all-gather.17.cloned.1.call-done), channel_id=1, source_target_pairs={{0,16},{16,0},{1,17},{17,1},{2,18},{18,2},{3,19},{19,3},{4,20},{20... | collective-permute-start | bytes 6291464 | tf_op jit(solution)/shard_map/ppermute | solution.py:31
  327.3 88.3 %collective-permute-start.30 = (bf16[2048,512]{1,0:T(8,128)(2,1)S(1)}, bf16[2048,512]{1,0:T(8,128)(2,1)}, u32[]{:S(2)}, u32[]{:S(2)}) collective-permute-start(bf16[2048,512]{1,0:T(8,128)(2,1)S(1)} %copy-done.37), channel_id=1, source_target_pairs={{0,16},{16,0},{1,17},{17,1},{2,18},{18,2},{3,19},{19,3},{4,20},{20... | collective-permute-start | bytes 6291464 | tf_op jit(solution)/shard_map/ppermute | solution.py:31
  327.8 91.1 %collective-permute-start.34 = (bf16[512,2048]{1,0:T(8,128)(2,1)S(1)}, bf16[512,2048]{1,0:T(8,128)(2,1)S(1)}, u32[]{:S(2)}, u32[]{:S(2)}) collective-permute-start(bf16[512,2048]{1,0:T(8,128)(2,1)S(1)} %copy-done.40), channel_id=1, source_target_pairs={{0,16},{16,0},{1,17},{17,1},{2,18},{18,2},{3,19},{19,3},{4,20},{20... | collective-permute-start | bytes 6291464 | tf_op jit(solution)/shard_map/ppermute | solution.py:31
  354.0 89.5 %collective-permute-start.33 = (bf16[128,2048]{1,0:T(8,128)(2,1)S(1)}, bf16[128,2048]{1,0:T(8,128)(2,1)S(1)}, u32[]{:S(2)}, u32[]{:S(2)}) collective-permute-start(bf16[128,2048]{1,0:T(8,128)(2,1)S(1)} %copy-done.44), channel_id=1, source_target_pairs={{0,12},{4,8},{8,4},{12,0},{1,13},{5,9},{9,5},{13,1},{2,14},{6,10},... | collective-permute-start | bytes 1572872 | tf_op jit(solution)/shard_map/ppermute | solution.py:31
  843.9 365.5 %collective-permute-start.54 = (bf16[512,2048]{1,0:T(8,128)(2,1)}, bf16[512,2048]{1,0:T(8,128)(2,1)}, u32[]{:S(2)}, u32[]{:S(2)}) collective-permute-start(bf16[512,2048]{1,0:T(8,128)(2,1)} %pad_maximum_fusion), channel_id=1, source_target_pairs={{0,16},{16,0},{1,17},{17,1},{2,18},{18,2},{3,19},{19,3},{4,20},{20... | collective-permute-start | bytes 6291464 | tf_op jit(solution)/shard_map/ppermute | solution.py:31
  1218.4 87.5 %reduce-scatter.19.cloned.1.call-start = ((), (), s32[]{:S(2)}) async-start(), calls=%async_computation.18 | async-start | bytes 2621440 | tf_op jit(solution)/shard_map/reduce_scatter | solution.py:579
  1230.4 121.0 %reduce-scatter.15.cloned.1.call-start = ((), (), s32[]{:S(2)}) async-start(), calls=%async_computation.15 | async-start | bytes 2621440 | tf_op jit(solution)/shard_map/reduce_scatter | solution.py:578
  1238.4 158.5 %reduce-scatter.13.cloned.1.call-start = ((), (), s32[]{:S(2)}) async-start(), calls=%async_computation.14 | async-start | bytes 2621440 | tf_op jit(solution)/shard_map/reduce_scatter | solution.py:578
  1269.6 172.7 %reduce-scatter.23.cloned.1.call-start = ((), (), s32[]{:S(2)}) async-start(), calls=%async_computation.21 | async-start | bytes 2621440 | tf_op jit(solution)/shard_map/reduce_scatter | solution.py:580
  1280.1 207.7 %reduce-scatter.21.cloned.1.call-start = ((), (), s32[]{:S(2)}) async-start(), calls=%async_computation.20 | async-start | bytes 2621440 | tf_op jit(solution)/shard_map/reduce_scatter | solution.py:580
  1289.3 225.3 %reduce-scatter.27.cloned.1.call-start = ((), (), s32[]{:S(2)}) async-start(), calls=%async_computation.24 | async-start | bytes 655360
  1299.5 268.4 %reduce-scatter.25.cloned.1.call-start = ((), (), s32[]{:S(2)}) async-start(), calls=%async_computation.23 | async-start | bytes 655360
  1304.7 330.6 %all-gather.25.cloned.1.call-start = ((), (), s32[]{:S(2)}) async-start(), calls=%async_computation.19 | async-start | bytes 5242880 | tf_op jit(solution)/shard_map/all_gather | solution.py:590
  1310.3 350.3 %all-gather.23.cloned.1.call-start = ((), (), s32[]{:S(2)}) async-start(), calls=%async_computation.16 | async-start | bytes 5242880 | tf_op jit(solution)/shard_map/all_gather | solution.py:590
  1401.3 307.2 %all-gather.27.cloned.1.call-start = ((), (), s32[]{:S(2)}) async-start(), calls=%async_computation.22 | async-start | bytes 5242880 | tf_op jit(solution)/shard_map/all_gather | solution.py:590
  1514.0 49.4 %collective-permute-start.51 = (bf16[128,2048]{1,0:T(8,128)(2,1)}, bf16[128,2048]{1,0:T(8,128)(2,1)}, u32[]{:S(2)}, u32[]{:S(2)}) collective-permute-start(bf16[128,2048]{1,0:T(8,128)(2,1)} %get-tuple-element.134), channel_id=1, source_target_pairs={{0,8},{4,12},{8,0},{12,4},{1,9},{5,13},{9,1},{13,5},{2,10},{6,14},... | collective-permute-start | bytes 1572872 | tf_op jit(solution)/shard_map/ppermute | solution.py:31
  1520.6 43.7 %collective-permute-start.50 = (bf16[128,2048]{1,0:T(8,128)(2,1)}, bf16[128,2048]{1,0:T(8,128)(2,1)S(1)}, u32[]{:S(2)}, u32[]{:S(2)}) collective-permute-start(bf16[128,2048]{1,0:T(8,128)(2,1)} %get-tuple-element.132), channel_id=1, source_target_pairs={{0,4},{4,0},{8,12},{12,8},{1,5},{5,1},{9,13},{13,9},{2,6},{6,2},{1... | collective-permute-start | bytes 1572872 | tf_op jit(solution)/shard_map/ppermute | solution.py:31
  1567.9 63.8 %collective-permute-start.53 = (f32[128,2048]{1,0:T(8,128)}, f32[128,2048]{1,0:T(8,128)}, u32[]{:S(2)}, u32[]{:S(2)}) collective-permute-start(f32[128,2048]{1,0:T(8,128)} %get-tuple-element.130), channel_id=1, source_target_pairs={{0,16},{16,0},{1,17},{17,1},{2,18},{18,2},{3,19},{19,3},{4,20},{20... | collective-permute-start | bytes 3145736 | tf_op jit(solution)/shard_map/ppermute | solution.py:31
  (169 other events, 4213.7 us)
Sparse Core Ops, SparseCore 0:
  32.8 48.6 all-gather.10
  83.5 51.9 all-gather.12
  137.7 44.8 all-gather.16
  184.0 44.6 all-gather.14
  230.1 44.6 all-gather.18
  276.3 44.6 all-gather.20
  1218.5 41.1 reduce-scatter.16
  1262.6 43.1 reduce-scatter.18
  1308.2 43.1 reduce-scatter.14
  1353.6 43.1 reduce-scatter.12
  1399.2 43.1 reduce-scatter.22
  1444.6 43.1 reduce-scatter.20
  1490.1 20.9 reduce-scatter.26
  1513.3 19.8 reduce-scatter.24
  1534.9 59.8 all-gather.24
  1596.5 57.5 all-gather.22
  1655.7 52.6 all-gather.26

commit v2 on v1

v2 whole, which is shorter than its diff:
```python
from functools import partial

import jax
import jax.numpy as jnp
from jax import lax
from jax.experimental import pallas as pl
from jax.experimental.pallas import tpu as pltpu
from jax.sharding import PartitionSpec as P

EPSILON = 1e-05
BF = jnp.bfloat16
F32 = jnp.float32
STATE = 16
RANK = 128
LANES = 128
ROWS = 8
MIB = 1024 * 1024


def dot(left, right, left_axis, right_axis, kind=F32):
    return lax.dot_general(
        left, right, (((left_axis,), (right_axis,)), ((), ())), preferred_element_type=kind
    )


def sig(value):
    return 1.0 / (1.0 + jnp.exp(-value))


def swap(value, axis, shift):
    return lax.ppermute(value, axis, [(i, i ^ shift) for i in range(lax.axis_size(axis))])


def directed(value, axis, pairs):
    return lax.ppermute(value, axis, pairs)


def peers(value):
    return [swap(value, "grp", d) for d in range(1, lax.axis_size("grp"))]


def call(body, out_shape, **kwargs):
    limit = kwargs.pop("vmem", 48)
    return pl.pallas_call(
        body,
        out_shape=out_shape,
        compiler_params=pltpu.CompilerParams(vmem_limit_bytes=limit * MIB),
        **kwargs,
    )


def cost(flops):
    return pl.CostEstimate(flops=int(flops), bytes_accessed=0, transcendentals=0)


def shape(dims, kind):
    return jax.ShapeDtypeStruct(dims, kind)


def proj_body(a_ref, near_ref, far_ref, out_ref, *, w_axis):
    @pl.when(pl.program_id(0) == 0)
    def _():
        out_ref[...] = dot(a_ref[...], near_ref[...], 1, w_axis)

    @pl.when(pl.program_id(0) == 1)
    def _():
        out_ref[...] = dot(a_ref[...], far_ref[...], 1, w_axis)


def proj(a, near, far, w_axis):
    rows = a.shape[0]
    half = near.shape[1 - w_axis]

    def whole(v):
        return pl.BlockSpec(v.shape, lambda i: (0,) * v.ndim)

    return call(
        partial(proj_body, w_axis=w_axis),
        shape((rows, 2 * half), F32),
        grid=(2,),
        in_specs=[whole(a), whole(near), whole(far)],
        out_specs=pl.BlockSpec((rows, half), lambda i: (0, i)),
        cost_estimate=cost(4 * rows * half * a.shape[1]),
    )(a, near, far)


def total_body(n, w_axis, *refs):
    lefts, rights, out_ref = refs[:n], refs[n : 2 * n], refs[2 * n]
    total = dot(lefts[0][...], rights[0][...], 1, w_axis)
    for left, right in zip(lefts[1:], rights[1:]):
        total = total + dot(left[...], right[...], 1, w_axis)
    out_ref[...] = total.astype(BF)


def total_of(lefts, rights, w_axis):
    rows = lefts[0].shape[0]
    width = rights[0].shape[1 - w_axis]
    step = 512

    def left_spec(v):
        return pl.BlockSpec(v.shape, lambda i: (0, 0))

    def right_spec(v):
        if w_axis == 0:
            return pl.BlockSpec((v.shape[0], step), lambda i: (0, i))
        return pl.BlockSpec((step, v.shape[1]), lambda i: (i, 0))

    return call(
        partial(total_body, len(lefts), w_axis),
        shape((rows, width), BF),
        grid=(width // step,),
        in_specs=[left_spec(v) for v in lefts] + [right_spec(v) for v in rights],
        out_specs=pl.BlockSpec((rows, step), lambda i: (0, i)),
        cost_estimate=cost(2 * rows * width * sum(v.shape[1] for v in lefts)),
    )(*lefts, *rights)


def conv_of(x_ref, rows, pad_ref, mask_ref, vec_ref, cols):
    length = pad_ref.shape[0] - ROWS
    x = x_ref[rows, cols]
    pad_ref[0:ROWS, :] = jnp.zeros((ROWS, LANES), F32)
    pad_ref[ROWS : ROWS + length, :] = x
    total = vec_ref[4:5, cols] + vec_ref[0:1, cols] * x
    shifted = []
    for j in (1, 2, 3):
        earlier = pad_ref[ROWS - j : ROWS - j + length, :] * mask_ref[rows, j * LANES : (j + 1) * LANES]
        shifted.append(earlier)
        total = total + vec_ref[j : j + 1, cols] * earlier
    return total, shifted


def proj_conv_body(n_slots, a_ref, near_ref, far_ref, mask_ref, vec_ref, cat_ref, x_ref, inner_ref, part_ref,
                   pad_ref, sum_ref):
    i = pl.program_id(0)
    rows_all, half = x_ref.shape
    length = rows_all // n_slots

    @pl.when(i == 0)
    def _():
        x_ref[...] = dot(a_ref[...], near_ref[...], 1, 0)

    @pl.when(i == 1)
    def _():
        x_ref[...] = dot(a_ref[...], far_ref[...], 1, 0)

    for j in range(n_slots):
        rows = slice(j * length, (j + 1) * length)
        for b in range(half // LANES):
            cols = slice(b * LANES, (b + 1) * LANES)
            c, _ = conv_of(x_ref, rows, pad_ref, mask_ref, vec_ref, cols)
            inner_ref[rows, cols] = (c * sig(c)).astype(BF)
    both = dot(inner_ref[...], cat_ref[...], 1, 1)

    @pl.when(i == 0)
    def _():
        sum_ref[...] = both

    @pl.when(i == 1)
    def _():
        total = sum_ref[...] + both
        part_ref[...] = pack(total[:, :RANK], total[:, RANK:])


def proj_conv(n_slots, a, near, far, masks, vec, cat):
    rows = a.shape[0]
    half = near.shape[1]

    def whole(v):
        return pl.BlockSpec(v.shape, lambda i: (0,) * v.ndim)

    def block(n):
        return pl.BlockSpec((n, half), lambda i: (0, i))

    part_like = shape((rows, 2 * LANES), BF)
    return call(
        partial(proj_conv_body, n_slots),
        (shape((rows, 2 * half), F32), shape((rows, 2 * half), BF), part_like),
        grid=(2,),
        in_specs=[whole(a), whole(near), whole(far), whole(masks), block(vec.shape[0]), block(cat.shape[0])],
        out_specs=(block(rows), block(rows), whole(part_like)),
        scratch_shapes=[pltpu.VMEM((ROWS + rows // n_slots, LANES), F32), pltpu.VMEM((rows, 2 * LANES), F32)],
        cost_estimate=cost(4 * rows * half * a.shape[1]),
    )(a, near, far, masks, vec, cat)


def pack(low_rank, kq):
    high = kq.astype(BF).astype(F32)
    rest = pltpu.roll(kq - high, 64, axis=1)
    return jnp.concatenate([low_rank, high + rest], axis=1).astype(BF)


def summed_parts(parts, j, length):
    low_rank = jnp.zeros((length, RANK), F32)
    kq = jnp.zeros((length, LANES), F32)
    for d, part in enumerate(parts):
        rows = slice((j ^ d) * length, ((j ^ d) + 1) * length)
        low_rank = low_rank + part[rows, :RANK].astype(F32)
        kq = kq + part[rows, RANK:].astype(F32)
    kq = kq + pltpu.roll(kq, 64, axis=1)
    lane = lax.broadcasted_iota(jnp.int32, (1, LANES), 1)
    return low_rank, jnp.where(lane < 2 * STATE, kq, 0.0)


def rec_body(backward, n_slots, length, width, *refs):
    n_parts = n_slots
    parts, refs = refs[:n_parts], refs[n_parts:]
    if backward:
        (inner, gate, dgated, wdt, vec, mask, gated_near, gated_far, lr_out, dgate_near, dgate_far,
         dstate_out, dpart_out, ddt_out, dvec_out,
         kq_n, kq_i, c_i, lr_n, step_i, p_i, y_i, kb, str_n, hist, dy_i, a_i, b_i, h_scr, dkq_i,
         dlr_n, corr_n, prod, gated_tmp, dgate_tmp, drate_out) = refs
    else:
        (inner, gate, wdt, vec, mask, gated_out,
         kq_n, kq_i, c_i, lr_n, step_i, p_i, y_i, kb, state) = refs
    nb = width // (2 * LANES)
    first = pl.program_id(0) == 0
    last = pl.program_id(0) == pl.num_programs(0) - 1
    lane = lax.broadcasted_iota(jnp.int32, (1, LANES), 1)
    pieces = [(hh, b, slice((hh * nb + b) * LANES, (hh * nb + b + 1) * LANES)) for hh in (0, 1) for b in range(nb)]

    def rows_of(j):
        return slice(j * length, (j + 1) * length)

    def spread(j, hh):
        return pl.ds(hh * n_slots + j, length, stride=ROWS)

    @pl.when(first)
    def _():
        for j in range(n_slots):
            low_rank, kq = summed_parts(parts, j, length)
            lr_n[rows_of(j), :] = low_rank.astype(BF)
            if backward:
                lr_out[rows_of(j), :] = low_rank.astype(BF)
            kq_n[rows_of(j), :] = kq
            for hh in (0, 1):
                kq_i[spread(j, hh), :] = kq
                c_i[spread(j, hh), :] = mask[rows_of(j), 0:LANES]
        kq = kq_i[...]
        high = kq.astype(BF).astype(F32)
        split = (high + pltpu.roll(kq - high, 64, axis=1)).astype(BF)
        source = lax.broadcasted_iota(jnp.int32, (LANES, 2 * LANES), 0) % 64
        column = lax.broadcasted_iota(jnp.int32, (LANES, 2 * LANES), 1) // LANES
        for n in range(0, 2 * STATE, 2):
            copied = dot(split, jnp.where(source == n + column, 1.0, 0.0).astype(BF), 1, 0)
            kb[n] = copied[:, :LANES]
            kb[n + 1] = copied[:, LANES:]
        if backward:
            dkq_i[...] = jnp.zeros(dkq_i.shape, F32)
            dlr_n[...] = jnp.zeros(dlr_n.shape, F32)
            corr_n[...] = jnp.zeros(corr_n.shape, F32)

    for j in range(n_slots):
        rows = rows_of(j)
        rate = dot(lr_n[rows, :], wdt[...], 1, 0)
        kq = kq_n[rows, :]
        ks = jnp.sum(jnp.where(lane < STATE, kq * kq, 0.0), axis=1, keepdims=True)
        for hh, b, cols in pieces:
            strength = sig(rate[:, cols] + vec[0:1, cols])
            step = strength / (1.0 + strength * ks)
            step_i[b, spread(j, hh), :] = step
            p_i[b, spread(j, hh), :] = step * inner[rows, cols].astype(F32)
            if backward:
                str_n[rows, cols] = strength
                g = gate[rows, cols]
                dy_i[b, spread(j, hh), :] = dgated[rows, cols] * (g * sig(g))

    if backward:
        hist[0] = jnp.zeros(hist.shape[1:], F32)
    else:
        state[...] = jnp.zeros(state.shape, F32)

    def forward_step(t, carry):
        now = pl.ds(pl.multiple_of(t * ROWS, ROWS), ROWS)
        c = c_i[now, :]
        steps = [step_i[b, now, :] for b in range(nb)]
        ps = [p_i[b, now, :] for b in range(nb)]
        ys = [jnp.zeros((ROWS, LANES), F32) for _ in range(nb)]
        for n in range(STATE):
            k, q = kb[n, now, :], kb[STATE + n, now, :]
            ck2 = c * k * k
            for b in range(nb):
                before = hist[t, n * nb + b] if backward else state[n * nb + b]
                after = (c - ck2 * steps[b]) * before + k * ps[b]
                if backward:
                    hist[t + 1, n * nb + b] = after
                else:
                    state[n * nb + b] = after
                ys[b] = ys[b] + q * after
        for b in range(nb):
            y_i[b, now, :] = ys[b]
        return carry

    lax.fori_loop(0, length, forward_step, 0)

    if not backward:
        for j in range(n_slots):
            rows = rows_of(j)
            for hh, b, cols in pieces:
                y = y_i[b, spread(j, hh), :] + vec[1:2, cols] * inner[rows, cols].astype(F32)
                g = gate[rows, cols]
                gated_out[rows, cols] = (y * (g * sig(g))).astype(BF)
        return

    h_scr[...] = jnp.zeros(h_scr.shape, F32)

    def backward_step(start, i, carry):
        t = length - 1 - i
        at = pl.ds(pl.multiple_of((piece - 1 - (i - start)) * 2 * ROWS, 2 * ROWS), 2 * ROWS)
        now = pl.ds(pl.multiple_of(t * ROWS, ROWS), ROWS)
        c = c_i[now, :]
        steps = [step_i[b, now, :] for b in range(nb)]
        ps = [p_i[b, now, :] for b in range(nb)]
        dys = [dy_i[b, now, :] for b in range(nb)]
        a_sum = [jnp.zeros((ROWS, LANES), F32) for _ in range(nb)]
        b_sum = [jnp.zeros((ROWS, LANES), F32) for _ in range(nb)]
        for n in range(STATE):
            k, q = kb[n, now, :], kb[STATE + n, now, :]
            ck = c * k
            ck2 = ck * k
            dk1 = dk2 = dq = None
            for b in range(nb):
                before, after = hist[t, n * nb + b], hist[t + 1, n * nb + b]
                grad = dys[b] * q + h_scr[n * nb + b]
                a_sum[b] = a_sum[b] + grad * k
                both = grad * before
                b_sum[b] = b_sum[b] + ck2 * both
                h_scr[n * nb + b] = (c - ck2 * steps[b]) * grad
                one, two, three = ps[b] * grad, steps[b] * both, dys[b] * after
                dk1 = one if dk1 is None else dk1 + one
                dk2 = two if dk2 is None else dk2 + two
                dq = three if dq is None else dq + three
            dk = dk1 - (2.0 * ck) * dk2
            prod[at, n * LANES : (n + 1) * LANES] = jnp.concatenate([dk, dq], axis=0).astype(BF)
        for b in range(nb):
            a_i[b, now, :] = a_sum[b]
            b_i[b, now, :] = b_sum[b]
        return carry

    piece = prod.shape[0] // (2 * ROWS)
    source = lax.broadcasted_iota(jnp.int32, (STATE * LANES, LANES), 0) // LANES
    sums = jnp.where(source == lax.broadcasted_iota(jnp.int32, (STATE * LANES, LANES), 1), 1.0, 0.0).astype(BF)
    for part in range(length // piece):
        lax.fori_loop(part * piece, (part + 1) * piece, partial(backward_step, part * piece), 0)
        at = pl.ds((length - (part + 1) * piece) * 2 * ROWS, prod.shape[0])
        dkq_i[at, :] = dkq_i[at, :] + dot(prod[...], sums, 1, 0)

    ddt = [jnp.zeros((1, LANES), F32) for _ in pieces]
    dskip = [jnp.zeros((1, LANES), F32) for _ in pieces]
    for j in range(n_slots):
        rows = rows_of(j)
        kq = kq_n[rows, :]
        ks = jnp.sum(jnp.where(lane < STATE, kq * kq, 0.0), axis=1, keepdims=True)
        corr = jnp.zeros((length, 1), F32)
        for i, (hh, b, cols) in enumerate(pieces):
            at = spread(j, hh)
            inn = inner[rows, cols].astype(F32)
            a, step, dy = a_i[b, at, :], step_i[b, at, :], dy_i[b, at, :]
            skip = vec[1:2, cols]
            dstep = inn * a - b_i[b, at, :]
            strength = str_n[rows, cols]
            inv = 1.0 / (1.0 + strength * ks)
            drate = (dstep * (inv * inv) * (strength * (1.0 - strength))).astype(BF)
            drate_out[rows, cols] = drate
            dstate_out[rows, cols] = step * a + skip * dy
            corr = corr + jnp.sum(dstep * (step * step), axis=1, keepdims=True)
            y = y_i[b, at, :] + skip * inn
            g = gate[rows, cols]
            s = sig(g)
            gated_tmp[rows, cols] = (y * (g * s)).astype(BF)
            dgate_tmp[rows, cols] = (dgated[rows, cols] * y * (s * (1.0 + g * (1.0 - s)))).astype(BF)
            ddt[i] = ddt[i] + jnp.sum(drate.astype(F32), axis=0, keepdims=True)
            dskip[i] = dskip[i] + jnp.sum(dy * inn, axis=0, keepdims=True)
        corr_n[rows, :] = corr_n[rows, :] + corr
        dlr_n[rows, :] = dlr_n[rows, :] + dot(drate_out[rows, :], wdt[...], 1, 1)
    ddt_out[...] = dot(lr_n[...], drate_out[...], 0, 0)
    dvec_out[...] = jnp.concatenate(
        [jnp.concatenate(ddt, axis=1), jnp.concatenate(dskip, axis=1), jnp.zeros((6, width), F32)], axis=0
    )

    @pl.when(first)
    def _():
        gated_near[...] = gated_tmp[...]
        dgate_near[...] = dgate_tmp[...]

    @pl.when(last)
    def _():
        gated_far[...] = gated_tmp[...]
        dgate_far[...] = dgate_tmp[...]
        for j in range(n_slots):
            rows = rows_of(j)
            dk, dq = [
                dkq_i[pl.ds(m * ROWS + j, length, stride=2 * ROWS), :]
                + dkq_i[pl.ds(m * ROWS + n_slots + j, length, stride=2 * ROWS), :]
                for m in (0, 1)
            ]
            dkq = dk + pltpu.roll(dq, STATE, axis=1)
            dkq = dkq - jnp.where(lane < STATE, 2.0 * kq_n[rows, :] * corr_n[rows, :], 0.0)
            dpart_out[rows, :] = pack(dlr_n[rows, :], dkq)


def rec(backward, parts, inner, gate, dgated, wdt, vec, masks):
    rows, channels = inner.shape
    n_slots = len(parts)
    length = rows // n_slots
    width = channels // 2
    nb = width // (2 * LANES)

    def whole(a):
        return pl.BlockSpec(a.shape, lambda i: (0,) * a.ndim)

    def block(n):
        return pl.BlockSpec((n, width), lambda i: (0, i))

    wide = pltpu.VMEM((nb, ROWS * length, LANES), F32)
    row = pltpu.VMEM((rows, LANES), F32)
    spread = pltpu.VMEM((ROWS * length, LANES), F32)
    scratch = [row, spread, spread, pltpu.VMEM((rows, RANK), BF), wide, wide, wide]
    scratch += [pltpu.VMEM((2 * STATE, ROWS * length, LANES), F32)]
    if not backward:
        scratch += [pltpu.VMEM((STATE * nb, ROWS, LANES), F32)]
        return call(
            partial(rec_body, False, n_slots, length, width),
            shape((rows, channels), BF),
            grid=(2,),
            in_specs=[whole(p) for p in parts] + [block(rows), block(rows), block(RANK), block(vec.shape[0]), whole(masks)],
            out_specs=block(rows),
            scratch_shapes=scratch,
            cost_estimate=cost(25e9),
        )(*parts, inner, gate, wdt, vec, masks)
    scratch += [
        pltpu.VMEM((rows, width), F32),
        pltpu.VMEM((length + 1, STATE * nb, ROWS, LANES), F32),
        wide,
        wide,
        wide,
        pltpu.VMEM((STATE * nb, ROWS, LANES), F32),
        pltpu.VMEM((2 * ROWS * length, LANES), F32),
        pltpu.VMEM((rows, RANK), F32),
        row,
        pltpu.VMEM((4 * ROWS * ROWS * 2, STATE * LANES), BF),
        pltpu.VMEM((rows, width), BF),
        pltpu.VMEM((rows, width), BF),
        pltpu.VMEM((rows, width), BF),
    ]
    side = shape((rows, width), BF)
    lr_like = shape((rows, RANK), BF)
    part_like = shape((rows, 2 * LANES), BF)
    return call(
        partial(rec_body, True, n_slots, length, width),
        (
            side,
            side,
            lr_like,
            side,
            side,
            shape((rows, channels), F32),
            part_like,
            shape((RANK, channels), F32),
            shape((ROWS, channels), F32),
        ),
        grid=(2,),
        in_specs=[whole(p) for p in parts]
        + [block(rows), block(rows), block(rows), block(RANK), block(vec.shape[0]), whole(masks)],
        out_specs=(whole(side), whole(side), whole(lr_like), whole(side), whole(side), block(rows), whole(part_like), block(RANK), block(ROWS)),
        scratch_shapes=scratch,
        cost_estimate=cost(50e9),
        vmem=62,
    )(*parts, inner, gate, dgated, wdt, vec, masks)


def conv_bwd_body(n_slots, p0, p1, p2, p3, x_ref, inner, dstate, mask_ref, vec_ref, wdk_ref,
                  dx_near, dx_far, dsmall_out, dvec_out, pad_ref, late_ref, dcat):
    j = pl.program_id(0)
    length, channels = x_ref.shape
    lane = lax.broadcasted_iota(jnp.int32, (1, LANES), 1)

    @pl.when(j == 0)
    def _():
        dsmall_out[...] = jnp.zeros(dsmall_out.shape, F32)
        dvec_out[...] = jnp.zeros(dvec_out.shape, F32)

    low_rank = jnp.zeros((length, RANK), F32)
    kq = jnp.zeros((length, LANES), F32)
    for d, part in enumerate((p0, p1, p2, p3)):
        rows = pl.ds(pl.multiple_of((j ^ d) * length, length), length)
        low_rank = low_rank + part[rows, :RANK].astype(F32)
        kq = kq + part[rows, RANK:].astype(F32)
    kq = kq + pltpu.roll(kq, 64, axis=1)
    dcat[:, :RANK] = low_rank.astype(BF)
    dcat[:, RANK:] = jnp.where(lane < 2 * STATE, kq, 0.0).astype(BF)
    dsmall_out[...] += dot(dcat[...], inner[...], 0, 0)
    late_ref[length : length + ROWS, :] = jnp.zeros((ROWS, LANES), F32)
    for b in range(channels // LANES):
        cols = slice(b * LANES, (b + 1) * LANES)
        c, earlier = conv_of(x_ref, slice(0, length), pad_ref, mask_ref, vec_ref, cols)
        dinner = dstate[:, cols] + dot(dcat[...], wdk_ref[:, cols], 1, 0)
        s = sig(c)
        dc = dinner * (s * (1.0 + c * (1.0 - s)))
        dx = vec_ref[0:1, cols] * dc
        sums = [jnp.sum(dc * x_ref[:, cols], axis=0, keepdims=True)]
        for lag in (1, 2, 3):
            sums.append(jnp.sum(dc * earlier[lag - 1], axis=0, keepdims=True))
            late_ref[0:length, :] = dc * mask_ref[:, lag * LANES : (lag + 1) * LANES]
            dx = dx + vec_ref[lag : lag + 1, cols] * late_ref[lag : lag + length, :]
        sums.append(jnp.sum(dc, axis=0, keepdims=True))
        half = channels // 2
        dx_out = dx_near if b * LANES < half else dx_far
        dx_out[:, (b * LANES) % half : (b * LANES) % half + LANES] = dx.astype(BF)
        for i, value in enumerate(sums):
            dvec_out[i : i + 1, cols] += value


def conv_bwd(parts, x, inner, dstate, masks, vec, wdk):
    rows, channels = x.shape
    n_slots = len(parts)
    length = rows // n_slots

    def whole(a):
        return pl.BlockSpec(a.shape, lambda i: (0,) * a.ndim)

    slot = pl.BlockSpec((length, channels), lambda j: (j, 0))
    slot_half = pl.BlockSpec((length, channels // 2), lambda j: (j, 0))
    side = shape((rows, channels // 2), BF)
    small = shape((2 * LANES, channels), F32)
    vecs = shape((ROWS, channels), F32)
    return call(
        partial(conv_bwd_body, n_slots),
        (side, side, small, vecs),
        grid=(n_slots,),
        in_specs=[whole(p) for p in parts]
        + [slot, slot, slot, pl.BlockSpec((length, 4 * LANES), lambda j: (j, 0)), whole(vec), whole(wdk)],
        out_specs=(slot_half, slot_half, whole(small), whole(vecs)),
        scratch_shapes=[
            pltpu.VMEM((ROWS + length, LANES), F32),
            pltpu.VMEM((ROWS + length, LANES), F32),
            pltpu.VMEM((length, 2 * LANES), BF),
        ],
    )(*parts, x, inner, dstate, masks, vec, wdk)


def cut_body(where_ref, w_ref, gain_ref, keep_ref, send_ref):
    half = w_ref.shape[1] // 2
    scaled = w_ref[...].astype(F32) * gain_ref[...]
    first, second = scaled[:, :half].astype(BF), scaled[:, half:].astype(BF)
    mine = where_ref[1] == 0
    keep_ref[...] = jnp.where(mine, first, second)
    send_ref[...] = jnp.where(mine, second, first)


def cut(where, weight, gain, side, n_dp, n_grp, sub):
    rows = weight.shape[0]
    out = shape((rows, n_dp * sub), BF)
    return call(
        cut_body,
        (out, out),
        grid_spec=pltpu.PrefetchScalarGridSpec(
            num_scalar_prefetch=1,
            grid=(n_dp,),
            in_specs=[
                pl.BlockSpec((rows, 2 * sub), lambda i, w: (0, (side * n_dp + i) * n_grp + w[0])),
                pl.BlockSpec((rows, 1), lambda i, w: (0, 0)),
            ],
            out_specs=[pl.BlockSpec((rows, sub), lambda i, w: (0, i))] * 2,
        ),
        cost_estimate=cost(2e9),
    )(where, weight, gain)


def join_body(where_ref, w_ref, gain_ref, *refs):
    parts, out_ref, sum_ref = refs[:-3], refs[-2], refs[-1]
    n = len(parts) // 2
    sub = parts[0].shape[2]
    mine = where_ref[1] == 0

    @pl.when(pl.program_id(0) == 0)
    def _():
        sum_ref[...] = jnp.zeros(sum_ref.shape, F32)

    for d in range(n):
        for h in (0, 1):
            value = jnp.where(mine, parts[d][h], parts[n + d][h]).astype(F32)
            at = pl.ds(pl.multiple_of(((where_ref[0] ^ d) * 2 + h) * sub, sub), sub)
            out_ref[:, at] = value * gain_ref[...]
            sum_ref[...] += value * w_ref[:, at].astype(F32)


def join(where, weight, gain, parts, before, side, n_dp):
    rows = weight.shape[0]
    sub = parts[0].shape[2] // n_dp
    wide = 2 * (len(parts) // 2) * sub
    part = pl.BlockSpec((2, rows, sub), lambda i, w: (0, 0, i))
    return call(
        join_body,
        (shape(weight.shape, F32), shape((rows, sub), F32)),
        grid_spec=pltpu.PrefetchScalarGridSpec(
            num_scalar_prefetch=1,
            grid=(n_dp,),
            in_specs=[
                pl.BlockSpec((rows, wide), lambda i, w: (0, side * n_dp + i)),
                pl.BlockSpec((rows, 1), lambda i, w: (0, 0)),
            ]
            + [part] * len(parts)
            + [pl.BlockSpec(memory_space=pl.ANY)],
            out_specs=[
                pl.BlockSpec((rows, wide), lambda i, w: (0, side * n_dp + i)),
                pl.BlockSpec((rows, sub), lambda i, w: (0, 0)),
            ],
        ),
        input_output_aliases={3 + len(parts): 0} if before.shape == weight.shape else {},
        cost_estimate=cost(5e9),
    )(where, weight, gain, *parts, before)


def join_rows_body(where_ref, *refs):
    parts, out_ref = refs[:-1], refs[-1]
    n = len(parts) // 2
    sub = parts[0].shape[1]
    mine = where_ref[1] == 0
    for d in range(n):
        for h in (0, 1):
            value = jnp.where(mine, parts[d][h], parts[n + d][h]).astype(F32)
            out_ref[pl.ds(pl.multiple_of(((where_ref[0] ^ d) * 2 + h) * sub, sub), sub), :] = value


def join_rows(where, parts, width):
    sub = parts[0].shape[1]
    rows = len(parts) * sub
    step = 512
    return call(
        join_rows_body,
        shape((rows, width), F32),
        grid_spec=pltpu.PrefetchScalarGridSpec(
            num_scalar_prefetch=1,
            grid=(width // step,),
            in_specs=[pl.BlockSpec((2, sub, step), lambda i, w: (0, 0, i))] * len(parts),
            out_specs=pl.BlockSpec((rows, step), lambda i, w: (0, i)),
        ),
        cost_estimate=cost(4e9),
    )(where, *parts)


def rms_of(hidden):
    return lax.rsqrt(jnp.mean(hidden * hidden, axis=1, keepdims=True) + EPSILON)


def slot_masks(lengths, length):
    ends = jnp.cumsum(lengths, axis=1)
    position = jnp.arange(length, dtype=jnp.int32)
    segment = jnp.sum((position[None, :, None] >= ends[:, None, :]).astype(jnp.int32), axis=2)
    valid = (position[None, :] < ends[:, -1:]).astype(F32)
    same = []
    for lag in (1, 2, 3):
        before = jnp.concatenate([jnp.full((segment.shape[0], lag), -1, jnp.int32), segment[:, :-lag]], axis=1)
        same.append((before == segment).astype(F32))
    stack = jnp.stack([same[0]] + same, axis=2).reshape(-1, 4, 1)
    spread = jnp.broadcast_to(stack, stack.shape[:2] + (LANES,)).reshape(-1, 4 * LANES)
    return spread, valid


def gathered(value, axis):
    n_dp = lax.axis_size("dp")
    if n_dp != 4:
        return lax.all_gather(value, "dp", axis=axis, tiled=True)
    z = lax.axis_index("dp")
    left = lax.ppermute(value, "dp", [(i, (i + 1) % 4) for i in range(4)])
    right = lax.ppermute(value, "dp", [(i, (i - 1) % 4) for i in range(4)])
    up = lax.ppermute(left, "dp", [(1, 2), (2, 3)])
    down = lax.ppermute(right, "dp", [(1, 0), (2, 1)])
    across = jnp.where(z < 2, down, up)
    size = value.shape[axis]
    dims = list(value.shape)
    dims[axis] = 4 * size
    out = jnp.zeros(dims, value.dtype)
    for shift, piece in ((0, value), (3, left), (1, right), (2, across)):
        out = lax.dynamic_update_slice_in_dim(out, piece, (z + shift) % 4 * size, axis)
    return out


def on_device(boundary, doc_lengths, norm_gain, in_weight, conv_weight, conv_bias, down_weight, kq_weight,
              dt_weight, dt_bias, skip_weight, out_weight):
    s = lax.axis_index("section")
    g = lax.axis_index("grp")
    n_grp = lax.axis_size("grp")
    n_dp = lax.axis_size("dp")
    length, width = boundary.shape[3], boundary.shape[4]
    inner = in_weight.shape[2] // 2
    block = inner // n_dp
    sub = block // (2 * n_grp)
    half = sub * n_dp
    aligned = sub % LANES == 0
    mine_first = s == 0
    where = jnp.stack([g, s]).astype(jnp.int32)
    gain = norm_gain[0].astype(F32)[:, None]

    def pick(first, second):
        return jnp.where(mine_first, first, second)

    rows = boundary[0, :, 0]
    traded = swap(pick(rows[1], rows[0]), "section", 1)
    hidden = pick(rows[0], traded)
    cotangent = pick(traded, rows[1])
    lengths = lax.dynamic_index_in_dim(doc_lengths[:, 0], s, 0, keepdims=True)
    all_lengths = jnp.concatenate([lengths] + peers(lengths), axis=0)
    masks, valid = slot_masks(all_lengths, length)
    valid = valid[0][:, None]

    def columns(array):
        blocks = array.shape[1] // block
        view = array.reshape(array.shape[0], blocks, n_grp, 2, sub)
        view = lax.dynamic_index_in_dim(view, g, 2, keepdims=False)
        halves = [view[:, :, h].reshape(array.shape[0], blocks * sub) for h in (0, 1)]
        return pick(*halves), pick(halves[1], halves[0])

    def side(which):
        if aligned:
            return cut(where, in_weight[0], gain, which, n_dp, n_grp, sub)
        part = in_weight[0, :, which * inner : (which + 1) * inner]
        return columns((part.astype(F32) * gain).astype(BF))

    def out_side():
        view = lax.dynamic_slice_in_dim(out_weight[0], g * 2 * sub, 2 * sub, 0)
        return pick(view[:sub], view[sub:]), pick(view[sub:], view[:sub])

    def small_side():
        def lanes(array):
            return lax.dynamic_slice_in_dim(array, g * 2 * sub, 2 * sub, 1)

        down = lax.dynamic_slice_in_dim(down_weight[0], g * 2 * sub, 2 * sub, 0).T
        view = jnp.concatenate(
            [down, lanes(kq_weight[0]), jnp.zeros((2 * LANES - RANK - 2 * STATE, 2 * sub), BF), lanes(dt_weight[0]),
             lanes(conv_weight[0]), lanes(conv_bias), lanes(dt_bias), lanes(skip_weight)], axis=0)
        return pick(view[:, :sub], view[:, sub:]), pick(view[:, sub:], view[:, :sub])

    def two_layers(keep, send):
        come = swap(send, "section", 1)
        return pick(keep, come), pick(come, keep)

    x_sides, s_sides = two_layers(*side(0)), two_layers(*small_side())
    g_sides, o_sides = two_layers(*side(1)), two_layers(*out_side())

    def with_far(near):
        return near, swap(near, "section", 1)

    layers = []
    for l in (0, 1):
        w_s = jnp.concatenate(with_far(gathered(s_sides[l], 1)), axis=1)
        w_x = with_far(gathered(x_sides[l], 0))
        w_g = with_far(gathered(g_sides[l], 0))
        w_o = with_far(gathered(o_sides[l], 0))
        cat = w_s[: 2 * LANES]
        wdt = w_s[2 * LANES : 2 * LANES + RANK]
        tail = w_s[2 * LANES + RANK :].astype(F32)
        conv_vec = jnp.concatenate([tail[:5], jnp.zeros((3, tail.shape[1]), F32)], axis=0)
        rate_vec = jnp.concatenate([tail[5:7], jnp.zeros((6, tail.shape[1]), F32)], axis=0)
        layers.append((w_x, w_g, w_o, cat, wdt, conv_vec, rate_vec))

    def group(value):
        return jnp.concatenate([value] + peers(value), axis=0)

    def scatter(value):
        total = value[:length].astype(F32)
        for d in range(1, n_grp):
            total = total + swap(value[d * length : (d + 1) * length], "grp", d).astype(F32)
        return total

    def forward(h, layer):
        w_x, w_g, w_o, cat, wdt, conv_vec, rate_vec = layer
        a = group((h * rms_of(h)).astype(BF))
        x, act, part = proj_conv(n_grp, a, *w_x, masks, conv_vec, cat)
        gate = proj(a, *w_g, 0)
        return a, x, gate, act, [part] + peers(part)

    def backward(h, dout, dbranch, layer, saved, rec_out):
        w_x, w_g, w_o, cat, wdt, conv_vec, rate_vec = layer
        a, x, gate, act, parts = saved
        gated_near, gated_far, lr, dgate_near, dgate_far, dstate, dpart, ddt, dvec = rec_out
        dx_near, dx_far, dsmall, dconv = conv_bwd([dpart] + peers(dpart), x, act, dstate, masks, conv_vec, cat)
        scaled = scatter(total_of([dx_near, dx_far, dgate_near, dgate_far], [*w_x, *w_g], 1))
        rms = rms_of(h)
        own = h * rms
        dh = dout + rms * (scaled - own * jnp.mean(scaled * own, axis=1, keepdims=True))

        a_far, dbranch_far = swap(a, "section", 1), swap(dbranch, "section", 1)
        dgate_come, gated_come = swap(dgate_far, "section", 1), swap(gated_far, "section", 1)
        dx_come = swap(dx_far, "section", 1)

        def both(left, right, left_come, right_come):
            return (dot(left, right, 0, 0) + dot(left_come, right_come, 0, 0)).astype(BF)

        grad_g = both(a, dgate_near, a_far, dgate_come)
        grad_o = both(gated_near, dbranch, gated_come, dbranch_far)
        grad_x = both(a, dx_near, a_far, dx_come)
        grad_s = jnp.concatenate([dsmall, ddt, dconv[:5], dvec[:2], jnp.zeros((1, ddt.shape[1]), F32)], axis=0)
        grad_s = grad_s[:, :half] + swap(grad_s[:, half:].astype(BF), "section", 1).astype(F32)
        grad_o = jnp.concatenate([grad_o, grad_s.T.astype(BF)], axis=1)
        return dh, (grad_g, grad_o, grad_x)

    h0 = hidden.astype(F32)
    saved0 = forward(h0, layers[0])
    gated0 = rec(False, saved0[4], saved0[3], saved0[2], None, layers[0][4], layers[0][6], masks)
    branch0 = scatter(total_of([gated0[:, :half], gated0[:, half:]], layers[0][2], 0))
    h1 = (h0 + valid * branch0).astype(BF).astype(F32)
    saved1 = forward(h1, layers[1])
    dout1 = cotangent.astype(F32)
    dbranch1 = group((valid * dout1).astype(BF))
    dgated1 = proj(dbranch1, *layers[1][2], 1)
    rec1 = rec(True, saved1[4], saved1[3], saved1[2], dgated1, layers[1][4], layers[1][6], masks)
    branch1 = scatter(total_of(rec1[:2], layers[1][2], 0))
    out1 = h1 + valid * branch1
    dh1, grads1 = backward(h1, dout1, dbranch1, layers[1], saved1, rec1)
    dout0 = dh1.astype(BF).astype(F32)
    dbranch0 = group((valid * dout0).astype(BF))
    dgated0 = proj(dbranch0, *layers[0][2], 1)
    rec0 = rec(True, saved0[4], saved0[3], saved0[2], dgated0, layers[0][4], layers[0][6], masks)
    dh0, grads0 = backward(h0, dout0, dbranch0, layers[0], saved0, rec0)

    far = swap(pick(out1, dh0), "section", 1)
    result = pick(jnp.stack([dh0, far]), jnp.stack([far, out1]))
    result = result.reshape(1, 2, 1, length, width)

    def collected(l, grad):
        near = lax.psum_scatter(grad, "dp", scatter_dimension=0, tiled=True)
        far = directed(near, "section", [(1 - l, l)])
        halves = jnp.stack([near, far] if l == 0 else [far, near])
        out = [halves]
        for d in range(1, n_grp):
            pairs = [(l * n_grp + i, l * n_grp + (i ^ d)) for i in range(n_grp)]
            out.append(directed(halves, ("section", "grp"), pairs))
        return out

    (g1, o1, x1), (g0, o0, x0) = [[collected(l, grad) for grad in grads] for l, grads in ((1, grads1), (0, grads0))]

    def in_order(firsts, seconds):
        return jnp.stack([pick(a, b) for a, b in zip(firsts, seconds)])[jnp.arange(n_grp) ^ g]

    smalls = in_order([v[:, :, width:] for v in o0], [v[:, :, width:] for v in o1]).astype(F32)
    grad_small = smalls.transpose(3, 0, 1, 2).reshape(smalls.shape[3], block)
    if aligned:
        grad_in, sum_g = join(where, in_weight[0], gain, g0 + g1, gain, 1, n_dp)
        grad_in, sum_x = join(where, in_weight[0], gain, x0 + x1, grad_in, 0, n_dp)
        grad_gain = jnp.sum(sum_g + sum_x, axis=1)
        grad_out = join_rows(where, o0 + o1, width)
    else:
        sides = []
        for first, second in ((x0, x1), (g0, g1)):
            value = in_order(first, second).reshape(n_grp, 2, -1, n_dp, sub)
            sides.append(value.transpose(2, 3, 0, 1, 4).reshape(value.shape[2], inner))
        product = jnp.concatenate(sides, axis=1).astype(F32)
        grad_in = product * gain
        grad_gain = jnp.sum(product * in_weight[0].astype(F32), axis=1)
        grad_out = in_order([v[:, :, :width] for v in o0], [v[:, :, :width] for v in o1]).astype(F32).reshape(block, width)
    base = 2 * LANES + RANK
    return (
        result,
        grad_gain[None],
        grad_in[None],
        grad_small[None, base : base + 4],
        grad_small[base + 4][None],
        grad_small[:RANK].T[None],
        grad_small[None, RANK : RANK + 2 * STATE],
        grad_small[None, 2 * LANES : base],
        grad_small[base + 5][None],
        grad_small[base + 6][None],
        grad_out[None],
    )


def solution(mesh):
    return jax.shard_map(
        on_device,
        mesh=mesh,
        in_specs=(
            P("section", None, ("grp", "dp"), None, None),
            P(None, ("grp", "dp"), None),
            P("section", "dp"),
            P("section", "dp", None),
            P("section", None, "dp"),
            P("section", "dp"),
            P("section", "dp", None),
            P("section", None, "dp"),
            P("section", None, "dp"),
            P("section", "dp"),
            P("section", "dp"),
            P("section", "dp", None),
        ),
        out_specs=(
            P("section", None, ("grp", "dp"), None, None),
            P("section", "dp"),
            P("section", "dp", None),
            P("section", None, "dp"),
            P("section", "dp"),
            P("section", "dp", None),
            P("section", None, "dp"),
            P("section", None, "dp"),
            P("section", "dp"),
            P("section", "dp"),
            P("section", "dp", None),
        ),
        check_vma=False,
    )
```

time: 1730 us -> 1010 us (0.58)
  the two profiles are of different devices: /device:TPU:0 before, /device:TPU:7 now
where the time goes in v2:
time: 1010 us; the launch traced here: 1000 us
  waiting for transfers between devices  365 us (36%)
  Pallas kernels  240 us (24%)
  starting transfers between devices  178 us (18%)
  local copies, waits for them, and re-layouts  114 us (11%)
  other arithmetic  57 us (6%)
  matrix products  30.2 us (3%)
  between operations  17.3 us (2%)
    ppermute x65, waiting for transfers between devices, swap(): lax.ppermute(value, axis, [(i, i ^ shift) for i in range(lax.axis_size(ax...  144 us
    pallas_call x2, Pallas kernels, rec(): call(partial(rec_body, True, n_slots, length, width), (side, side, lr_lik...  107 us
    reduce_scatter x6, waiting for transfers between devices, collected(): near = lax.psum_scatter(grad, 'dp', scatter_dimension=0, tiled=True)  64.6 us
    ppermute x65, starting transfers between devices, swap(): lax.ppermute(value, axis, [(i, i ^ shift) for i in range(lax.axis_size(ax...  60.1 us
    ppermute x24, starting transfers between devices, directed(): return lax.ppermute(value, axis, pairs)  50.1 us
    ppermute x8, waiting for transfers between devices, gathered(): down = lax.ppermute(right, 'dp', [(1, 0), (2, 1)])  42.6 us
    ppermute x24, waiting for transfers between devices, directed(): return lax.ppermute(value, axis, pairs)  41.8 us
    ppermute x8, waiting for transfers between devices, gathered(): right = lax.ppermute(value, 'dp', [(i, (i - 1) % 4) for i in range(4)])  40.6 us
  transfers between devices with their start and end apart: 127, of which 37 were waited for; matrix products, arithmetic and copies ran while one was open for 15% of the time, Pallas kernels for 23%

profile of v2, /device:TPU:7, one launch (start us, length us, event | category | flops | bytes accessed | tf_op | source)
XLA Modules:
  0.0 1001.9 jit_solution(14305918403819820753)
XLA Ops:
  80.0 17.0 %collective-permute-done.29 = bf16[128,2048]{1,0:T(8,128)(2,1)S(1)} collective-permute-done((bf16[128,2048]{1,0:T(8,128)(2,1)S(1)}, bf16[128,2048]{1,0:T(8,128)(2,1)S(1)}, u32[]{:S(2)}, u32[]{:S(2)}) %collective-permute-start.29) | collective-permute-done | bytes 524320 | tf_op jit(solution)/shard_map/ppermute | solution.py:665
  97.0 20.9 %collective-permute-start.23 = (bf16[512,512]{1,0:T(8,128)(2,1)S(1)}, bf16[512,512]{1,0:T(8,128)(2,1)S(1)}, u32[]{:S(2)}, u32[]{:S(2)}) collective-permute-start(bf16[512,512]{1,0:T(8,128)(2,1)S(1)} %get-tuple-element.151), channel_id=1, source_target_pairs={{0,1},{1,2},{2,3},{3,0},{4,5},{5,6},{6,7},{7,4},{8,9},{9,10},{10,1... | collective-permute-start | bytes 1572872 | tf_op jit(solution)/shard_map/ppermute | solution.py:665
  121.6 10.7 %collective-permute-done.23 = bf16[512,512]{1,0:T(8,128)(2,1)S(1)} collective-permute-done((bf16[512,512]{1,0:T(8,128)(2,1)S(1)}, bf16[512,512]{1,0:T(8,128)(2,1)S(1)}, u32[]{:S(2)}, u32[]{:S(2)}) %collective-permute-start.23) | collective-permute-done | bytes 524320 | tf_op jit(solution)/shard_map/ppermute | solution.py:665
  136.4 18.5 %collective-permute-done.10 = bf16[512,512]{1,0:T(8,128)(2,1)S(1)} collective-permute-done((bf16[512,512]{1,0:T(8,128)(2,1)S(1)}, bf16[512,512]{1,0:T(8,128)(2,1)S(1)}, u32[]{:S(2)}, u32[]{:S(2)}) %collective-permute-start.10) | collective-permute-done | bytes 524320 | tf_op jit(solution)/shard_map/ppermute | solution.py:668
  156.5 9.6 collective-permute-done.25
  168.7 10.4 %collective-permute-start.54 = (bf16[512,512]{1,0:T(8,128)(2,1)S(1)}, bf16[512,512]{1,0:T(8,128)(2,1)}, u32[]{:S(2)}, u32[]{:S(2)}) collective-permute-start(bf16[512,512]{1,0:T(8,128)(2,1)S(1)} %get-tuple-element.141), channel_id=1, source_target_pairs={{0,3},{1,0},{2,1},{3,2},{4,7},{5,4},{6,5},{7,6},{8,11},{9,8},{10,9... | collective-permute-start | bytes 1572872 | tf_op jit(solution)/shard_map/ppermute | solution.py:666
  179.1 20.8 %collective-permute-done.41 = bf16[512,512]{1,0:T(8,128)(2,1)} collective-permute-done((bf16[512,512]{1,0:T(8,128)(2,1)S(1)}, bf16[512,512]{1,0:T(8,128)(2,1)}, u32[]{:S(2)}, u32[]{:S(2)}) %collective-permute-start.41) | collective-permute-done | bytes 524320 | tf_op jit(solution)/shard_map/ppermute | solution.py:666
  212.4 9.9 collective-permute-done.62
  228.2 9.2 collective-permute-done.31
  242.6 8.3 shard_map.204
  270.4 17.6 %shard_map.207 = bf16[512,1024]{1,0:T(8,128)(2,1)S(1)} custom-call(bf16[512,256]{1,0:T(8,128)(2,1)S(1)} %get-tuple-element.51.refs_0_, bf16[512,256]{1,0:T(8,128)(2,1)S(1)} %collective-permute-done.19.refs_1_, bf16[512,256]{1,0:T(8,128)(2,1)S(1)} %collective-permute-done.20.refs_2_, bf16[512,256]{1,0:T(8,128)(2,1)S(1)} %collective-permute-done.21.refs_3_, ...), custom_call_target="tpu_custom_call" | custom-call | flops 24999999488 | tf_op jit(solution)/shard_map/pallas_call | solution.py:421
  307.8 11.5 %collective-permute-done.35 = bf16[128,2048]{1,0:T(8,128)(2,1)S(1)} collective-permute-done((bf16[128,2048]{1,0:T(8,128)(2,1)S(1)}, bf16[128,2048]{1,0:T(8,128)(2,1)S(1)}, u32[]{:S(2)}, u32[]{:S(2)}) %collective-permute-start.35) | collective-permute-done | bytes 524320 | tf_op jit(solution)/shard_map/ppermute | solution.py:31
  321.3 8.7 collective-permute-done.60
  331.3 10.2 %collective-permute-done.59 = bf16[128,2048]{1,0:T(8,128)(2,1)S(1)} collective-permute-done((bf16[128,2048]{1,0:T(8,128)(2,1)S(1)}, bf16[128,2048]{1,0:T(8,128)(2,1)S(1)}, u32[]{:S(2)}, u32[]{:S(2)}) %collective-permute-start.59) | collective-permute-done | bytes 524320 | tf_op jit(solution)/shard_map/ppermute | solution.py:31
  342.9 12.5 %collective-permute-done.39 = bf16[128,2048]{1,0:T(8,128)(2,1)S(1)} collective-permute-done((bf16[128,2048]{1,0:T(8,128)(2,1)S(1)}, bf16[128,2048]{1,0:T(8,128)(2,1)S(1)}, u32[]{:S(2)}, u32[]{:S(2)}) %collective-permute-start.39) | collective-permute-done | bytes 524320 | tf_op jit(solution)/shard_map/ppermute | solution.py:31
  358.5 8.9 collective-permute-done.38
  369.6 8.1 shard_map.209
  389.7 12.7 %shard_map.210.refs_5_ = f32[512,1024]{1,0:T(8,128)S(1)} custom-call(bf16[512,2048]{1,0:T(8,128)(2,1)S(1)} %copy-done.6, bf16[2048,512]{1,0:T(8,128)(2,1)} %copy-done.82, bf16[2048,512]{1,0:T(8,128)(2,1)} %collective-permute-done.57.far_ref.refs_7_), custom_call_target="tpu_custom_call" | custom-call | flops 2147483648 | tf_op jit(solution)/shard_map/pallas_call | solution.py:77
  405.2 53.6 %shard_map.212 = (bf16[512,512]{1,0:T(8,128)(2,1)}, bf16[512,512]{1,0:T(8,128)(2,1)}, bf16[512,128]{1,0:T(8,128)(2,1)}, bf16[512,512]{1,0:T(8,128)(2,1)}, bf16[5...) custom-call(bf16[512,256]{1,0:T(8,128)(2,1)} %copy-done.67, ...), custom_call_target="tpu_custom_call" | custom-call | flops 49999998976 | tf_op jit(solution)/shard_map/pallas_call | solution.py:448
  473.3 7.7 shard_map.213
  481.0 7.8 shard_map.214
  525.5 9.3 collective-permute-done.74
  534.9 12.1 %collective-permute-done.73 = bf16[128,2048]{1,0:T(8,128)(2,1)S(1)} collective-permute-done((bf16[128,2048]{1,0:T(8,128)(2,1)S(1)}, bf16[128,2048]{1,0:T(8,128)(2,1)S(1)}, u32[]{:S(2)}, u32[]{:S(2)}) %collective-permute-start.73) | collective-permute-done | bytes 524320 | tf_op jit(solution)/shard_map/ppermute | solution.py:31
  556.2 53.7 %shard_map.216 = (bf16[512,512]{1,0:T(8,128)(2,1)}, bf16[512,512]{1,0:T(8,128)(2,1)}, bf16[512,128]{1,0:T(8,128)(2,1)}, bf16[512,512]{1,0:T(8,128)(2,1)}, bf16[5...) custom-call(bf16[512,256]{1,0:T(8,128)(2,1)} %copy-done.63, ...), custom_call_target="tpu_custom_call" | custom-call | flops 49999998976 | tf_op jit(solution)/shard_map/pallas_call | solution.py:448
  652.5 7.3 shard_map.217
  716.5 10.9 %collective-permute-done.79 = bf16[128,2048]{1,0:T(8,128)(2,1)S(1)} collective-permute-done((bf16[128,2048]{1,0:T(8,128)(2,1)S(1)}, bf16[128,2048]{1,0:T(8,128)(2,1)S(1)}, u32[]{:S(2)}, u32[]{:S(2)}) %collective-permute-start.79) | collective-permute-done | bytes 524320 | tf_op jit(solution)/shard_map/ppermute | solution.py:31
  738.3 11.4 %collective-permute-done.82 = bf16[128,2048]{1,0:T(8,128)(2,1)} collective-permute-done((bf16[128,2048]{1,0:T(8,128)(2,1)}, bf16[128,2048]{1,0:T(8,128)(2,1)}, u32[]{:S(2)}, u32[]{:S(2)}) %collective-permute-start.82) | collective-permute-done | bytes 524320 | tf_op jit(solution)/shard_map/ppermute | solution.py:31
  773.0 34.6 %reduce-scatter.11.cloned.1.call-done = bf16[512,512]{1,0:T(8,128)(2,1)} async-done(((bf16[2048,512]{1,0:T(8,128)(2,1)}), bf16[512,512]{1,0:T(8,128)(2,1)}) %reduce-scatter.11.cloned.1.call-update) | async-done | bytes 524304 | tf_op jit(solution)/shard_map/reduce_scatter | solution.py:822
  831.8 30.0 %reduce-scatter.15.cloned.1.call-done = bf16[128,2440]{1,0:T(8,128)(2,1)} async-done(((bf16[512,2440]{1,0:T(8,128)(2,1)}), bf16[128,2440]{1,0:T(8,128)(2,1)}) %reduce-scatter.15.cloned.1.call-update) | async-done | bytes 624656 | tf_op jit(solution)/shard_map/reduce_scatter | solution.py:822
  883.1 41.7 %collective-permute-done.105.refs_6_ = bf16[2,512,512]{2,1,0:T(8,128)(2,1)} collective-permute-done((bf16[2,512,512]{2,1,0:T(8,128)(2,1)S(1)}, bf16[2,512,512]{2,1,0:T(8,128)(2,1)}, u32[]{:S(2)}, u32[]{:S(2)}) %collective-permute-start.105) | collective-permute-done | bytes 1048608 | tf_op jit(solution)/shard_map/ppermute | solution.py:35
  945.3 9.0 shard_map.220
  954.4 9.5 shard_map.221
  (730 shorter events, 460.5 us)
Async XLA Ops:
  7.2 721.3 %reduce-scatter.17.cloned.1.call-start = ((), (), s32[]{:S(2)}) async-start(), calls=%async_computation.11 | async-start | bytes 3276800 | tf_op jit(solution)/shard_map/reduce_scatter | solution.py:822
  12.6 47.0 %collective-permute-start = (bf16[128,2048]{1,0:T(8,128)(2,1)}, bf16[128,2048]{1,0:T(8,128)(2,1)S(1)}, u32[]{:S(2)}, u32[]{:S(2)}) collective-permute-start(bf16[128,2048]{1,0:T(8,128)(2,1)} %bitcast_select_fusion.3), channel_id=1, source_target_pairs={{0,16},{16,0},{1,17},{17,1},{2,18},{18,2},{3,19},{19,3},{4,20},{20... | collective-permute-start | bytes 1572872 | tf_op jit(solution)/shard_map/ppermute | solution.py:31
  58.8 59.1 %collective-permute-start.8 = (bf16[512,512]{1,0:T(8,128)(2,1)S(1)}, bf16[512,512]{1,0:T(8,128)(2,1)S(1)}, u32[]{:S(2)}, u32[]{:S(2)}) collective-permute-start(bf16[512,512]{1,0:T(8,128)(2,1)S(1)} %get-tuple-element.155), channel_id=1, source_target_pairs={{0,1},{1,2},{2,3},{3,0},{4,5},{5,6},{6,7},{7,4},{8,9},{9,10},{10,1... | collective-permute-start | bytes 1572872 | tf_op jit(solution)/shard_map/ppermute | solution.py:665
  59.7 58.5 %collective-permute-start.9 = (bf16[512,512]{1,0:T(8,128)(2,1)S(1)}, bf16[512,512]{1,0:T(8,128)(2,1)S(1)}, u32[]{:S(2)}, u32[]{:S(2)}) collective-permute-start(bf16[512,512]{1,0:T(8,128)(2,1)S(1)} %get-tuple-element.155), channel_id=1, source_target_pairs={{0,3},{1,0},{2,1},{3,2},{4,7},{5,4},{6,5},{7,6},{8,11},{9,8},{10,9... | collective-permute-start | bytes 1572872 | tf_op jit(solution)/shard_map/ppermute | solution.py:666
  70.1 49.3 %collective-permute-start.30 = (bf16[128,2048]{1,0:T(8,128)(2,1)S(1)}, bf16[128,2048]{1,0:T(8,128)(2,1)S(1)}, u32[]{:S(2)}, u32[]{:S(2)}) collective-permute-start(bf16[128,2048]{1,0:T(8,128)(2,1)S(1)} %get-tuple-element.149), channel_id=1, source_target_pairs={{0,3},{1,0},{2,1},{3,2},{4,7},{5,4},{6,5},{7,6},{8,11},{9,8},{10,9... | collective-permute-start | bytes 1572872 | tf_op jit(solution)/shard_map/ppermute | solution.py:666
  120.2 45.9 %collective-permute-start.25 = (bf16[512,512]{1,0:T(8,128)(2,1)S(1)}, bf16[512,512]{1,0:T(8,128)(2,1)S(1)}, u32[]{:S(2)}, u32[]{:S(2)}) collective-permute-start(bf16[512,512]{1,0:T(8,128)(2,1)S(1)} %collective-permute-done.24), channel_id=1, source_target_pairs={{1,0},{2,1},{5,4},{6,5},{9,8},{10,9},{13,12},{14,13},{17,16},{18,1... | collective-permute-start | bytes 1572872 | tf_op jit(solution)/shard_map/ppermute | solution.py:668
  166.1 74.5 %collective-permute-start.12 = (bf16[2048,512]{1,0:T(8,128)(2,1)S(1)}, bf16[2048,512]{1,0:T(8,128)(2,1)S(1)}, u32[]{:S(2)}, u32[]{:S(2)}) collective-permute-start(bf16[2048,512]{1,0:T(8,128)(2,1)S(1)} %select_dynamic-update-slice_fusion.5.near_ref.refs_4_), channel_id=1, source_target_pairs={{0,16},{16,0},{1,17},{17,1},{2,18},{18,2},{3,19},{19,3},{4,20},{20... | collective-permute-start | bytes 6291464 | tf_op jit(solution)/shard_map/ppermute | solution.py:31
  199.9 56.9 %collective-permute-start.27 = (bf16[2048,512]{1,0:T(8,128)(2,1)}, bf16[2048,512]{1,0:T(8,128)(2,1)}, u32[]{:S(2)}, u32[]{:S(2)}) collective-permute-start(bf16[2048,512]{1,0:T(8,128)(2,1)} %select_dynamic-update-slice_fusion.4.near_ref.refs_6_), channel_id=1, source_target_pairs={{0,16},{16,0},{1,17},{17,1},{2,18},{18,2},{3,19},{19,3},{4,20},{20... | collective-permute-start | bytes 6291464 | tf_op jit(solution)/shard_map/ppermute | solution.py:31
  238.9 55.4 %collective-permute-start.55 = (bf16[512,512]{1,0:T(8,128)(2,1)}, bf16[512,512]{1,0:T(8,128)(2,1)}, u32[]{:S(2)}, u32[]{:S(2)}) collective-permute-start(bf16[512,512]{1,0:T(8,128)(2,1)} %collective-permute-done.54), channel_id=1, source_target_pairs={{1,0},{2,1},{5,4},{6,5},{9,8},{10,9},{13,12},{14,13},{17,16},{18,1... | collective-permute-start | bytes 1572872 | tf_op jit(solution)/shard_map/ppermute | solution.py:668
  319.3 50.3 %collective-permute-start.44 = (bf16[2048,512]{1,0:T(8,128)(2,1)S(1)}, bf16[2048,512]{1,0:T(8,128)(2,1)}, u32[]{:S(2)}, u32[]{:S(2)}) collective-permute-start(bf16[2048,512]{1,0:T(8,128)(2,1)S(1)} %copy-done.98), channel_id=1, source_target_pairs={{0,16},{16,0},{1,17},{17,1},{2,18},{18,2},{3,19},{19,3},{4,20},{20... | collective-permute-start | bytes 6291464 | tf_op jit(solution)/shard_map/ppermute | solution.py:31
  320.0 69.8 %collective-permute-start.57 = (bf16[2048,512]{1,0:T(8,128)(2,1)S(1)}, bf16[2048,512]{1,0:T(8,128)(2,1)}, u32[]{:S(2)}, u32[]{:S(2)}) collective-permute-start(bf16[2048,512]{1,0:T(8,128)(2,1)S(1)} %select_dynamic-update-slice_fusion.1.near_ref.refs_6_), channel_id=1, source_target_pairs={{0,16},{16,0},{1,17},{17,1},{2,18},{18,2},{3,19},{19,3},{4,20},{20... | collective-permute-start | bytes 6291464 | tf_op jit(solution)/shard_map/ppermute | solution.py:31
  320.6 61.1 %collective-permute-start.65 = (bf16[512,2048]{1,0:T(8,128)(2,1)S(1)}, bf16[512,2048]{1,0:T(8,128)(2,1)}, u32[]{:S(2)}, u32[]{:S(2)}) collective-permute-start(bf16[512,2048]{1,0:T(8,128)(2,1)S(1)} %select_dynamic-update-slice_fusion.near_ref.refs_2_), channel_id=1, source_target_pairs={{0,16},{16,0},{1,17},{17,1},{2,18},{18,2},{3,19},{19,3},{4,20},{20... | collective-permute-start | bytes 6291464 | tf_op jit(solution)/shard_map/ppermute | solution.py:31
  367.4 133.0 %collective-permute-start.112 = (bf16[512,2048]{1,0:T(8,128)(2,1)}, bf16[512,2048]{1,0:T(8,128)(2,1)}, u32[]{:S(2)}, u32[]{:S(2)}) collective-permute-start(bf16[512,2048]{1,0:T(8,128)(2,1)} %pad_maximum_fusion.4.a_ref), channel_id=1, source_target_pairs={{0,16},{16,0},{1,17},{17,1},{2,18},{18,2},{3,19},{19,3},{4,20},{20... | collective-permute-start | bytes 6291464 | tf_op jit(solution)/shard_map/ppermute | solution.py:31
  461.5 148.9 %collective-permute-start.85 = (bf16[512,2048]{1,0:T(8,128)(2,1)}, bf16[512,2048]{1,0:T(8,128)(2,1)}, u32[]{:S(2)}, u32[]{:S(2)}) collective-permute-start(bf16[512,2048]{1,0:T(8,128)(2,1)} %pad_maximum_fusion.2.a_ref), channel_id=1, source_target_pairs={{0,16},{16,0},{1,17},{17,1},{2,18},{18,2},{3,19},{19,3},{4,20},{20... | collective-permute-start | bytes 6291464 | tf_op jit(solution)/shard_map/ppermute | solution.py:31
  525.5 237.3 %reduce-scatter.7.cloned.1.call-start = ((), (), s32[]{:S(2)}) async-start(), calls=%async_computation.6 | async-start | bytes 2621440 | tf_op jit(solution)/shard_map/reduce_scatter | solution.py:822
  617.7 147.1 %reduce-scatter.9.cloned.1.call-start = ((), (), s32[]{:S(2)}) async-start(), calls=%async_computation.7 | async-start | bytes 2621440 | tf_op jit(solution)/shard_map/reduce_scatter | solution.py:822
  629.7 142.0 %reduce-scatter.13.cloned.1.call-start = ((), (), s32[]{:S(2)}) async-start(), calls=%async_computation.9 | async-start | bytes 2621440 | tf_op jit(solution)/shard_map/reduce_scatter | solution.py:822
  638.2 169.4 %reduce-scatter.11.cloned.1.call-start = ((), (), s32[]{:S(2)}) async-start(), calls=%async_computation.8 | async-start | bytes 2621440 | tf_op jit(solution)/shard_map/reduce_scatter | solution.py:822
  668.3 193.5 %reduce-scatter.15.cloned.1.call-start = ((), (), s32[]{:S(2)}) async-start(), calls=%async_computation.10 | async-start | bytes 3276800 | tf_op jit(solution)/shard_map/reduce_scatter | solution.py:822
  759.7 54.3 %collective-permute-start.120 = (bf16[2,128,2440]{1,2,0:T(8,128)(2,1)}, bf16[2,128,2440]{1,2,0:T(8,128)(2,1)S(1)}, u32[]{:S(2)}, u32[]{:S(2)}) collective-permute-start(bf16[2,128,2440]{1,2,0:T(8,128)(2,1)} %copy.124), channel_id=1, source_target_pairs={{16,28},{20,24},{24,20},{28,16},{17,29},{21,25},{25,21},{29,17},{1... | collective-permute-start | bytes 3747848 | tf_op jit(solution)/shard_map/ppermute | solution.py:35
  766.3 51.7 %collective-permute-start.118 = (bf16[2,128,2440]{1,2,0:T(8,128)(2,1)}, bf16[2,128,2440]{1,2,0:T(8,128)(2,1)}, u32[]{:S(2)}, u32[]{:S(2)}) collective-permute-start(bf16[2,128,2440]{1,2,0:T(8,128)(2,1)} %copy.124), channel_id=1, source_target_pairs={{16,24},{20,28},{24,16},{28,20},{17,25},{21,29},{25,17},{29,21},{1... | collective-permute-start | bytes 3747848 | tf_op jit(solution)/shard_map/ppermute | solution.py:35
  769.2 51.0 %collective-permute-start.116 = (bf16[2,128,2440]{1,2,0:T(8,128)(2,1)}, bf16[2,128,2440]{1,2,0:T(8,128)(2,1)}, u32[]{:S(2)}, u32[]{:S(2)}) collective-permute-start(bf16[2,128,2440]{1,2,0:T(8,128)(2,1)} %copy.124), channel_id=1, source_target_pairs={{16,20},{20,16},{24,28},{28,24},{17,21},{21,17},{25,29},{29,25},{1... | collective-permute-start | bytes 3747848 | tf_op jit(solution)/shard_map/ppermute | solution.py:35
  814.0 50.0 %collective-permute-start.90 = (bf16[2,512,512]{2,1,0:T(8,128)(2,1)S(1)}, bf16[2,512,512]{2,1,0:T(8,128)(2,1)}, u32[]{:S(2)}, u32[]{:S(2)}) collective-permute-start(bf16[2,512,512]{2,1,0:T(8,128)(2,1)S(1)} %pad_maximum_fusion.8.refs_0_), channel_id=1, source_target_pairs={{0,12},{4,8},{8,4},{12,0},{1,13},{5,9},{9,5},{13,1},{2,14},{6,10},... | collective-permute-start | bytes 3145736 | tf_op jit(solution)/shard_map/ppermute | solution.py:35
  817.9 48.9 %collective-permute-start.94 = (bf16[2,512,512]{2,1,0:T(8,128)(2,1)}, bf16[2,512,512]{2,1,0:T(8,128)(2,1)}, u32[]{:S(2)}, u32[]{:S(2)}) collective-permute-start(bf16[2,512,512]{2,1,0:T(8,128)(2,1)} %pad_maximum_fusion.9.refs_4_), channel_id=1, source_target_pairs={{16,20},{20,16},{24,28},{28,24},{17,21},{21,17},{25,29},{29,25},{1... | collective-permute-start | bytes 3145736 | tf_op jit(solution)/shard_map/ppermute | solution.py:35
  820.3 48.7 %collective-permute-start.95 = (bf16[2,512,512]{2,1,0:T(8,128)(2,1)}, bf16[2,512,512]{2,1,0:T(8,128)(2,1)}, u32[]{:S(2)}, u32[]{:S(2)}) collective-permute-start(bf16[2,512,512]{2,1,0:T(8,128)(2,1)} %pad_maximum_fusion.9.refs_4_), channel_id=1, source_target_pairs={{16,24},{20,28},{24,16},{28,20},{17,25},{21,29},{25,17},{29,21},{1... | collective-permute-start | bytes 3145736 | tf_op jit(solution)/shard_map/ppermute | solution.py:35
  824.6 52.4 %collective-permute-start.96 = (bf16[2,512,512]{2,1,0:T(8,128)(2,1)}, bf16[2,512,512]{2,1,0:T(8,128)(2,1)}, u32[]{:S(2)}, u32[]{:S(2)}) collective-permute-start(bf16[2,512,512]{2,1,0:T(8,128)(2,1)} %pad_maximum_fusion.9.refs_4_), channel_id=1, source_target_pairs={{16,28},{20,24},{24,20},{28,16},{17,29},{21,25},{25,21},{29,17},{1... | collective-permute-start | bytes 3145736 | tf_op jit(solution)/shard_map/ppermute | solution.py:35
  829.6 49.1 %collective-permute-start.104 = (bf16[2,512,512]{2,1,0:T(8,128)(2,1)S(1)}, bf16[2,512,512]{2,1,0:T(8,128)(2,1)}, u32[]{:S(2)}, u32[]{:S(2)}) collective-permute-start(bf16[2,512,512]{2,1,0:T(8,128)(2,1)S(1)} %pad_maximum_fusion.11.refs_4_), channel_id=1, source_target_pairs={{16,20},{20,16},{24,28},{28,24},{17,21},{21,17},{25,29},{29,25},{1... | collective-permute-start | bytes 3145736 | tf_op jit(solution)/shard_map/ppermute | solution.py:35
  866.8 58.0 %collective-permute-start.105 = (bf16[2,512,512]{2,1,0:T(8,128)(2,1)S(1)}, bf16[2,512,512]{2,1,0:T(8,128)(2,1)}, u32[]{:S(2)}, u32[]{:S(2)}) collective-permute-start(bf16[2,512,512]{2,1,0:T(8,128)(2,1)S(1)} %pad_maximum_fusion.11.refs_4_), channel_id=1, source_target_pairs={{16,24},{20,28},{24,16},{28,20},{17,25},{21,29},{25,17},{29,21},{1... | collective-permute-start | bytes 3145736 | tf_op jit(solution)/shard_map/ppermute | solution.py:35
  869.0 57.5 %collective-permute-start.106 = (bf16[2,512,512]{2,1,0:T(8,128)(2,1)S(1)}, bf16[2,512,512]{2,1,0:T(8,128)(2,1)}, u32[]{:S(2)}, u32[]{:S(2)}) collective-permute-start(bf16[2,512,512]{2,1,0:T(8,128)(2,1)S(1)} %pad_maximum_fusion.11.refs_4_), channel_id=1, source_target_pairs={{16,28},{20,24},{24,20},{28,16},{17,29},{21,25},{25,21},{29,17},{1... | collective-permute-start | bytes 3145736 | tf_op jit(solution)/shard_map/ppermute | solution.py:35
  874.3 65.6 %collective-permute-start.99 = (bf16[2,512,512]{2,1,0:T(8,128)(2,1)}, bf16[2,512,512]{2,1,0:T(8,128)(2,1)}, u32[]{:S(2)}, u32[]{:S(2)}) collective-permute-start(bf16[2,512,512]{2,1,0:T(8,128)(2,1)} %pad_maximum_fusion.10.refs_0_), channel_id=1, source_target_pairs={{0,4},{4,0},{8,12},{12,8},{1,5},{5,1},{9,13},{13,9},{2,6},{6,2},{1... | collective-permute-start | bytes 3145736 | tf_op jit(solution)/shard_map/ppermute | solution.py:35
  877.1 77.2 %collective-permute-start.100 = (bf16[2,512,512]{2,1,0:T(8,128)(2,1)}, bf16[2,512,512]{2,1,0:T(8,128)(2,1)}, u32[]{:S(2)}, u32[]{:S(2)}) collective-permute-start(bf16[2,512,512]{2,1,0:T(8,128)(2,1)} %pad_maximum_fusion.10.refs_0_), channel_id=1, source_target_pairs={{0,8},{4,12},{8,0},{12,4},{1,9},{5,13},{9,1},{13,5},{2,10},{6,14},... | collective-permute-start | bytes 3145736 | tf_op jit(solution)/shard_map/ppermute | solution.py:35
  878.8 75.6 %collective-permute-start.101 = (bf16[2,512,512]{2,1,0:T(8,128)(2,1)}, bf16[2,512,512]{2,1,0:T(8,128)(2,1)}, u32[]{:S(2)}, u32[]{:S(2)}) collective-permute-start(bf16[2,512,512]{2,1,0:T(8,128)(2,1)} %pad_maximum_fusion.10.refs_0_), channel_id=1, source_target_pairs={{0,12},{4,8},{8,4},{12,0},{1,13},{5,9},{9,5},{13,1},{2,14},{6,10},... | collective-permute-start | bytes 3145736 | tf_op jit(solution)/shard_map/ppermute | solution.py:35
  (251 other events, 5170.3 us)
Sparse Core Ops, SparseCore 0:
  525.6 62.5 reduce-scatter.16
  617.9 53.2 reduce-scatter.6
  673.5 43.1 reduce-scatter.8
  718.9 43.1 reduce-scatter.12
  764.4 43.1 reduce-scatter.10
  810.3 51.4 reduce-scatter.14

commit v3 on v2

--- a/solution.py
+++ b/solution.py
@@ -50,7 +50,7 @@
 
 
 def cost(flops):
-    return pl.CostEstimate(flops=int(flops), bytes_accessed=0, transcendentals=0)
+    return pl.CostEstimate(flops=int(3 * flops), bytes_accessed=0, transcendentals=0)
 
 
 def shape(dims, kind):
@@ -201,17 +201,17 @@
     return low_rank, jnp.where(lane < 2 * STATE, kq, 0.0)
 
 
-def rec_body(backward, n_slots, length, width, *refs):
-    n_parts = n_slots
-    parts, refs = refs[:n_parts], refs[n_parts:]
+def rec_body(backward, keep_y, n_slots, length, width, *refs):
+    parts, refs = refs[:n_slots], refs[n_slots:]
+    y_out = None
     if backward:
-        (inner, gate, dgated, wdt, vec, mask, gated_near, gated_far, lr_out, dgate_near, dgate_far,
-         dstate_out, dpart_out, ddt_out, dvec_out,
-         kq_n, kq_i, c_i, lr_n, step_i, p_i, y_i, kb, str_n, hist, dy_i, a_i, b_i, h_scr, dkq_i,
-         dlr_n, corr_n, prod, gated_tmp, dgate_tmp, drate_out) = refs
+        (inner, dy_ref, wdt, vec, mask, lr_out, dstate_out, dpart_out, ddt_out, dvec_out), refs = refs[:10], refs[10:]
+        if keep_y:
+            y_out, refs = refs[0], refs[1:]
+        (kq_n, kq_i, c_i, lr_n, step_i, p_i, y_i, kb, str_n, hist, dy_i, a_i, b_i, h_scr, dkq_i,
+         dlr_n, corr_n, prod, drate_n) = refs
     else:
-        (inner, gate, wdt, vec, mask, gated_out,
-         kq_n, kq_i, c_i, lr_n, step_i, p_i, y_i, kb, state) = refs
+        (inner, wdt, vec, mask, y_out, kq_n, kq_i, c_i, lr_n, step_i, p_i, y_i, kb, state) = refs
     nb = width // (2 * LANES)
     first = pl.program_id(0) == 0
     last = pl.program_id(0) == pl.num_programs(0) - 1
@@ -255,14 +255,13 @@
         kq = kq_n[rows, :]
         ks = jnp.sum(jnp.where(lane < STATE, kq * kq, 0.0), axis=1, keepdims=True)
         for hh, b, cols in pieces:
-            strength = sig(rate[:, cols] + vec[0:1, cols])
+            strength = sig(rate[:, cols] + vec[5:6, cols])
             step = strength / (1.0 + strength * ks)
             step_i[b, spread(j, hh), :] = step
             p_i[b, spread(j, hh), :] = step * inner[rows, cols].astype(F32)
             if backward:
                 str_n[rows, cols] = strength
-                g = gate[rows, cols]
-                dy_i[b, spread(j, hh), :] = dgated[rows, cols] * (g * sig(g))
+                dy_i[b, spread(j, hh), :] = dy_ref[rows, cols]
 
     if backward:
         hist[0] = jnp.zeros(hist.shape[1:], F32)
@@ -276,8 +275,10 @@
         ps = [p_i[b, now, :] for b in range(nb)]
         ys = [jnp.zeros((ROWS, LANES), F32) for _ in range(nb)]
         for n in range(STATE):
-            k, q = kb[n, now, :], kb[STATE + n, now, :]
+            k = kb[n, now, :]
             ck2 = c * k * k
+            if y_out is not None:
+                q = kb[STATE + n, now, :]
             for b in range(nb):
                 before = hist[t, n * nb + b] if backward else state[n * nb + b]
                 after = (c - ck2 * steps[b]) * before + k * ps[b]
@@ -285,20 +286,21 @@
                     hist[t + 1, n * nb + b] = after
                 else:
                     state[n * nb + b] = after
-                ys[b] = ys[b] + q * after
-        for b in range(nb):
-            y_i[b, now, :] = ys[b]
+                if y_out is not None:
+                    ys[b] = ys[b] + q * after
+        if y_out is not None:
+            for b in range(nb):
+                y_i[b, now, :] = ys[b]
         return carry
 
     lax.fori_loop(0, length, forward_step, 0)
 
-    if not backward:
+    if y_out is not None:
         for j in range(n_slots):
             rows = rows_of(j)
             for hh, b, cols in pieces:
-                y = y_i[b, spread(j, hh), :] + vec[1:2, cols] * inner[rows, cols].astype(F32)
-                g = gate[rows, cols]
-                gated_out[rows, cols] = (y * (g * sig(g))).astype(BF)
+                y_out[rows, cols] = y_i[b, spread(j, hh), :] + vec[6:7, cols] * inner[rows, cols].astype(F32)
+    if not backward:
         return
 
     h_scr[...] = jnp.zeros(h_scr.shape, F32)
@@ -354,38 +356,25 @@
         for i, (hh, b, cols) in enumerate(pieces):
             at = spread(j, hh)
             inn = inner[rows, cols].astype(F32)
-            a, step, dy = a_i[b, at, :], step_i[b, at, :], dy_i[b, at, :]
-            skip = vec[1:2, cols]
+            a, step, dy = a_i[b, at, :], step_i[b, at, :], dy_ref[rows, cols]
             dstep = inn * a - b_i[b, at, :]
             strength = str_n[rows, cols]
             inv = 1.0 / (1.0 + strength * ks)
             drate = (dstep * (inv * inv) * (strength * (1.0 - strength))).astype(BF)
-            drate_out[rows, cols] = drate
-            dstate_out[rows, cols] = step * a + skip * dy
+            drate_n[rows, cols] = drate
+            dstate_out[rows, cols] = step * a + vec[6:7, cols] * dy
             corr = corr + jnp.sum(dstep * (step * step), axis=1, keepdims=True)
-            y = y_i[b, at, :] + skip * inn
-            g = gate[rows, cols]
-            s = sig(g)
-            gated_tmp[rows, cols] = (y * (g * s)).astype(BF)
-            dgate_tmp[rows, cols] = (dgated[rows, cols] * y * (s * (1.0 + g * (1.0 - s)))).astype(BF)
             ddt[i] = ddt[i] + jnp.sum(drate.astype(F32), axis=0, keepdims=True)
             dskip[i] = dskip[i] + jnp.sum(dy * inn, axis=0, keepdims=True)
         corr_n[rows, :] = corr_n[rows, :] + corr
-        dlr_n[rows, :] = dlr_n[rows, :] + dot(drate_out[rows, :], wdt[...], 1, 1)
-    ddt_out[...] = dot(lr_n[...], drate_out[...], 0, 0)
+        dlr_n[rows, :] = dlr_n[rows, :] + dot(drate_n[rows, :], wdt[...], 1, 1)
+    ddt_out[...] = dot(lr_n[...], drate_n[...], 0, 0)
     dvec_out[...] = jnp.concatenate(
         [jnp.concatenate(ddt, axis=1), jnp.concatenate(dskip, axis=1), jnp.zeros((6, width), F32)], axis=0
     )
 
-    @pl.when(first)
-    def _():
-        gated_near[...] = gated_tmp[...]
-        dgate_near[...] = dgate_tmp[...]
-
     @pl.when(last)
     def _():
-        gated_far[...] = gated_tmp[...]
-        dgate_far[...] = dgate_tmp[...]
         for j in range(n_slots):
             rows = rows_of(j)
             dk, dq = [
@@ -398,7 +387,7 @@
             dpart_out[rows, :] = pack(dlr_n[rows, :], dkq)
 
 
-def rec(backward, parts, inner, gate, dgated, wdt, vec, masks):
+def rec(parts, inner, dy, wdt, vec, masks, keep_y):
     rows, channels = inner.shape
     n_slots = len(parts)
     length = rows // n_slots
@@ -414,19 +403,20 @@
     wide = pltpu.VMEM((nb, ROWS * length, LANES), F32)
     row = pltpu.VMEM((rows, LANES), F32)
     spread = pltpu.VMEM((ROWS * length, LANES), F32)
+    y_like = shape((rows, channels), F32)
     scratch = [row, spread, spread, pltpu.VMEM((rows, RANK), BF), wide, wide, wide]
     scratch += [pltpu.VMEM((2 * STATE, ROWS * length, LANES), F32)]
-    if not backward:
+    if dy is None:
         scratch += [pltpu.VMEM((STATE * nb, ROWS, LANES), F32)]
         return call(
-            partial(rec_body, False, n_slots, length, width),
-            shape((rows, channels), BF),
+            partial(rec_body, False, True, n_slots, length, width),
+            y_like,
             grid=(2,),
-            in_specs=[whole(p) for p in parts] + [block(rows), block(rows), block(RANK), block(vec.shape[0]), whole(masks)],
+            in_specs=[whole(p) for p in parts] + [block(rows), block(RANK), block(vec.shape[0]), whole(masks)],
             out_specs=block(rows),
             scratch_shapes=scratch,
-            cost_estimate=cost(25e9),
-        )(*parts, inner, gate, wdt, vec, masks)
+            cost_estimate=cost(20e9),
+        )(*parts, inner, wdt, vec, masks)
     scratch += [
         pltpu.VMEM((rows, width), F32),
         pltpu.VMEM((length + 1, STATE * nb, ROWS, LANES), F32),
@@ -439,33 +429,53 @@
         row,
         pltpu.VMEM((4 * ROWS * ROWS * 2, STATE * LANES), BF),
         pltpu.VMEM((rows, width), BF),
-        pltpu.VMEM((rows, width), BF),
-        pltpu.VMEM((rows, width), BF),
     ]
-    side = shape((rows, width), BF)
     lr_like = shape((rows, RANK), BF)
     part_like = shape((rows, 2 * LANES), BF)
+    outs = [lr_like, y_like, part_like, shape((RANK, channels), F32), shape((ROWS, channels), F32)]
+    specs = [whole(lr_like), block(rows), whole(part_like), block(RANK), block(ROWS)]
+    if keep_y:
+        outs, specs = outs + [y_like], specs + [block(rows)]
     return call(
-        partial(rec_body, True, n_slots, length, width),
-        (
-            side,
-            side,
-            lr_like,
-            side,
-            side,
-            shape((rows, channels), F32),
-            part_like,
-            shape((RANK, channels), F32),
-            shape((ROWS, channels), F32),
-        ),
+        partial(rec_body, True, keep_y, n_slots, length, width),
+        tuple(outs),
         grid=(2,),
-        in_specs=[whole(p) for p in parts]
-        + [block(rows), block(rows), block(rows), block(RANK), block(vec.shape[0]), whole(masks)],
-        out_specs=(whole(side), whole(side), whole(lr_like), whole(side), whole(side), block(rows), whole(part_like), block(RANK), block(ROWS)),
+        in_specs=[whole(p) for p in parts] + [block(rows), block(rows), block(RANK), block(vec.shape[0]), whole(masks)],
+        out_specs=tuple(specs),
         scratch_shapes=scratch,
-        cost_estimate=cost(50e9),
+        cost_estimate=cost(55e9),
         vmem=62,
-    )(*parts, inner, gate, dgated, wdt, vec, masks)
+    )(*parts, inner, dy, wdt, vec, masks)
+
+
+def gate_values(y, gate):
+    s = sig(gate)
+    return y * (gate * s), y * (s * (1.0 + gate * (1.0 - s)))
+
+
+def gate_back_body(y_ref, gate_ref, dgated_ref, gated_near, gated_far, dgate_near, dgate_far):
+    half = gated_near.shape[1]
+    for h, (gated, dgate) in enumerate([(gated_near, dgate_near), (gated_far, dgate_far)]):
+        for b in range(half // LANES):
+            cols = slice(b * LANES, (b + 1) * LANES)
+            at = slice(h * half + b * LANES, h * half + (b + 1) * LANES)
+            one, two = gate_values(y_ref[:, at], gate_ref[:, at])
+            gated[:, cols] = one.astype(BF)
+            dgate[:, cols] = (dgated_ref[:, at] * two).astype(BF)
+
+
+def gate_back(n_slots, y, gate, dgated):
+    rows, channels = y.shape
+    length = rows // n_slots
+    side = shape((rows, channels // 2), BF)
+    return call(
+        gate_back_body,
+        (side,) * 4,
+        grid=(n_slots,),
+        in_specs=[pl.BlockSpec((length, channels), lambda j: (j, 0))] * 3,
+        out_specs=[pl.BlockSpec((length, channels // 2), lambda j: (j, 0))] * 4,
+        cost_estimate=cost(3e9),
+    )(y, gate, dgated)
 
 
 def conv_bwd_body(n_slots, p0, p1, p2, p3, x_ref, inner, dstate, mask_ref, vec_ref, wdk_ref,
@@ -538,60 +548,436 @@
     )(*parts, x, inner, dstate, masks, vec, wdk)
 
 
-def cut_body(where_ref, w_ref, gain_ref, keep_ref, send_ref):
-    half = w_ref.shape[1] // 2
+SMALL = 448
+DOWN, KQ, DT, VEC = 0, 128, 160, 288
+
+
+def cut_small_body(where_ref, w_ref, gain_ref, *refs):
+    sources, (keep_ref, send_ref, small), fetched, sems = refs[:7], refs[7:10], refs[10:17], refs[17]
+    i = pl.program_id(0)
+    rows, sub = w_ref.shape[0], keep_ref.shape[1]
+    part = keep_ref.shape[0] - rows
+    copies = [pltpu.make_async_copy(v, f, sems.at[n]) for n, (v, f) in enumerate(zip(sources, fetched))]
+
+    @pl.when(i == 0)
+    def _():
+        for copy in copies:
+            copy.start()
+
+    mine = where_ref[1] == 0
     scaled = w_ref[...].astype(F32) * gain_ref[...]
-    first, second = scaled[:, :half].astype(BF), scaled[:, half:].astype(BF)
-    mine = where_ref[1] == 0
-    keep_ref[...] = jnp.where(mine, first, second)
-    send_ref[...] = jnp.where(mine, second, first)
-
-
-def cut(where, weight, gain, side, n_dp, n_grp, sub):
+    first, second = scaled[:, :sub].astype(BF), scaled[:, sub:].astype(BF)
+    keep_ref[0:rows, :] = jnp.where(mine, first, second)
+    send_ref[0:rows, :] = jnp.where(mine, second, first)
+
+    @pl.when(i == 0)
+    def _():
+        for copy in copies:
+            copy.wait()
+        down, kq, dt, conv, conv_bias, dt_bias, skip = fetched
+        at = pl.ds(pl.multiple_of(where_ref[0] * 2 * sub, 2 * sub), 2 * sub)
+        small[DOWN:KQ, :] = down[at, :].astype(F32).T.astype(BF)
+        small[KQ:DT, :] = kq[:, at]
+        small[DT:VEC, :] = dt[:, at]
+        last = [v[:, at].astype(F32) for v in (conv, conv_bias, dt_bias, skip)] + [jnp.zeros((9, 2 * sub), F32)]
+        small[VEC : VEC + 16, :] = jnp.concatenate(last, axis=0).astype(BF)
+        small[VEC + 16 :, :] = jnp.zeros((SMALL - VEC - 16, 2 * sub), BF)
+
+    piece = small[pl.ds(pl.multiple_of(i * part, 16), part), :]
+    first, second = piece[:, :sub], piece[:, sub:]
+    keep_ref[rows:, :] = jnp.where(mine, first, second)
+    send_ref[rows:, :] = jnp.where(mine, second, first)
+
+
+def cut_small(where, weight, gain, down, kq, dt, conv, conv_bias, dt_bias, skip, n_dp, n_grp, sub):
     rows = weight.shape[0]
-    out = shape((rows, n_dp * sub), BF)
+    part = SMALL // n_dp
+    out = shape((rows + part, n_dp * sub), BF)
+    smalls = [down, kq, dt, conv, conv_bias, dt_bias, skip]
     return call(
-        cut_body,
+        cut_small_body,
         (out, out),
         grid_spec=pltpu.PrefetchScalarGridSpec(
             num_scalar_prefetch=1,
             grid=(n_dp,),
             in_specs=[
-                pl.BlockSpec((rows, 2 * sub), lambda i, w: (0, (side * n_dp + i) * n_grp + w[0])),
+                pl.BlockSpec((rows, 2 * sub), lambda i, w: (0, i * n_grp + w[0])),
                 pl.BlockSpec((rows, 1), lambda i, w: (0, 0)),
+            ]
+            + [pl.BlockSpec(memory_space=pltpu.HBM)] * 7,
+            out_specs=[pl.BlockSpec((rows + part, sub), lambda i, w: (0, i))] * 2,
+            scratch_shapes=[pltpu.VMEM((SMALL, 2 * sub), BF)]
+            + [pltpu.VMEM(v.shape, BF) for v in smalls]
+            + [pltpu.SemaphoreType.DMA((7,))],
+        ),
+        cost_estimate=cost(3e9),
+    )(where, weight, gain, *smalls)
+
+
+def cut_out_body(where_ref, w_ref, gain_ref, o_ref, keep_ref, send_ref):
+    i = pl.program_id(0)
+    rows, sub = w_ref.shape[0], keep_ref.shape[1]
+    mine = where_ref[1] == 0
+    scaled = w_ref[...].astype(F32) * gain_ref[...]
+    first, second = scaled[:, :sub].astype(BF), scaled[:, sub:].astype(BF)
+    keep_ref[0:rows, :] = jnp.where(mine, first, second)
+    send_ref[0:rows, :] = jnp.where(mine, second, first)
+    n = pl.num_programs(0)
+    wide = o_ref.shape[1] // 4
+    for c in range(4):
+        lanes = pl.ds(pl.multiple_of(c * wide + i * sub, sub), sub)
+        first, second = o_ref[0:sub, lanes], o_ref[sub:, lanes]
+        at = slice(rows + c * sub, rows + (c + 1) * sub)
+        keep_ref[at, :] = jnp.where(mine, first, second)
+        send_ref[at, :] = jnp.where(mine, second, first)
+
+
+def cut_out(where, weight, gain, out_weight, n_dp, n_grp, sub):
+    rows = weight.shape[0]
+    out = shape((rows + 4 * sub, n_dp * sub), BF)
+    return call(
+        cut_out_body,
+        (out, out),
+        grid_spec=pltpu.PrefetchScalarGridSpec(
+            num_scalar_prefetch=1,
+            grid=(n_dp,),
+            in_specs=[
+                pl.BlockSpec((rows, 2 * sub), lambda i, w: (0, (n_dp + i) * n_grp + w[0])),
+                pl.BlockSpec((rows, 1), lambda i, w: (0, 0)),
+                pl.BlockSpec((2 * sub, out_weight.shape[1]), lambda i, w: (w[0], 0)),
             ],
-            out_specs=[pl.BlockSpec((rows, sub), lambda i, w: (0, i))] * 2,
+            out_specs=[pl.BlockSpec((rows + 4 * sub, sub), lambda i, w: (0, i))] * 2,
         ),
+        cost_estimate=cost(3e9),
+    )(where, weight, gain, out_weight)
+
+
+def flat_call(body, out_shape, arrays, specs=None, scratch=(), flops=0, vmem=48):
+    def whole(v):
+        return pl.BlockSpec(v.shape, lambda i: (0,) * len(v.shape))
+
+    outs = out_shape if isinstance(out_shape, tuple) else (out_shape,)
+    out_specs = tuple(whole(v) for v in outs)
+    return call(
+        body,
+        out_shape,
+        grid=(1,),
+        in_specs=[(specs or {}).get(n, whole(v)) for n, v in enumerate(arrays)],
+        out_specs=out_specs if isinstance(out_shape, tuple) else out_specs[0],
+        scratch_shapes=list(scratch),
+        cost_estimate=cost(flops),
+        vmem=vmem,
+    )(*arrays)
+
+
+def q_block(q, which, rows):
+    return pl.BlockSpec((q.shape[0], rows, q.shape[2]), lambda i: (0, which, 0))
+
+
+def blocks_sum(a_ref, w_ref, rows):
+    total = None
+    for p in range(w_ref.shape[0]):
+        term = dot(a_ref[:, p * rows : (p + 1) * rows], w_ref[p, 0:rows, :], 1, 0)
+        total = term if total is None else total + term
+    return total
+
+
+def first_body(n_slots, rows, a_ref, mask_ref, near_ref, far_ref, *refs):
+    x_ref, inner_ref, part_ref, cat_ref, wdt_ref, vec_ref, pad_ref, small = refs
+    half = x_ref.shape[1] // 2
+    n_dp = near_ref.shape[0]
+    sub = half // n_dp
+    length = x_ref.shape[0] // n_slots
+    part = SMALL // n_dp
+    for h, w_ref in enumerate((near_ref, far_ref)):
+        for p in range(n_dp):
+            lanes = slice(h * half + p * sub, h * half + (p + 1) * sub)
+            for i in range(n_dp):
+                small[i * part : (i + 1) * part, lanes] = w_ref[p, rows:, i * sub : (i + 1) * sub]
+    cat_ref[0:DT, :] = small[0:DT, :]
+    cat_ref[DT:, :] = jnp.zeros((cat_ref.shape[0] - DT, 2 * half), BF)
+    wdt_ref[...] = small[DT:VEC, :]
+    vec_ref[...] = small[VEC : VEC + 16, :].astype(F32)
+    both = jnp.zeros((x_ref.shape[0], 2 * LANES), F32)
+    for h, w_ref in enumerate((near_ref, far_ref)):
+        lanes = slice(h * half, (h + 1) * half)
+        x_ref[:, lanes] = blocks_sum(a_ref, w_ref, rows)
+        for j in range(n_slots):
+            at = slice(j * length, (j + 1) * length)
+            for b in range(half // LANES):
+                cols = slice(h * half + b * LANES, h * half + (b + 1) * LANES)
+                c, _ = conv_of(x_ref, at, pad_ref, mask_ref, vec_ref, cols)
+                inner_ref[at, cols] = (c * sig(c)).astype(BF)
+        both = both + dot(inner_ref[:, lanes], cat_ref[:, lanes], 1, 1)
+    part_ref[...] = pack(both[:, :RANK], both[:, RANK:])
+
+
+def first_products(n_slots, a, masks, near, far, rows):
+    n, half = a.shape[0], near.shape[2]
+    return flat_call(
+        partial(first_body, n_slots, rows),
+        (
+            shape((n, 2 * half), F32),
+            shape((n, 2 * half), BF),
+            shape((n, 2 * LANES), BF),
+            shape((2 * LANES, 2 * half), BF),
+            shape((RANK, 2 * half), BF),
+            shape((16, 2 * half), F32),
+        ),
+        [a, masks, near, far],
+        scratch=[pltpu.VMEM((ROWS + n // n_slots, LANES), F32), pltpu.VMEM((SMALL, 2 * half), BF)],
+        flops=8e9,
+    )
+
+
+def gate_body(rows, a_ref, y_ref, near_ref, far_ref, gate_ref, gated_near, gated_far):
+    half = gated_near.shape[1]
+    for h, (w_ref, gated) in enumerate([(near_ref, gated_near), (far_ref, gated_far)]):
+        at = slice(h * half, (h + 1) * half)
+        gate = blocks_sum(a_ref, w_ref, rows)
+        gate_ref[:, at] = gate
+        gated[...] = (y_ref[:, at] * (gate * sig(gate))).astype(BF)
+
+
+def gate_product(a, y, near, far, rows):
+    half = near.shape[2]
+    side = shape((a.shape[0], half), BF)
+    return flat_call(
+        partial(gate_body, rows),
+        (shape(y.shape, F32), side, side),
+        [a, y, near, far],
+        specs={2: q_block(near, 0, rows), 3: q_block(far, 0, rows)},
+        flops=6e9,
+    )
+
+
+def out_weight_of(near_ref, far_ref, w_scr):
+    half = w_scr.shape[0] // 2
+    n_dp = near_ref.shape[0]
+    sub = half // n_dp
+    wide = w_scr.shape[1] // 4
+    for h, w_ref in enumerate((near_ref, far_ref)):
+        for p in range(n_dp):
+            for c in range(4):
+                block = w_ref[p, c * sub : (c + 1) * sub, :]
+                w_scr[h * half + p * sub : h * half + (p + 1) * sub, c * wide : (c + 1) * wide] = block
+
+
+def branch_body(left_near, left_far, near_ref, far_ref, out_ref, w_scr):
+    out_weight_of(near_ref, far_ref, w_scr)
+    half = left_near.shape[1]
+    wide = w_scr.shape[1] // 4
+    for c in range(4):
+        lanes = slice(c * wide, (c + 1) * wide)
+        total = dot(left_near[...], w_scr[:half, lanes], 1, 0) + dot(left_far[...], w_scr[half:, lanes], 1, 0)
+        out_ref[:, lanes] = total.astype(BF)
+
+
+def branch_product(left_near, left_far, near, far, rows):
+    half = near.shape[2]
+    return flat_call(
+        branch_body,
+        shape((left_near.shape[0], 4 * half), BF),
+        [left_near, left_far, near, far],
+        specs={2: q_block(near, 1, rows), 3: q_block(far, 1, rows)},
+        scratch=[pltpu.VMEM((2 * half, 4 * half), BF)],
+        flops=5e9,
+    )
+
+
+def dgated_body(d_ref, y_ref, gate_ref, near_ref, far_ref, dy_ref, dgate_near, dgate_far, w_scr):
+    out_weight_of(near_ref, far_ref, w_scr)
+    half = dgate_near.shape[1]
+    for h, dgate in enumerate((dgate_near, dgate_far)):
+        at = slice(h * half, (h + 1) * half)
+        dgated = dot(d_ref[...], w_scr[at, :], 1, 1)
+        gate = gate_ref[:, at]
+        dy_ref[:, at] = dgated * (gate * sig(gate))
+        dgate[...] = (dgated * gate_values(y_ref[:, at], gate)[1]).astype(BF)
+
+
+def dgated_product(dbranch, y, gate, near, far, rows):
+    half = near.shape[2]
+    side = shape((dbranch.shape[0], half), BF)
+    return flat_call(
+        dgated_body,
+        (shape(y.shape, F32), side, side),
+        [dbranch, y, gate, near, far],
+        specs={3: q_block(near, 1, rows), 4: q_block(far, 1, rows)},
+        scratch=[pltpu.VMEM((2 * half, dbranch.shape[1]), BF)],
+        flops=6e9,
+    )
+
+
+def dnormed_body(rows, dx_near, dx_far, dg_near, dg_far, p_near, p_far, q_near, q_far, out_ref):
+    for p in range(p_near.shape[0]):
+        total = dot(dx_near[...], p_near[p, 0:rows, :], 1, 1) + dot(dx_far[...], p_far[p, 0:rows, :], 1, 1)
+        total = total + dot(dg_near[...], q_near[p], 1, 1) + dot(dg_far[...], q_far[p], 1, 1)
+        out_ref[:, p * rows : (p + 1) * rows] = total.astype(BF)
+
+
+def dnormed_product(lefts, p_near, p_far, q_near, q_far, rows):
+    n_dp = p_near.shape[0]
+    return flat_call(
+        partial(dnormed_body, rows),
+        shape((lefts[0].shape[0], n_dp * rows), BF),
+        [*lefts, p_near, p_far, q_near, q_far],
+        specs={6: q_block(q_near, 0, rows), 7: q_block(q_far, 0, rows)},
+        flops=8e9,
+    )
+
+
+def grad_p_body(a_ref, a_far, dx_ref, dx_come, small_ref, small_come, out_ref):
+    rows = a_ref.shape[1]
+    value = dot(a_ref[...], dx_ref[...], 0, 0) + dot(a_far[...], dx_come[...], 0, 0)
+    out_ref[0, 0:rows, :] = value.astype(BF)
+    out_ref[0, rows:, :] = (small_ref[...] + small_come[...].astype(F32)).astype(BF)
+
+
+def grad_p(a, a_far, dx, dx_come, small, small_come, n_dp):
+    rows = a.shape[1] // n_dp
+    part = small.shape[0] // n_dp
+    half = dx.shape[1]
+    col = pl.BlockSpec((a.shape[0], rows), lambda i: (0, i))
+    whole = pl.BlockSpec(dx.shape, lambda i: (0, 0))
+    block = pl.BlockSpec((part, half), lambda i: (i, 0))
+    return call(
+        grad_p_body,
+        shape((n_dp, rows + part, half), BF),
+        grid=(n_dp,),
+        in_specs=[col, col, whole, whole, block, block],
+        out_specs=pl.BlockSpec((1, rows + part, half), lambda i: (i, 0, 0)),
+        cost_estimate=cost(5e9),
+    )(a, a_far, dx, dx_come, small, small_come)
+
+
+def grad_q_body(a_ref, a_far, dg_ref, dg_come, gated_ref, gated_come, db_ref, db_far, out_ref):
+    rows = a_ref.shape[1]
+    sub = gated_ref.shape[1]
+    wide = db_ref.shape[1] // 4
+    value = dot(a_ref[...], dg_ref[...], 0, 0) + dot(a_far[...], dg_come[...], 0, 0)
+    out_ref[0, 0:rows, :] = value.astype(BF)
+    value = dot(gated_ref[...], db_ref[...], 0, 0) + dot(gated_come[...], db_far[...], 0, 0)
+    for c in range(4):
+        out_ref[0, rows + c * sub : rows + (c + 1) * sub, :] = value[:, c * wide : (c + 1) * wide].astype(BF)
+
+
+def grad_q(a, a_far, dg, dg_come, gated, gated_come, db, db_far, n_dp):
+    rows = a.shape[1] // n_dp
+    half = dg.shape[1]
+    sub = half // n_dp
+    col = pl.BlockSpec((a.shape[0], rows), lambda i: (0, i))
+    sub_col = pl.BlockSpec((a.shape[0], sub), lambda i: (0, i))
+
+    def whole(v):
+        return pl.BlockSpec(v.shape, lambda i: (0, 0))
+
+    return call(
+        grad_q_body,
+        shape((n_dp, rows + 4 * sub, half), BF),
+        grid=(n_dp,),
+        in_specs=[col, col, whole(dg), whole(dg), sub_col, sub_col, whole(db), whole(db)],
+        out_specs=pl.BlockSpec((1, rows + 4 * sub, half), lambda i: (i, 0, 0)),
+        cost_estimate=cost(8e9),
+    )(a, a_far, dg, dg_come, gated, gated_come, db, db_far)
+
+
+def small_grads_body(dsmall, ddt, dconv, dvec, near_ref, far_ref, scr):
+    half = near_ref.shape[1]
+    sub = half // 4
+    part = SMALL // 4
+    scr[DOWN:DT, :] = dsmall[0:DT, :]
+    scr[DT:VEC, :] = ddt[...]
+    rows = [dconv[0:5, :], dvec[0:2, :], jnp.zeros((1, 2 * half), F32)]
+    scr[VEC : VEC + 8, :] = jnp.concatenate(rows, axis=0)
+    scr[VEC + 8 :, :] = jnp.zeros((SMALL - VEC - 8, 2 * half), F32)
+    for block in range(4):
+        at = slice(block * part, (block + 1) * part)
+        for i in range(4):
+            rows = slice(i * part, (i + 1) * part)
+            lanes = slice(i * sub, (i + 1) * sub)
+            near_ref[at, lanes] = scr[rows, block * sub : (block + 1) * sub]
+            far_ref[at, lanes] = scr[rows, half + block * sub : half + (block + 1) * sub].astype(BF)
+
+
+def small_grads(dsmall, ddt, dconv, dvec):
+    half = ddt.shape[1] // 2
+    return call(
+        small_grads_body,
+        (shape((SMALL, half), F32), shape((SMALL, half), BF)),
+        scratch_shapes=[pltpu.VMEM((SMALL, 2 * half), F32)],
         cost_estimate=cost(2e9),
-    )(where, weight, gain)
-
-
-def join_body(where_ref, w_ref, gain_ref, *refs):
-    parts, out_ref, sum_ref = refs[:-3], refs[-2], refs[-1]
-    n = len(parts) // 2
-    sub = parts[0].shape[2]
+    )(dsmall, ddt, dconv, dvec)
+
+
+def join_values(n_grp, where_ref, parts):
     mine = where_ref[1] == 0
-
-    @pl.when(pl.program_id(0) == 0)
+    for d in range(n_grp):
+        for h in (0, 1):
+            sub = parts[0].shape[2]
+            at = pl.ds(pl.multiple_of(((where_ref[0] ^ d) * 2 + h) * sub, sub), sub)
+            yield at, jnp.where(mine, parts[d][h], parts[n_grp + d][h]).astype(F32)
+
+
+def join_p_body(n_grp, n_dp, where_ref, w_ref, gain_ref, *refs):
+    parts = refs[: 2 * n_grp]
+    out_ref, sum_ref, down_ref, kq_ref, dt_ref, conv_ref, cb_ref, db_ref, skip_ref, small = refs[2 * n_grp + 1 :]
+    i = pl.program_id(0)
+    rows, sub = w_ref.shape[0], parts[0].shape[2]
+    part = parts[0].shape[1] - rows
+
+    @pl.when(i == 0)
     def _():
         sum_ref[...] = jnp.zeros(sum_ref.shape, F32)
 
-    for d in range(n):
-        for h in (0, 1):
-            value = jnp.where(mine, parts[d][h], parts[n + d][h]).astype(F32)
-            at = pl.ds(pl.multiple_of(((where_ref[0] ^ d) * 2 + h) * sub, sub), sub)
-            out_ref[:, at] = value * gain_ref[...]
-            sum_ref[...] += value * w_ref[:, at].astype(F32)
-
-
-def join(where, weight, gain, parts, before, side, n_dp):
+    for at, value in join_values(n_grp, where_ref, parts):
+        out_ref[:, at] = value[:rows] * gain_ref[...]
+        sum_ref[...] += value[:rows] * w_ref[:, at].astype(F32)
+        small[pl.ds(pl.multiple_of(i * part, 16), part), at] = value[rows:]
+
+    @pl.when(i == n_dp - 1)
+    def _():
+        for b in range(down_ref.shape[0] // LANES):
+            at = slice(b * LANES, (b + 1) * LANES)
+            down_ref[at, :] = small[DOWN:KQ, at].T
+        kq_ref[...] = small[KQ:DT, :]
+        dt_ref[...] = small[DT:VEC, :]
+        conv_ref[...] = small[VEC : VEC + 4, :]
+        cb_ref[...] = small[VEC + 4 : VEC + 5, :]
+        db_ref[...] = small[VEC + 5 : VEC + 6, :]
+        skip_ref[...] = small[VEC + 6 : VEC + 7, :]
+
+
+def join_q_body(n_grp, n_dp, where_ref, w_ref, gain_ref, *refs):
+    parts, out_ref, sum_ref, o_ref = refs[: 2 * n_grp], refs[-3], refs[-2], refs[-1]
+    i = pl.program_id(0)
+    rows, sub = w_ref.shape[0], parts[0].shape[2]
+    wide = o_ref.shape[1] // 4
+
+    @pl.when(i == 0)
+    def _():
+        sum_ref[...] = jnp.zeros(sum_ref.shape, F32)
+
+    for at, value in join_values(n_grp, where_ref, parts):
+        out_ref[:, at] = value[:rows] * gain_ref[...]
+        sum_ref[...] += value[:rows] * w_ref[:, at].astype(F32)
+        for c in range(4):
+            lanes = pl.ds(pl.multiple_of(c * wide + i * sub, sub), sub)
+            o_ref[at, lanes] = value[rows + c * sub : rows + (c + 1) * sub]
+
+
+def join_packed(body, where, weight, gain, parts, before, side, n_dp, extras, scratch=()):
     rows = weight.shape[0]
+    n_grp = len(parts) // 2
     sub = parts[0].shape[2] // n_dp
-    wide = 2 * (len(parts) // 2) * sub
-    part = pl.BlockSpec((2, rows, sub), lambda i, w: (0, 0, i))
+    wide = 2 * n_grp * sub
+    dims = (2, parts[0].shape[1], sub)
+    mine = pl.BlockSpec(dims, lambda i, w: (0, 0, i * (1 - w[1])))
+    other = pl.BlockSpec(dims, lambda i, w: (0, 0, i * w[1]))
+    last = [] if before is None else [before]
     return call(
-        join_body,
-        (shape(weight.shape, F32), shape((rows, sub), F32)),
+        partial(body, n_grp, n_dp),
+        (shape(weight.shape, F32), shape((rows, sub), F32), *extras),
         grid_spec=pltpu.PrefetchScalarGridSpec(
             num_scalar_prefetch=1,
             grid=(n_dp,),
@@ -599,44 +985,19 @@
                 pl.BlockSpec((rows, wide), lambda i, w: (0, side * n_dp + i)),
                 pl.BlockSpec((rows, 1), lambda i, w: (0, 0)),
             ]
-            + [part] * len(parts)
-            + [pl.BlockSpec(memory_space=pl.ANY)],
+            + [mine] * n_grp
+            + [other] * n_grp
+            + [pl.BlockSpec(memory_space=pl.ANY)] * len(last),
             out_specs=[
                 pl.BlockSpec((rows, wide), lambda i, w: (0, side * n_dp + i)),
                 pl.BlockSpec((rows, sub), lambda i, w: (0, 0)),
-            ],
+            ]
+            + [pl.BlockSpec(v.shape, lambda i, w: (0, 0)) for v in extras],
+            scratch_shapes=list(scratch),
         ),
-        input_output_aliases={3 + len(parts): 0} if before.shape == weight.shape else {},
-        cost_estimate=cost(5e9),
-    )(where, weight, gain, *parts, before)
-
-
-def join_rows_body(where_ref, *refs):
-    parts, out_ref = refs[:-1], refs[-1]
-    n = len(parts) // 2
-    sub = parts[0].shape[1]
-    mine = where_ref[1] == 0
-    for d in range(n):
-        for h in (0, 1):
-            value = jnp.where(mine, parts[d][h], parts[n + d][h]).astype(F32)
-            out_ref[pl.ds(pl.multiple_of(((where_ref[0] ^ d) * 2 + h) * sub, sub), sub), :] = value
-
-
-def join_rows(where, parts, width):
-    sub = parts[0].shape[1]
-    rows = len(parts) * sub
-    step = 512
-    return call(
-        join_rows_body,
-        shape((rows, width), F32),
-        grid_spec=pltpu.PrefetchScalarGridSpec(
-            num_scalar_prefetch=1,
-            grid=(width // step,),
-            in_specs=[pl.BlockSpec((2, sub, step), lambda i, w: (0, 0, i))] * len(parts),
-            out_specs=pl.BlockSpec((rows, step), lambda i, w: (0, i)),
-        ),
-        cost_estimate=cost(4e9),
-    )(where, *parts)
+        input_output_aliases={3 + len(parts): 0} if last else {},
+        cost_estimate=cost(8e9),
+    )(where, weight, gain, *parts, *last)
 
 
 def rms_of(hidden):
@@ -657,26 +1018,15 @@
     return spread, valid
 
 
-def gathered(value, axis):
-    n_dp = lax.axis_size("dp")
-    if n_dp != 4:
-        return lax.all_gather(value, "dp", axis=axis, tiled=True)
-    z = lax.axis_index("dp")
-    left = lax.ppermute(value, "dp", [(i, (i + 1) % 4) for i in range(4)])
-    right = lax.ppermute(value, "dp", [(i, (i - 1) % 4) for i in range(4)])
-    up = lax.ppermute(left, "dp", [(1, 2), (2, 3)])
-    down = lax.ppermute(right, "dp", [(1, 0), (2, 1)])
-    across = jnp.where(z < 2, down, up)
-    size = value.shape[axis]
-    dims = list(value.shape)
-    dims[axis] = 4 * size
-    out = jnp.zeros(dims, value.dtype)
-    for shift, piece in ((0, value), (3, left), (1, right), (2, across)):
-        out = lax.dynamic_update_slice_in_dim(out, piece, (z + shift) % 4 * size, axis)
-    return out
-
-
-def on_device(boundary, doc_lengths, norm_gain, in_weight, conv_weight, conv_bias, down_weight, kq_weight,
+def everywhere(value, axis):
+    return lax.all_gather(value, "dp", axis=axis, tiled=True)
+
+
+def after(value, *others):
+    return lax.optimization_barrier((value, *others))[0]
+
+
+def on_any_line(boundary, doc_lengths, norm_gain, in_weight, conv_weight, conv_bias, down_weight, kq_weight,
               dt_weight, dt_bias, skip_weight, out_weight):
     s = lax.axis_index("section")
     g = lax.axis_index("grp")
@@ -687,9 +1037,7 @@
     block = inner // n_dp
     sub = block // (2 * n_grp)
     half = sub * n_dp
-    aligned = sub % LANES == 0
     mine_first = s == 0
-    where = jnp.stack([g, s]).astype(jnp.int32)
     gain = norm_gain[0].astype(F32)[:, None]
 
     def pick(first, second):
@@ -712,8 +1060,6 @@
         return pick(*halves), pick(halves[1], halves[0])
 
     def side(which):
-        if aligned:
-            return cut(where, in_weight[0], gain, which, n_dp, n_grp, sub)
         part = in_weight[0, :, which * inner : (which + 1) * inner]
         return columns((part.astype(F32) * gain).astype(BF))
 
@@ -743,16 +1089,15 @@
 
     layers = []
     for l in (0, 1):
-        w_s = jnp.concatenate(with_far(gathered(s_sides[l], 1)), axis=1)
-        w_x = with_far(gathered(x_sides[l], 0))
-        w_g = with_far(gathered(g_sides[l], 0))
-        w_o = with_far(gathered(o_sides[l], 0))
+        w_s = jnp.concatenate(with_far(everywhere(s_sides[l], 1)), axis=1)
+        w_x = with_far(everywhere(x_sides[l], 0))
+        w_g = with_far(everywhere(g_sides[l], 0))
+        w_o = with_far(everywhere(o_sides[l], 0))
         cat = w_s[: 2 * LANES]
         wdt = w_s[2 * LANES : 2 * LANES + RANK]
         tail = w_s[2 * LANES + RANK :].astype(F32)
-        conv_vec = jnp.concatenate([tail[:5], jnp.zeros((3, tail.shape[1]), F32)], axis=0)
-        rate_vec = jnp.concatenate([tail[5:7], jnp.zeros((6, tail.shape[1]), F32)], axis=0)
-        layers.append((w_x, w_g, w_o, cat, wdt, conv_vec, rate_vec))
+        vec = jnp.concatenate([tail, jnp.zeros((9, tail.shape[1]), F32)], axis=0)
+        layers.append((w_x, w_g, w_o, cat, wdt, vec))
 
     def group(value):
         return jnp.concatenate([value] + peers(value), axis=0)
@@ -764,17 +1109,23 @@
         return total
 
     def forward(h, layer):
-        w_x, w_g, w_o, cat, wdt, conv_vec, rate_vec = layer
+        w_x, w_g, w_o, cat, wdt, vec = layer
         a = group((h * rms_of(h)).astype(BF))
-        x, act, part = proj_conv(n_grp, a, *w_x, masks, conv_vec, cat)
+        x, act, part = proj_conv(n_grp, a, *w_x, masks, vec, cat)
         gate = proj(a, *w_g, 0)
         return a, x, gate, act, [part] + peers(part)
 
+    def gated_back(saved, layer, dgated, y, rec_out):
+        gate = saved[2]
+        if y is None:
+            y = rec_out[5]
+        return gate_back(n_grp, y, gate, dgated) + tuple(rec_out)
+
     def backward(h, dout, dbranch, layer, saved, rec_out):
-        w_x, w_g, w_o, cat, wdt, conv_vec, rate_vec = layer
+        w_x, w_g, w_o, cat, wdt, vec = layer
         a, x, gate, act, parts = saved
-        gated_near, gated_far, lr, dgate_near, dgate_far, dstate, dpart, ddt, dvec = rec_out
-        dx_near, dx_far, dsmall, dconv = conv_bwd([dpart] + peers(dpart), x, act, dstate, masks, conv_vec, cat)
+        gated_near, gated_far, dgate_near, dgate_far, lr, dstate, dpart, ddt, dvec = rec_out[:9]
+        dx_near, dx_far, dsmall, dconv = conv_bwd([dpart] + peers(dpart), x, act, dstate, masks, vec, cat)
         scaled = scatter(total_of([dx_near, dx_far, dgate_near, dgate_far], [*w_x, *w_g], 1))
         rms = rms_of(h)
         own = h * rms
@@ -797,21 +1148,26 @@
 
     h0 = hidden.astype(F32)
     saved0 = forward(h0, layers[0])
-    gated0 = rec(False, saved0[4], saved0[3], saved0[2], None, layers[0][4], layers[0][6], masks)
+    y0 = rec(saved0[4], saved0[3], None, layers[0][4], layers[0][5], masks, True)
+    gated0 = gate_values(y0, saved0[2])[0].astype(BF)
     branch0 = scatter(total_of([gated0[:, :half], gated0[:, half:]], layers[0][2], 0))
     h1 = (h0 + valid * branch0).astype(BF).astype(F32)
     saved1 = forward(h1, layers[1])
     dout1 = cotangent.astype(F32)
     dbranch1 = group((valid * dout1).astype(BF))
     dgated1 = proj(dbranch1, *layers[1][2], 1)
-    rec1 = rec(True, saved1[4], saved1[3], saved1[2], dgated1, layers[1][4], layers[1][6], masks)
+    dy1 = gate_values(dgated1, saved1[2])[0]
+    rec1 = rec(saved1[4], saved1[3], dy1, layers[1][4], layers[1][5], masks, True)
+    rec1 = gated_back(saved1, layers[1], dgated1, None, rec1)
     branch1 = scatter(total_of(rec1[:2], layers[1][2], 0))
     out1 = h1 + valid * branch1
     dh1, grads1 = backward(h1, dout1, dbranch1, layers[1], saved1, rec1)
     dout0 = dh1.astype(BF).astype(F32)
     dbranch0 = group((valid * dout0).astype(BF))
     dgated0 = proj(dbranch0, *layers[0][2], 1)
-    rec0 = rec(True, saved0[4], saved0[3], saved0[2], dgated0, layers[0][4], layers[0][6], masks)
+    dy0 = gate_values(dgated0, saved0[2])[0]
+    rec0 = rec(saved0[4], saved0[3], dy0, layers[0][4], layers[0][5], masks, False)
+    rec0 = gated_back(saved0, layers[0], dgated0, y0, rec0)
     dh0, grads0 = backward(h0, dout0, dbranch0, layers[0], saved0, rec0)
 
     far = swap(pick(out1, dh0), "section", 1)
@@ -835,20 +1191,14 @@
 
     smalls = in_order([v[:, :, width:] for v in o0], [v[:, :, width:] for v in o1]).astype(F32)
     grad_small = smalls.transpose(3, 0, 1, 2).reshape(smalls.shape[3], block)
-    if aligned:
-        grad_in, sum_g = join(where, in_weight[0], gain, g0 + g1, gain, 1, n_dp)
-        grad_in, sum_x = join(where, in_weight[0], gain, x0 + x1, grad_in, 0, n_dp)
-        grad_gain = jnp.sum(sum_g + sum_x, axis=1)
-        grad_out = join_rows(where, o0 + o1, width)
-    else:
-        sides = []
-        for first, second in ((x0, x1), (g0, g1)):
-            value = in_order(first, second).reshape(n_grp, 2, -1, n_dp, sub)
-            sides.append(value.transpose(2, 3, 0, 1, 4).reshape(value.shape[2], inner))
-        product = jnp.concatenate(sides, axis=1).astype(F32)
-        grad_in = product * gain
-        grad_gain = jnp.sum(product * in_weight[0].astype(F32), axis=1)
-        grad_out = in_order([v[:, :, :width] for v in o0], [v[:, :, :width] for v in o1]).astype(F32).reshape(block, width)
+    sides = []
+    for first, second in ((x0, x1), (g0, g1)):
+        value = in_order(first, second).reshape(n_grp, 2, -1, n_dp, sub)
+        sides.append(value.transpose(2, 3, 0, 1, 4).reshape(value.shape[2], inner))
+    product = jnp.concatenate(sides, axis=1).astype(F32)
+    grad_in = product * gain
+    grad_gain = jnp.sum(product * in_weight[0].astype(F32), axis=1)
+    grad_out = in_order([v[:, :, :width] for v in o0], [v[:, :, :width] for v in o1]).astype(F32).reshape(block, width)
     base = 2 * LANES + RANK
     return (
         result,
@@ -865,9 +1215,173 @@
     )
 
 
+def on_device(boundary, doc_lengths, norm_gain, in_weight, conv_weight, conv_bias, down_weight, kq_weight,
+              dt_weight, dt_bias, skip_weight, out_weight):
+    s = lax.axis_index("section")
+    g = lax.axis_index("grp")
+    n_grp = lax.axis_size("grp")
+    n_dp = lax.axis_size("dp")
+    length, width = boundary.shape[3], boundary.shape[4]
+    inner = in_weight.shape[2] // 2
+    block = inner // n_dp
+    sub = block // (2 * n_grp)
+    n_rows = width // n_dp
+    mine_first = s == 0
+    where = jnp.stack([g, s]).astype(jnp.int32)
+    gain = norm_gain[0].astype(F32)[:, None]
+
+    def pick(first, second):
+        return jnp.where(mine_first, first, second)
+
+    def section(value):
+        return swap(value, "section", 1)
+
+    def two_layers(keep, send):
+        come = section(send)
+        return pick(keep, come), pick(come, keep)
+
+    def group(value):
+        return jnp.concatenate([value] + peers(value), axis=0)
+
+    def scatter(value):
+        total = value[:length].astype(F32)
+        for d in range(1, n_grp):
+            total = total + swap(value[d * length : (d + 1) * length], "grp", d).astype(F32)
+        return total
+
+    def line(value):
+        return lax.all_gather(value, "dp", axis=0)
+
+    p_sides = two_layers(*cut_small(where, in_weight[0], gain, down_weight[0], kq_weight[0], dt_weight[0],
+                                    conv_weight[0], conv_bias, dt_bias, skip_weight, n_dp, n_grp, sub))
+    p0 = line(p_sides[0])
+    p0_far = section(p0)
+    rows = boundary[0, :, 0]
+    traded = section(pick(rows[1], rows[0]))
+    hidden = pick(rows[0], traded)
+    cotangent = pick(traded, rows[1])
+    lengths = lax.dynamic_index_in_dim(doc_lengths[:, 0], s, 0, keepdims=True)
+    all_lengths = jnp.concatenate([lengths] + peers(lengths), axis=0)
+    masks, valid = slot_masks(all_lengths, length)
+    valid = valid[0][:, None]
+    h0 = hidden.astype(F32)
+    a0_parts = peers((h0 * rms_of(h0)).astype(BF))
+    a0 = jnp.concatenate([(h0 * rms_of(h0)).astype(BF)] + a0_parts, axis=0)
+    q_sides = two_layers(*cut_out(where, in_weight[0], gain, out_weight[0], n_dp, n_grp, sub))
+    q0 = line(after(q_sides[0], p0, a0))
+    q0_far = section(q0)
+    dout1 = cotangent.astype(F32)
+
+    def input_gradient(h, dout, scaled):
+        rms = rms_of(h)
+        own = h * rms
+        return dout + rms * (scaled - own * jnp.mean(scaled * own, axis=1, keepdims=True))
+
+    def summed(grad):
+        return lax.psum_scatter(grad, "dp", scatter_dimension=0, tiled=True)[0]
+
+    def collected(l, near):
+        far = directed(near, "section", [(1 - l, l)])
+        halves = jnp.stack([near, far] if l == 0 else [far, near])
+        out = [halves]
+        for d in range(1, n_grp):
+            pairs = [(l * n_grp + i, l * n_grp + (i ^ d)) for i in range(n_grp)]
+            out.append(directed(halves, ("section", "grp"), pairs))
+        return out
+
+    def gradient_q(a, a_far, dbranch, dbranch_far, gated, gated_far, dgate, dgate_far):
+        return grad_q(a, a_far, dgate, section(dgate_far), gated, section(gated_far), dbranch, dbranch_far, n_dp)
+
+    def gradient_p(a, a_far, dx_near, dx_far, dsmall, ddt, dconv, dvec):
+        small_near, small_far = small_grads(dsmall, ddt, dconv, dvec)
+        return grad_p(a, a_far, dx_near, section(dx_far), small_near, section(small_far), n_dp)
+
+    x0, act0, part0, cat0, wdt0, vec0 = first_products(n_grp, a0, masks, p0, p0_far, n_rows)
+    parts0 = [part0] + peers(part0)
+    dbranch1 = group(after((valid * dout1).astype(BF), *parts0))
+    y0 = rec(parts0, act0, None, wdt0, vec0, masks, True)
+    p1 = line(after(p_sides[1], q0, *parts0))
+    p1_far = section(p1)
+    a0_far = section(after(a0, y0))
+    gate0, gated0_near, gated0_far = gate_product(a0, after(y0, dbranch1), q0, q0_far, n_rows)
+    branch0 = scatter(branch_product(gated0_near, gated0_far, q0, q0_far, n_rows))
+    h1 = (h0 + valid * branch0).astype(BF).astype(F32)
+
+    q1 = line(after(q_sides[1], p1, h1))
+    q1_far = section(q1)
+    a1 = group((h1 * rms_of(h1)).astype(BF))
+    dbranch1_far = section(after(dbranch1, h1))
+    x1, act1, part1, cat1, wdt1, vec1 = first_products(n_grp, a1, masks, p1, p1_far, n_rows)
+    parts1 = [part1] + peers(part1)
+    a1_far = section(after(a1, part1))
+    y1 = rec(parts1, act1, None, wdt1, vec1, masks, True)
+    gate1, gated1_near, gated1_far = gate_product(a1, y1, q1, q1_far, n_rows)
+
+    dy1, dgate1_near, dgate1_far = dgated_product(dbranch1, y1, gate1, q1, q1_far, n_rows)
+    gq1 = gradient_q(a1, a1_far, dbranch1, dbranch1_far, gated1_near, gated1_far, dgate1_near, dgate1_far)
+    sq1 = summed(gq1)
+    branch1 = branch_product(gated1_near, gated1_far, q1, q1_far, n_rows)
+    lr1, dstate1, dpart1, ddt1, dvec1 = rec(parts1, act1, after(dy1, gq1, branch1), wdt1, vec1, masks, False)
+    out1 = h1 + valid * scatter(branch1)
+    dparts1 = [dpart1] + peers(dpart1)
+    dstate1 = after(dstate1, out1)
+    dx1_near, dx1_far, dsmall1, dconv1 = conv_bwd(dparts1, x1, act1, dstate1, masks, vec1, cat1)
+    dnormed1 = dnormed_product(
+        [dx1_near, dx1_far, dgate1_near, dgate1_far], p1, p1_far, q1, q1_far, n_rows)
+    dh1 = input_gradient(h1, dout1, scatter(dnormed1))
+    gp1 = gradient_p(a1, a1_far, after(dx1_near, dnormed1), dx1_far, dsmall1, ddt1, dconv1, dvec1)
+    sp1 = summed(after(gp1, sq1))
+    dout0 = dh1.astype(BF).astype(F32)
+    dbranch0 = group((valid * dout0).astype(BF))
+
+    q_parts1 = collected(1, after(sq1, dbranch0))
+    dbranch0_far = section(dbranch0)
+    dy0, dgate0_near, dgate0_far = dgated_product(after(dbranch0, gp1), y0, gate0, q0, q0_far, n_rows)
+    gq0 = gradient_q(a0, a0_far, dbranch0, dbranch0_far, gated0_near, gated0_far, dgate0_near, dgate0_far)
+    lr0, dstate0, dpart0, ddt0, dvec0 = rec(parts0, act0, after(dy0, gq0, sp1), wdt0, vec0, masks, False)
+    p_parts1 = collected(1, sp1)
+    sq0 = summed(after(gq0, sp1))
+    dparts0 = [dpart0] + peers(dpart0)
+    dstate0 = after(dstate0, *q_parts1, *p_parts1)
+    dx0_near, dx0_far, dsmall0, dconv0 = conv_bwd(dparts0, x0, act0, dstate0, masks, vec0, cat0)
+    gp0 = gradient_p(a0, a0_far, dx0_near, dx0_far, dsmall0, ddt0, dconv0, dvec0)
+    sp0 = summed(after(gp0, sq0))
+    dnormed0 = dnormed_product(
+        [after(dx0_near, gp0), dx0_far, dgate0_near, dgate0_far], p0, p0_far, q0, q0_far, n_rows)
+    dh0 = input_gradient(h0, dout0, scatter(dnormed0))
+    q_parts0, p_parts0 = collected(0, sq0), collected(0, sp0)
+
+    out_far = directed(out1, "section", [(0, 1)])
+    dh_far = directed(dh0, "section", [(1, 0)])
+    result = jnp.stack([pick(dh0, out_far), pick(dh_far, out1)]).reshape(1, 2, 1, length, width)
+
+    grad_in, sum_q, grad_out = join_packed(
+        join_q_body, where, in_weight[0], gain, q_parts0 + q_parts1, None, 1, n_dp, [shape((block, width), F32)])
+    smalls = [shape(v, F32) for v in ((block, RANK), (2 * STATE, block), (RANK, block), (4, block))]
+    smalls += [shape((1, block), F32)] * 3
+    grad_in, sum_p, grad_down, grad_kq, grad_dt, grad_conv, grad_cb, grad_db, grad_skip = join_packed(
+        join_p_body, where, in_weight[0], gain, p_parts0 + p_parts1, grad_in, 0, n_dp, smalls,
+        [pltpu.VMEM((SMALL, block), F32)])
+    grad_gain = jnp.sum(sum_q + sum_p, axis=1)
+    return (
+        result,
+        grad_gain[None],
+        grad_in[None],
+        grad_conv[None],
+        grad_cb,
+        grad_down[None],
+        grad_kq[None],
+        grad_dt[None],
+        grad_db,
+        grad_skip,
+        grad_out[None],
+    )
+
+
 def solution(mesh):
+    packed = mesh.shape["dp"] == 4 and mesh.shape["grp"] == 4
     return jax.shard_map(
-        on_device,
+        on_device if packed else on_any_line,
         mesh=mesh,
         in_specs=(
             P("section", None, ("grp", "dp"), None, None),

time: 1010 us -> 795 us (0.79)
  the two profiles are of different devices: /device:TPU:7 before, /device:TPU:0 now
where the time goes in v3:
time: 795 us; the launch traced here: 785 us
  waiting for transfers between devices  320 us (40%)
  Pallas kernels  278 us (35%)
  starting transfers between devices  93.8 us (12%)
  local copies, waits for them, and re-layouts  46.6 us (6%)
  other arithmetic  31.3 us (4%)
  between operations  15.7 us (2%)
    ppermute x58, waiting for transfers between devices, swap(): lax.ppermute(value, axis, [(i, i ^ shift) for i in range(lax.axis_size(ax...  179 us
    all_gather x4, waiting for transfers between devices, line(): return lax.all_gather(value, 'dp', axis=0)  103 us
    pallas_call x2, Pallas kernels, rec(): call(partial(rec_body, True, keep_y, n_slots, length, width), tuple(outs)...  98.7 us
    pallas_call x10, Pallas kernels, flat_call(): call(body, out_shape, grid=(1,), in_specs=[(specs or {}).get(n, whole(v))...  69.5 us
    ppermute x58, starting transfers between devices, swap(): lax.ppermute(value, axis, [(i, i ^ shift) for i in range(lax.axis_size(ax...  50.5 us
    ppermute x18, starting transfers between devices, directed(): return lax.ppermute(value, axis, pairs)  42.8 us
    unnamed x182, local copies, waits for them, and re-layouts  41.9 us
    ppermute x18, waiting for transfers between devices, directed(): return lax.ppermute(value, axis, pairs)  38.2 us
  transfers between devices with their start and end apart: 84, of which 37 were waited for; matrix products, arithmetic and copies ran while one was open for 5% of the time, Pallas kernels for 34%

profile of v3, /device:TPU:0, one launch (start us, length us, event | category | flops | bytes accessed | tf_op | source)
XLA Modules:
  0.0 785.2 jit_solution(2806304627261593738)
XLA Ops:
  36.7 12.2 %collective-permute-done.6 = bf16[128,2048]{1,0:T(8,128)(2,1)S(1)} collective-permute-done((bf16[128,2048]{1,0:T(8,128)(2,1)S(1)}, bf16[128,2048]{1,0:T(8,128)(2,1)S(1)}, u32[]{:S(2)}, u32[]{:S(2)}) %collective-permute-start.6) | collective-permute-done | bytes 524320 | tf_op jit(solution)/shard_map/ppermute | solution.py:31
  48.9 10.5 %collective-permute-done.5 = bf16[128,2048]{1,0:T(8,128)(2,1)S(1)} collective-permute-done((bf16[128,2048]{1,0:T(8,128)(2,1)S(1)}, bf16[128,2048]{1,0:T(8,128)(2,1)S(1)}, u32[]{:S(2)}, u32[]{:S(2)}) %collective-permute-start.5) | collective-permute-done | bytes 524320 | tf_op jit(solution)/shard_map/ppermute | solution.py:31
  63.9 15.8 %all-gather.9.cloned.1.call-done = bf16[2496,512]{1,0:T(8,128)(2,1)} async-done(((bf16[624,512]{1,0:T(8,128)(2,1)}), bf16[2496,512]{1,0:T(8,128)(2,1)}) %all-gather.9.cloned.1.call-update) | async-done | bytes 2555920 | tf_op jit(solution)/shard_map/all_gather | solution.py:1253
  85.0 7.8 shard_map.204
  114.7 46.8 %all-gather.11.cloned.1.call-done = bf16[4096,512]{1,0:T(8,128)(2,1)} async-done(((bf16[1024,512]{1,0:T(8,128)(2,1)}), bf16[4096,512]{1,0:T(8,128)(2,1)}) %all-gather.11.cloned.1.call-update) | async-done | bytes 4194320 | tf_op jit(solution)/shard_map/all_gather | solution.py:1253
  164.3 16.2 %shard_map.205.y_ref = f32[512,1024]{1,0:T(8,128)S(1)} custom-call(bf16[512,256]{1,0:T(8,128)(2,1)S(1)} %get-tuple-element.92.refs_0_, bf16[512,256]{1,0:T(8,128)(2,1)S(1)} %copy-done.35, bf16[512,256]{1,0:T(8,128)(2,1)S(1)} %copy-done.33, bf16[512,256]{1,0:T(8,128)(2,1)S(1)} %collective-permute-done.11.refs_3_, ...), custom_call_target="tpu_custom_call" | custom-call | flops 60000002048 | tf_op jit(solution)/shard_map/pallas_call | solution.py:411
  206.7 11.2 %collective-permute-done.17 = bf16[128,2048]{1,0:T(8,128)(2,1)S(1)} collective-permute-done((bf16[128,2048]{1,0:T(8,128)(2,1)S(1)}, bf16[128,2048]{1,0:T(8,128)(2,1)S(1)}, u32[]{:S(2)}, u32[]{:S(2)}) %collective-permute-start.17) | collective-permute-done | bytes 524320 | tf_op jit(solution)/shard_map/ppermute | solution.py:31
  217.9 11.9 %collective-permute-done.19 = bf16[128,2048]{1,0:T(8,128)(2,1)S(1)} collective-permute-done((bf16[128,2048]{1,0:T(8,128)(2,1)S(1)}, bf16[128,2048]{1,0:T(8,128)(2,1)S(1)}, u32[]{:S(2)}, u32[]{:S(2)}) %collective-permute-start.19) | collective-permute-done | bytes 524320 | tf_op jit(solution)/shard_map/ppermute | solution.py:31
  231.7 9.4 %all-gather.13.cloned.1.call-done = bf16[2496,512]{1,0:T(8,128)(2,1)} async-done(((bf16[624,512]{1,0:T(8,128)(2,1)}), bf16[2496,512]{1,0:T(8,128)(2,1)}) %all-gather.13.cloned.1.call-update) | async-done | bytes 2555920 | tf_op jit(solution)/shard_map/all_gather | solution.py:1253
  245.0 12.2 %collective-permute-done.22 = bf16[128,2048]{1,0:T(8,128)(2,1)S(1)} collective-permute-done((bf16[128,2048]{1,0:T(8,128)(2,1)S(1)}, bf16[128,2048]{1,0:T(8,128)(2,1)S(1)}, u32[]{:S(2)}, u32[]{:S(2)}) %collective-permute-start.22) | collective-permute-done | bytes 524320 | tf_op jit(solution)/shard_map/ppermute | solution.py:31
  257.2 10.8 %collective-permute-done.21 = bf16[128,2048]{1,0:T(8,128)(2,1)S(1)} collective-permute-done((bf16[128,2048]{1,0:T(8,128)(2,1)S(1)}, bf16[128,2048]{1,0:T(8,128)(2,1)S(1)}, u32[]{:S(2)}, u32[]{:S(2)}) %collective-permute-start.21) | collective-permute-done | bytes 524320 | tf_op jit(solution)/shard_map/ppermute | solution.py:31
  291.6 31.1 %all-gather.15.cloned.1.call-done = bf16[4096,512]{1,0:T(8,128)(2,1)} async-done(((bf16[1024,512]{1,0:T(8,128)(2,1)}), bf16[4096,512]{1,0:T(8,128)(2,1)}) %all-gather.15.cloned.1.call-update) | async-done | bytes 4194320 | tf_op jit(solution)/shard_map/all_gather | solution.py:1253
  323.7 17.4 %shard_map.210.y_ref = f32[512,1024]{1,0:T(8,128)S(1)} custom-call(bf16[512,256]{1,0:T(8,128)(2,1)S(1)} %get-tuple-element.104.refs_0_, bf16[512,256]{1,0:T(8,128)(2,1)} %collective-permute-done.24.refs_1_, bf16[512,256]{1,0:T(8,128)(2,1)} %collective-permute-done.25.refs_2_, bf16[512,256]{1,0:T(8,128)(2,1)S(1)} %collective-permute-done.26.refs_3_, ...), custom_call_target="tpu_custom_call" | custom-call | flops 60000002048 | tf_op jit(solution)/shard_map/pallas_call | solution.py:411
  371.4 9.2 %shard_map.213 = bf16[4,1024,512]{2,1,0:T(8,128)(2,1)} custom-call(bf16[512,2048]{1,0:T(8,128)(2,1)} %pad_maximum_fusion.1.a_ref, bf16[512,2048]{1,0:T(8,128)(2,1)} %collective-permute-done.28.a_far, bf16[512,512]{1,0:T(8,128)(2,1)S(1)} %get-tuple-element.112.dg_ref.dg_near, bf16[512,512]{1,0:T(8,128)(2,1)S(1)} %collective-permute-done.29.dg_come, ...), custom_call_target="tpu_custom_call" | custom-call | flops 24000000000 | tf_op jit(solution)/shard_map/pallas_call | solution.py:875
  380.7 49.4 %shard_map.215 = (bf16[512,128]{1,0:T(8,128)(2,1)}, f32[512,1024]{1,0:T(8,128)}, bf16[512,256]{1,0:T(8,128)(2,1)}, f32[128,1024]{1,0:T(8,128)}, f32[8,1024]{1,0:T(8,128)}) custom-call(bf16[512,256]{1,0:T(8,128)(2,1)} %copy-done.36, bf16[512,256]{1,0:T(8,128)(2,1)} %collective-permute-done.24.refs_1_, bf16[512,256]{1,0:T(8,128)(2,1)} %collective-permute-done.25.refs_2_, ...), custom_call_target="tpu_custom_call" | custom-call | flops 165000003584 | tf_op jit(solution)/shard_map/pallas_call | solution.py:439
  444.9 7.8 shard_map.216
  453.9 8.3 %shard_map.217 = bf16[512,2048]{1,0:T(8,128)(2,1)S(1)} custom-call(bf16[512,512]{1,0:T(8,128)(2,1)S(1)} %get-tuple-element.125.dx_near.dx_ref, bf16[512,512]{1,0:T(8,128)(2,1)S(1)} %get-tuple-element.124.dx_far, bf16[512,512]{1,0:T(8,128)(2,1)S(1)} %copy-done.59, bf16[512,512]{1,0:T(8,128)(2,1)S(1)} %copy-done.27, bf16[4,624,512]{2,1,0:T(8,128)(2,1)} %bitcast.114, ...), custom_call_target="tpu_custom_call" | custom-call | flops 24000000000 | tf_op jit(solution)/shard_map/pallas_call | solution.py:661
  471.9 11.3 %collective-permute-done.38 = bf16[128,2048]{1,0:T(8,128)(2,1)S(1)} collective-permute-done((bf16[128,2048]{1,0:T(8,128)(2,1)S(1)}, bf16[128,2048]{1,0:T(8,128)(2,1)S(1)}, u32[]{:S(2)}, u32[]{:S(2)}) %collective-permute-start.38) | collective-permute-done | bytes 524320 | tf_op jit(solution)/shard_map/ppermute | solution.py:31
  483.2 11.4 %collective-permute-done.40 = bf16[128,2048]{1,0:T(8,128)(2,1)S(1)} collective-permute-done((bf16[128,2048]{1,0:T(8,128)(2,1)S(1)}, bf16[128,2048]{1,0:T(8,128)(2,1)S(1)}, u32[]{:S(2)}, u32[]{:S(2)}) %collective-permute-start.40) | collective-permute-done | bytes 524320 | tf_op jit(solution)/shard_map/ppermute | solution.py:31
  503.3 11.8 %collective-permute-done.43 = bf16[128,2048]{1,0:T(8,128)(2,1)S(1)} collective-permute-done((bf16[128,2048]{1,0:T(8,128)(2,1)S(1)}, bf16[128,2048]{1,0:T(8,128)(2,1)S(1)}, u32[]{:S(2)}, u32[]{:S(2)}) %collective-permute-start.43) | collective-permute-done | bytes 524320 | tf_op jit(solution)/shard_map/ppermute | solution.py:31
  526.1 7.9 %shard_map.220 = (f32[512,1024]{1,0:T(8,128)S(1)}, bf16[512,512]{1,0:T(8,128)(2,1)S(1)}, bf16[512,512]{1,0:T(8,128)(2,1)}) custom-call(bf16[512,2048]{1,0:T(8,128)(2,1)} %pad_maximum_fusion.2.d_ref.db_ref, f32[512,1024]{1,0:T(8,128)} %copy-done.47, f32[512,1024]{1,0:T(8,128)} %copy-done.48, bf16[4,1024,512]{2,1,0:T(8,128)(2,1)} %bitcast.102, ...), custom_call_target="tpu_custom_call" | custom-call | flops 17999998976 | tf_op jit(solution)/shard_map/pallas_call | solution.py:661
  543.9 9.0 %shard_map.221 = bf16[4,1024,512]{2,1,0:T(8,128)(2,1)} custom-call(bf16[512,2048]{1,0:T(8,128)(2,1)S(1)} %copy-done.7, bf16[512,2048]{1,0:T(8,128)(2,1)} %collective-permute-done.46.a_far, bf16[512,512]{1,0:T(8,128)(2,1)S(1)} %copy-done.56, bf16[512,512]{1,0:T(8,128)(2,1)} %collective-permute-done.47.dg_come, bf16[512,512]{1,0:T(8,128)(2,1)S(1)} %copy-done.54, ...), custom_call_target="tpu_custom_call" | custom-call | flops 24000000000 | tf_op jit(solution)/shard_map/pallas_call | solution.py:875
  565.4 49.3 %shard_map.222 = (bf16[512,128]{1,0:T(8,128)(2,1)}, f32[512,1024]{1,0:T(8,128)}, bf16[512,256]{1,0:T(8,128)(2,1)}, f32[128,1024]{1,0:T(8,128)}, f32[8,1024]{1,0:T(8,128)}) custom-call(bf16[512,256]{1,0:T(8,128)(2,1)} %copy-done.30, bf16[512,256]{1,0:T(8,128)(2,1)} %copy-done.34, bf16[512,256]{1,0:T(8,128)(2,1)} %copy-done.32, bf16[512,256]{1,0:T(8,128)(2,1)} %copy-done.31, ...), custom_call_target="tpu_custom_call" | custom-call | flops 165000003584 | tf_op jit(solution)/shard_map/pallas_call | solution.py:439
  622.8 7.8 collective-permute-done.51.p2
  632.8 7.6 shard_map.223
  649.9 9.0 %shard_map.226 = bf16[512,2048]{1,0:T(8,128)(2,1)S(1)} custom-call(bf16[512,512]{1,0:T(8,128)(2,1)S(1)} %get-tuple-element.154.dx_ref.dx_near, bf16[512,512]{1,0:T(8,128)(2,1)S(1)} %get-tuple-element.147.dx_far, bf16[512,512]{1,0:T(8,128)(2,1)S(1)} %copy-done.57, bf16[512,512]{1,0:T(8,128)(2,1)} %get-tuple-element.137.dg_far, ...), custom_call_target="tpu_custom_call" | custom-call | flops 24000000000 | tf_op jit(solution)/shard_map/pallas_call | solution.py:661
  666.4 8.8 %collective-permute-done.63 = bf16[128,2048]{1,0:T(8,128)(2,1)S(1)} collective-permute-done((bf16[128,2048]{1,0:T(8,128)(2,1)S(1)}, bf16[128,2048]{1,0:T(8,128)(2,1)S(1)}, u32[]{:S(2)}, u32[]{:S(2)}) %collective-permute-start.63) | collective-permute-done | bytes 524320 | tf_op jit(solution)/shard_map/ppermute | solution.py:31
  675.2 10.9 %collective-permute-done.65 = bf16[128,2048]{1,0:T(8,128)(2,1)S(1)} collective-permute-done((bf16[128,2048]{1,0:T(8,128)(2,1)S(1)}, bf16[128,2048]{1,0:T(8,128)(2,1)S(1)}, u32[]{:S(2)}, u32[]{:S(2)}) %collective-permute-start.65) | collective-permute-done | bytes 524320 | tf_op jit(solution)/shard_map/ppermute | solution.py:31
  721.1 19.0 %collective-permute-done.70.refs_2_ = bf16[2,1024,512]{2,1,0:T(8,128)(2,1)} collective-permute-done((bf16[2,1024,512]{2,1,0:T(8,128)(2,1)S(1)}, bf16[2,1024,512]{2,1,0:T(8,128)(2,1)}, u32[]{:S(2)}, u32[]{:S(2)}) %collective-permute-start.70) | collective-permute-done | bytes 2097184 | tf_op jit(solution)/shard_map/ppermute | solution.py:35
  740.5 13.7 %shard_map.227 = (f32[512,8192]{1,0:T(8,128)}, f32[512,128]{1,0:T(8,128)S(1)}, f32[1024,2048]{1,0:T(8,128)}) custom-call(s32[2]{0:T(128)S(1)} %copy-done.44, bf16[512,8192]{1,0:T(8,128)(2,1)} %bitcast.96, f32[512,1]{1,0:T(8,128)S(1)} %copy-done.21, bf16[2,1024,512]{2,1,0:T(8,128)(2,1)S(1)} %pad_maximum_fusion.4.refs_0_, ...), custom_call_target="tpu_custom_call" | custom-call | flops 24000000000 | tf_op jit(solution)/shard_map/pallas_call | solution.py:978
  754.2 13.2 %collective-permute-done.74.refs_2_ = bf16[2,624,512]{2,1,0:T(8,128)(2,1)S(1)} collective-permute-done((bf16[2,624,512]{2,1,0:T(8,128)(2,1)S(1)}, bf16[2,624,512]{2,1,0:T(8,128)(2,1)S(1)}, u32[]{:S(2)}, u32[]{:S(2)}) %collective-permute-start.74) | collective-permute-done | bytes 1277984 | tf_op jit(solution)/shard_map/ppermute | solution.py:35
  767.8 9.4 %shard_map.228 = (f32[512,8192]{1,0:T(8,128)}, f32[512,128]{1,0:T(8,128)S(1)}, f32[1024,128]{1,0:T(8,128)}, f32[32,1024]{1,0:T(8,128)}, f32[128,1024]{1,0:T(8,12...) custom-call(s32[2]{0:T(128)S(1)} %copy-done.44, ...), custom_call_target="tpu_custom_call", output_to_operand_aliasing={{0}: (11, {})} | custom-call | flops 24000000000 | tf_op jit(solution)/shard_map/pallas_call | solution.py:978
  (401 shorter events, 281.4 us)
Async XLA Ops:
  7.2 72.5 %all-gather.9.cloned.1.call-start = ((), (), s32[]{:S(2)}) async-start(), calls=%async_computation.8 | async-start | bytes 3194880 | tf_op jit(solution)/shard_map/all_gather | solution.py:1253
  24.2 137.2 %all-gather.11.cloned.1.call-start = ((), (), s32[]{:S(2)}) async-start(), calls=%async_computation.9 | async-start | bytes 5242880 | tf_op jit(solution)/shard_map/all_gather | solution.py:1253
  28.9 32.3 %collective-permute-start.15 = (bf16[1024,512]{1,0:T(8,128)(2,1)S(1)}, bf16[1024,512]{1,0:T(8,128)(2,1)}, u32[]{:S(2)}, u32[]{:S(2)}) collective-permute-start(bf16[1024,512]{1,0:T(8,128)(2,1)S(1)} %get-tuple-element.99), channel_id=1, source_target_pairs={{0,16},{16,0},{1,17},{17,1},{2,18},{18,2},{3,19},{19,3},{4,20},{20... | collective-permute-start | bytes 3145736 | tf_op jit(solution)/shard_map/ppermute | solution.py:31
  79.8 161.4 %all-gather.13.cloned.1.call-start = ((), (), s32[]{:S(2)}) async-start(), calls=%async_computation.10 | async-start | bytes 3194880 | tf_op jit(solution)/shard_map/all_gather | solution.py:1253
  111.2 75.5 %collective-permute-start.14 = (bf16[128,2048]{1,0:T(8,128)(2,1)}, bf16[128,2048]{1,0:T(8,128)(2,1)}, u32[]{:S(2)}, u32[]{:S(2)}) collective-permute-start(bf16[128,2048]{1,0:T(8,128)(2,1)} %get-tuple-element.96), channel_id=1, source_target_pairs={{0,12},{4,8},{8,4},{12,0},{1,13},{5,9},{9,5},{13,1},{2,14},{6,10},... | collective-permute-start | bytes 1572872 | tf_op jit(solution)/shard_map/ppermute | solution.py:31
  112.9 71.8 %collective-permute-start.13 = (bf16[128,2048]{1,0:T(8,128)(2,1)}, bf16[128,2048]{1,0:T(8,128)(2,1)}, u32[]{:S(2)}, u32[]{:S(2)}) collective-permute-start(bf16[128,2048]{1,0:T(8,128)(2,1)} %get-tuple-element.96), channel_id=1, source_target_pairs={{0,8},{4,12},{8,0},{12,4},{1,9},{5,13},{9,1},{13,5},{2,10},{6,14},... | collective-permute-start | bytes 1572872 | tf_op jit(solution)/shard_map/ppermute | solution.py:31
  114.0 68.8 %collective-permute-start.12 = (bf16[128,2048]{1,0:T(8,128)(2,1)}, bf16[128,2048]{1,0:T(8,128)(2,1)}, u32[]{:S(2)}, u32[]{:S(2)}) collective-permute-start(bf16[128,2048]{1,0:T(8,128)(2,1)} %get-tuple-element.96), channel_id=1, source_target_pairs={{0,4},{4,0},{8,12},{12,8},{1,5},{5,1},{9,13},{13,9},{2,6},{6,2},{1... | collective-permute-start | bytes 1572872 | tf_op jit(solution)/shard_map/ppermute | solution.py:31
  188.6 134.1 %all-gather.15.cloned.1.call-start = ((), (), s32[]{:S(2)}) async-start(), calls=%async_computation.11 | async-start | bytes 5242880 | tf_op jit(solution)/shard_map/all_gather | solution.py:1253
  241.1 227.0 %reduce-scatter.5.cloned.1.call-start = ((), (), s32[]{:S(2)}) async-start(), calls=%async_computation.4 | async-start | bytes 5242880 | tf_op jit(solution)/shard_map/reduce_scatter | solution.py:1281
  283.2 39.5 %collective-permute-start.25 = (bf16[512,256]{1,0:T(8,128)(2,1)S(1)}, bf16[512,256]{1,0:T(8,128)(2,1)}, u32[]{:S(2)}, u32[]{:S(2)}) collective-permute-start(bf16[512,256]{1,0:T(8,128)(2,1)S(1)} %get-tuple-element.104.refs_0_), channel_id=1, source_target_pairs={{0,8},{4,12},{8,0},{12,4},{1,9},{5,13},{9,1},{13,5},{2,10},{6,14},... | collective-permute-start | bytes 786440 | tf_op jit(solution)/shard_map/ppermute | solution.py:31
  284.4 38.3 %collective-permute-start.24 = (bf16[512,256]{1,0:T(8,128)(2,1)S(1)}, bf16[512,256]{1,0:T(8,128)(2,1)}, u32[]{:S(2)}, u32[]{:S(2)}) collective-permute-start(bf16[512,256]{1,0:T(8,128)(2,1)S(1)} %get-tuple-element.104.refs_0_), channel_id=1, source_target_pairs={{0,4},{4,0},{8,12},{12,8},{1,5},{5,1},{9,13},{13,9},{2,6},{6,2},{1... | collective-permute-start | bytes 786440 | tf_op jit(solution)/shard_map/ppermute | solution.py:31
  285.0 84.4 %collective-permute-start.31 = (bf16[512,2048]{1,0:T(8,128)(2,1)}, bf16[512,2048]{1,0:T(8,128)(2,1)}, u32[]{:S(2)}, u32[]{:S(2)}) collective-permute-start(bf16[512,2048]{1,0:T(8,128)(2,1)} %constant_dynamic-update-slice_fusion.d_ref.db_ref), channel_id=1, source_target_pairs={{0,16},{16,0},{1,17},{17,1},{2,18},{18,2},{3,19},{19,3},{4,20},{20... | collective-permute-start | bytes 6291464 | tf_op jit(solution)/shard_map/ppermute | solution.py:31
  285.0 85.9 %collective-permute-start.28 = (bf16[512,2048]{1,0:T(8,128)(2,1)}, bf16[512,2048]{1,0:T(8,128)(2,1)}, u32[]{:S(2)}, u32[]{:S(2)}) collective-permute-start(bf16[512,2048]{1,0:T(8,128)(2,1)} %pad_maximum_fusion.1.a_ref), channel_id=1, source_target_pairs={{0,16},{16,0},{1,17},{17,1},{2,18},{18,2},{3,19},{19,3},{4,20},{20... | collective-permute-start | bytes 6291464 | tf_op jit(solution)/shard_map/ppermute | solution.py:31
  367.9 65.2 %collective-permute-start.35 = (bf16[128,2048]{1,0:T(8,128)(2,1)}, bf16[128,2048]{1,0:T(8,128)(2,1)}, u32[]{:S(2)}, u32[]{:S(2)}) collective-permute-start(bf16[128,2048]{1,0:T(8,128)(2,1)} %get-tuple-element.227), channel_id=1, source_target_pairs={{0,4},{4,0},{8,12},{12,8},{1,5},{5,1},{9,13},{13,9},{2,6},{6,2},{1... | collective-permute-start | bytes 1572872 | tf_op jit(solution)/shard_map/ppermute | solution.py:31
  369.4 64.3 %collective-permute-start.37 = (bf16[128,2048]{1,0:T(8,128)(2,1)}, bf16[128,2048]{1,0:T(8,128)(2,1)}, u32[]{:S(2)}, u32[]{:S(2)}) collective-permute-start(bf16[128,2048]{1,0:T(8,128)(2,1)} %get-tuple-element.228), channel_id=1, source_target_pairs={{0,12},{4,8},{8,4},{12,0},{1,13},{5,9},{9,5},{13,1},{2,14},{6,10},... | collective-permute-start | bytes 1572872 | tf_op jit(solution)/shard_map/ppermute | solution.py:31
  370.9 62.8 %collective-permute-start.36 = (bf16[128,2048]{1,0:T(8,128)(2,1)}, bf16[128,2048]{1,0:T(8,128)(2,1)}, u32[]{:S(2)}, u32[]{:S(2)}) collective-permute-start(bf16[128,2048]{1,0:T(8,128)(2,1)} %get-tuple-element.229), channel_id=1, source_target_pairs={{0,8},{4,12},{8,0},{12,4},{1,9},{5,13},{9,1},{13,5},{2,10},{6,14},... | collective-permute-start | bytes 1572872 | tf_op jit(solution)/shard_map/ppermute | solution.py:31
  380.6 157.7 %reduce-scatter.7.cloned.1.call-start = ((), (), s32[]{:S(2)}) async-start(), calls=%async_computation.5 | async-start | bytes 3194880 | tf_op jit(solution)/shard_map/reduce_scatter | solution.py:1281
  468.2 180.7 %reduce-scatter.9.cloned.1.call-start = ((), (), s32[]{:S(2)}) async-start(), calls=%async_computation.6 | async-start | bytes 5242880 | tf_op jit(solution)/shard_map/reduce_scatter | solution.py:1281
  502.8 35.5 %collective-permute-start.46 = (bf16[512,2048]{1,0:T(8,128)(2,1)S(1)}, bf16[512,2048]{1,0:T(8,128)(2,1)}, u32[]{:S(2)}, u32[]{:S(2)}) collective-permute-start(bf16[512,2048]{1,0:T(8,128)(2,1)S(1)} %copy-done.6), channel_id=1, source_target_pairs={{0,16},{16,0},{1,17},{17,1},{2,18},{18,2},{3,19},{19,3},{4,20},{20... | collective-permute-start | bytes 6291464 | tf_op jit(solution)/shard_map/ppermute | solution.py:31
  502.8 39.0 %collective-permute-start.48 = (bf16[512,512]{1,0:T(8,128)(2,1)}, bf16[512,512]{1,0:T(8,128)(2,1)}, u32[]{:S(2)}, u32[]{:S(2)}) collective-permute-start(bf16[512,512]{1,0:T(8,128)(2,1)} %get-tuple-element.102.left_far), channel_id=1, source_target_pairs={{0,16},{16,0},{1,17},{17,1},{2,18},{18,2},{3,19},{19,3},{4,20},{20... | collective-permute-start | bytes 1572872 | tf_op jit(solution)/shard_map/ppermute | solution.py:31
  552.9 61.8 %collective-permute-start.55 = (bf16[2,1024,512]{2,1,0:T(8,128)(2,1)}, bf16[2,1024,512]{2,1,0:T(8,128)(2,1)}, u32[]{:S(2)}, u32[]{:S(2)}) collective-permute-start(bf16[2,1024,512]{2,1,0:T(8,128)(2,1)} %pad_maximum_fusion.3.refs_4_), channel_id=1, source_target_pairs={{16,24},{20,28},{24,16},{28,20},{17,25},{21,29},{25,17},{29,21},{1... | collective-permute-start | bytes 6291464 | tf_op jit(solution)/shard_map/ppermute | solution.py:35
  554.9 61.5 %collective-permute-start.54 = (bf16[2,1024,512]{2,1,0:T(8,128)(2,1)}, bf16[2,1024,512]{2,1,0:T(8,128)(2,1)}, u32[]{:S(2)}, u32[]{:S(2)}) collective-permute-start(bf16[2,1024,512]{2,1,0:T(8,128)(2,1)} %pad_maximum_fusion.3.refs_4_), channel_id=1, source_target_pairs={{16,20},{20,16},{24,28},{28,24},{17,21},{21,17},{25,29},{29,25},{1... | collective-permute-start | bytes 6291464 | tf_op jit(solution)/shard_map/ppermute | solution.py:35
  556.9 144.4 %reduce-scatter.11.cloned.1.call-start = ((), (), s32[]{:S(2)}) async-start(), calls=%async_computation.7 | async-start | bytes 3194880 | tf_op jit(solution)/shard_map/reduce_scatter | solution.py:1281
  560.2 56.8 %collective-permute-start.60 = (bf16[2,624,512]{2,1,0:T(8,128)(2,1)}, bf16[2,624,512]{2,1,0:T(8,128)(2,1)}, u32[]{:S(2)}, u32[]{:S(2)}) collective-permute-start(bf16[2,624,512]{2,1,0:T(8,128)(2,1)} %pad_maximum_fusion.5.refs_4_), channel_id=1, source_target_pairs={{16,28},{20,24},{24,20},{28,16},{17,29},{21,25},{25,21},{29,17},{1... | collective-permute-start | bytes 3833864 | tf_op jit(solution)/shard_map/ppermute | solution.py:35
  562.0 56.3 %collective-permute-start.59 = (bf16[2,624,512]{2,1,0:T(8,128)(2,1)}, bf16[2,624,512]{2,1,0:T(8,128)(2,1)}, u32[]{:S(2)}, u32[]{:S(2)}) collective-permute-start(bf16[2,624,512]{2,1,0:T(8,128)(2,1)} %pad_maximum_fusion.5.refs_4_), channel_id=1, source_target_pairs={{16,24},{20,28},{24,16},{28,20},{17,25},{21,29},{25,17},{29,21},{1... | collective-permute-start | bytes 3833864 | tf_op jit(solution)/shard_map/ppermute | solution.py:35
  563.7 54.6 %collective-permute-start.58 = (bf16[2,624,512]{2,1,0:T(8,128)(2,1)}, bf16[2,624,512]{2,1,0:T(8,128)(2,1)}, u32[]{:S(2)}, u32[]{:S(2)}) collective-permute-start(bf16[2,624,512]{2,1,0:T(8,128)(2,1)} %pad_maximum_fusion.5.refs_4_), channel_id=1, source_target_pairs={{16,20},{20,16},{24,28},{28,24},{17,21},{21,17},{25,29},{29,25},{1... | collective-permute-start | bytes 3833864 | tf_op jit(solution)/shard_map/ppermute | solution.py:35
  664.1 33.9 %collective-permute-start.66 = (f32[128,2048]{1,0:T(8,128)S(1)}, f32[128,2048]{1,0:T(8,128)S(1)}, u32[]{:S(2)}, u32[]{:S(2)}) collective-permute-start(f32[128,2048]{1,0:T(8,128)S(1)} %copy-done.74), channel_id=1, source_target_pairs={{0,16},{1,17},{2,18},{3,19},{4,20},{5,21},{6,22},{7,23},{8,24},{9,... | collective-permute-start | bytes 3145736 | tf_op jit(solution)/shard_map/ppermute | solution.py:35
  692.2 47.9 %collective-permute-start.70 = (bf16[2,1024,512]{2,1,0:T(8,128)(2,1)S(1)}, bf16[2,1024,512]{2,1,0:T(8,128)(2,1)}, u32[]{:S(2)}, u32[]{:S(2)}) collective-permute-start(bf16[2,1024,512]{2,1,0:T(8,128)(2,1)S(1)} %pad_maximum_fusion.4.refs_0_), channel_id=1, source_target_pairs={{0,8},{4,12},{8,0},{12,4},{1,9},{5,13},{9,1},{13,5},{2,10},{6,14},... | collective-permute-start | bytes 6291464 | tf_op jit(solution)/shard_map/ppermute | solution.py:35
  695.5 45.0 %collective-permute-start.69 = (bf16[2,1024,512]{2,1,0:T(8,128)(2,1)S(1)}, bf16[2,1024,512]{2,1,0:T(8,128)(2,1)}, u32[]{:S(2)}, u32[]{:S(2)}) collective-permute-start(bf16[2,1024,512]{2,1,0:T(8,128)(2,1)S(1)} %pad_maximum_fusion.4.refs_0_), channel_id=1, source_target_pairs={{0,4},{4,0},{8,12},{12,8},{1,5},{5,1},{9,13},{13,9},{2,6},{6,2},{1... | collective-permute-start | bytes 6291464 | tf_op jit(solution)/shard_map/ppermute | solution.py:35
  708.0 46.2 %collective-permute-start.75 = (bf16[2,624,512]{2,1,0:T(8,128)(2,1)S(1)}, bf16[2,624,512]{2,1,0:T(8,128)(2,1)S(1)}, u32[]{:S(2)}, u32[]{:S(2)}) collective-permute-start(bf16[2,624,512]{2,1,0:T(8,128)(2,1)S(1)} %pad_maximum_fusion.6.refs_0_), channel_id=1, source_target_pairs={{0,12},{4,8},{8,4},{12,0},{1,13},{5,9},{9,5},{13,1},{2,14},{6,10},... | collective-permute-start | bytes 3833864 | tf_op jit(solution)/shard_map/ppermute | solution.py:35
  711.4 56.0 %collective-permute-start.74 = (bf16[2,624,512]{2,1,0:T(8,128)(2,1)S(1)}, bf16[2,624,512]{2,1,0:T(8,128)(2,1)S(1)}, u32[]{:S(2)}, u32[]{:S(2)}) collective-permute-start(bf16[2,624,512]{2,1,0:T(8,128)(2,1)S(1)} %pad_maximum_fusion.6.refs_0_), channel_id=1, source_target_pairs={{0,8},{4,12},{8,0},{12,4},{1,9},{5,13},{9,1},{13,5},{2,10},{6,14},... | collective-permute-start | bytes 3833864 | tf_op jit(solution)/shard_map/ppermute | solution.py:35
  717.8 50.0 %collective-permute-start.73 = (bf16[2,624,512]{2,1,0:T(8,128)(2,1)S(1)}, bf16[2,624,512]{2,1,0:T(8,128)(2,1)S(1)}, u32[]{:S(2)}, u32[]{:S(2)}) collective-permute-start(bf16[2,624,512]{2,1,0:T(8,128)(2,1)S(1)} %pad_maximum_fusion.6.refs_0_), channel_id=1, source_target_pairs={{0,4},{4,0},{8,12},{12,8},{1,5},{5,1},{9,13},{13,9},{2,6},{6,2},{1... | collective-permute-start | bytes 3833864 | tf_op jit(solution)/shard_map/ppermute | solution.py:35
  (141 other events, 2688.9 us)
Sparse Core Ops, SparseCore 0:
  24.3 55.3 all-gather.8
  81.9 79.5 all-gather.10
  188.7 52.4 all-gather.12
  243.1 79.5 all-gather.14
  380.7 75.2 reduce-scatter.4
  468.3 48.8 reduce-scatter.6
  557.0 74.3 reduce-scatter.8
  649.1 48.6 reduce-scatter.10

commit v4 on v3

--- a/solution.py
+++ b/solution.py
@@ -50,7 +50,7 @@
 
 
 def cost(flops):
-    return pl.CostEstimate(flops=int(3 * flops), bytes_accessed=0, transcendentals=0)
+    return pl.CostEstimate(flops=int(1 * flops), bytes_accessed=0, transcendentals=0)
 
 
 def shape(dims, kind):
@@ -208,7 +208,7 @@
         (inner, dy_ref, wdt, vec, mask, lr_out, dstate_out, dpart_out, ddt_out, dvec_out), refs = refs[:10], refs[10:]
         if keep_y:
             y_out, refs = refs[0], refs[1:]
-        (kq_n, kq_i, c_i, lr_n, step_i, p_i, y_i, kb, str_n, hist, dy_i, a_i, b_i, h_scr, dkq_i,
+        (kq_n, kq_i, c_i, lr_n, step_i, p_i, y_i, kb, str_n, hist, dy_i, a_i, h_scr, dkq_i,
          dlr_n, corr_n, prod, drate_n) = refs
     else:
         (inner, wdt, vec, mask, y_out, kq_n, kq_i, c_i, lr_n, step_i, p_i, y_i, kb, state) = refs
@@ -293,7 +293,7 @@
                 y_i[b, now, :] = ys[b]
         return carry
 
-    lax.fori_loop(0, length, forward_step, 0)
+    lax.fori_loop(0, length, forward_step, 0, unroll=2)
 
     if y_out is not None:
         for j in range(n_slots):
@@ -305,9 +305,9 @@
 
     h_scr[...] = jnp.zeros(h_scr.shape, F32)
 
-    def backward_step(start, i, carry):
+    def backward_step(i, carry):
         t = length - 1 - i
-        at = pl.ds(pl.multiple_of((piece - 1 - (i - start)) * 2 * ROWS, 2 * ROWS), 2 * ROWS)
+        at = pl.ds(pl.multiple_of(t * 2 * ROWS, 2 * ROWS), 2 * ROWS)
         now = pl.ds(pl.multiple_of(t * ROWS, ROWS), ROWS)
         c = c_i[now, :]
         steps = [step_i[b, now, :] for b in range(nb)]
@@ -335,16 +335,14 @@
             prod[at, n * LANES : (n + 1) * LANES] = jnp.concatenate([dk, dq], axis=0).astype(BF)
         for b in range(nb):
             a_i[b, now, :] = a_sum[b]
-            b_i[b, now, :] = b_sum[b]
+            p_i[b, now, :] = b_sum[b]
         return carry
 
-    piece = prod.shape[0] // (2 * ROWS)
+    lax.fori_loop(0, length, backward_step, 0, unroll=2)
+
     source = lax.broadcasted_iota(jnp.int32, (STATE * LANES, LANES), 0) // LANES
     sums = jnp.where(source == lax.broadcasted_iota(jnp.int32, (STATE * LANES, LANES), 1), 1.0, 0.0).astype(BF)
-    for part in range(length // piece):
-        lax.fori_loop(part * piece, (part + 1) * piece, partial(backward_step, part * piece), 0)
-        at = pl.ds((length - (part + 1) * piece) * 2 * ROWS, prod.shape[0])
-        dkq_i[at, :] = dkq_i[at, :] + dot(prod[...], sums, 1, 0)
+    dkq_i[...] = dkq_i[...] + dot(prod[...], sums, 1, 0)
 
     ddt = [jnp.zeros((1, LANES), F32) for _ in pieces]
     dskip = [jnp.zeros((1, LANES), F32) for _ in pieces]
@@ -357,7 +355,7 @@
             at = spread(j, hh)
             inn = inner[rows, cols].astype(F32)
             a, step, dy = a_i[b, at, :], step_i[b, at, :], dy_ref[rows, cols]
-            dstep = inn * a - b_i[b, at, :]
+            dstep = inn * a - p_i[b, at, :]
             strength = str_n[rows, cols]
             inv = 1.0 / (1.0 + strength * ks)
             drate = (dstep * (inv * inv) * (strength * (1.0 - strength))).astype(BF)
@@ -404,7 +402,8 @@
     row = pltpu.VMEM((rows, LANES), F32)
     spread = pltpu.VMEM((ROWS * length, LANES), F32)
     y_like = shape((rows, channels), F32)
-    scratch = [row, spread, spread, pltpu.VMEM((rows, RANK), BF), wide, wide, wide]
+    y_scratch = wide if dy is None or keep_y else pltpu.VMEM((ROWS, LANES), F32)
+    scratch = [row, spread, spread, pltpu.VMEM((rows, RANK), BF), wide, wide, y_scratch]
     scratch += [pltpu.VMEM((2 * STATE, ROWS * length, LANES), F32)]
     if dy is None:
         scratch += [pltpu.VMEM((STATE * nb, ROWS, LANES), F32)]
@@ -412,7 +411,7 @@
             partial(rec_body, False, True, n_slots, length, width),
             y_like,
             grid=(2,),
-            in_specs=[whole(p) for p in parts] + [block(rows), block(RANK), block(vec.shape[0]), whole(masks)],
+            in_specs=[whole(p) for p in parts] + [block(rows), block(RANK), block(vec.shape[0]), pl.BlockSpec((rows, LANES), lambda i: (0, 0))],
             out_specs=block(rows),
             scratch_shapes=scratch,
             cost_estimate=cost(20e9),
@@ -422,12 +421,11 @@
         pltpu.VMEM((length + 1, STATE * nb, ROWS, LANES), F32),
         wide,
         wide,
-        wide,
         pltpu.VMEM((STATE * nb, ROWS, LANES), F32),
         pltpu.VMEM((2 * ROWS * length, LANES), F32),
         pltpu.VMEM((rows, RANK), F32),
         row,
-        pltpu.VMEM((4 * ROWS * ROWS * 2, STATE * LANES), BF),
+        pltpu.VMEM((2 * ROWS * length, STATE * LANES), BF),
         pltpu.VMEM((rows, width), BF),
     ]
     lr_like = shape((rows, RANK), BF)
@@ -440,7 +438,7 @@
         partial(rec_body, True, keep_y, n_slots, length, width),
         tuple(outs),
         grid=(2,),
-        in_specs=[whole(p) for p in parts] + [block(rows), block(rows), block(RANK), block(vec.shape[0]), whole(masks)],
+        in_specs=[whole(p) for p in parts] + [block(rows), block(rows), block(RANK), block(vec.shape[0]), pl.BlockSpec((rows, LANES), lambda i: (0, 0))],
         out_specs=tuple(specs),
         scratch_shapes=scratch,
         cost_estimate=cost(55e9),
@@ -1245,9 +1243,10 @@
 
     def scatter(value):
         total = value[:length].astype(F32)
-        for d in range(1, n_grp):
-            total = total + swap(value[d * length : (d + 1) * length], "grp", d).astype(F32)
-        return total
+        come = [swap(value[d * length : (d + 1) * length], "grp", d) for d in range(1, n_grp)]
+        for piece in come:
+            total = total + piece.astype(F32)
+        return total, come
 
     def line(value):
         return lax.all_gather(value, "dp", axis=0)
@@ -1255,7 +1254,6 @@
     p_sides = two_layers(*cut_small(where, in_weight[0], gain, down_weight[0], kq_weight[0], dt_weight[0],
                                     conv_weight[0], conv_bias, dt_bias, skip_weight, n_dp, n_grp, sub))
     p0 = line(p_sides[0])
-    p0_far = section(p0)
     rows = boundary[0, :, 0]
     traded = section(pick(rows[1], rows[0]))
     hidden = pick(rows[0], traded)
@@ -1268,8 +1266,8 @@
     a0_parts = peers((h0 * rms_of(h0)).astype(BF))
     a0 = jnp.concatenate([(h0 * rms_of(h0)).astype(BF)] + a0_parts, axis=0)
     q_sides = two_layers(*cut_out(where, in_weight[0], gain, out_weight[0], n_dp, n_grp, sub))
+    p0_far = section(after(p0, q_sides[0], *a0_parts))
     q0 = line(after(q_sides[0], p0, a0))
-    q0_far = section(q0)
     dout1 = cotangent.astype(F32)
 
     def input_gradient(h, dout, scaled):
@@ -1298,23 +1296,24 @@
 
     x0, act0, part0, cat0, wdt0, vec0 = first_products(n_grp, a0, masks, p0, p0_far, n_rows)
     parts0 = [part0] + peers(part0)
-    dbranch1 = group(after((valid * dout1).astype(BF), *parts0))
     y0 = rec(parts0, act0, None, wdt0, vec0, masks, True)
-    p1 = line(after(p_sides[1], q0, *parts0))
-    p1_far = section(p1)
+    dbranch1 = group(after((valid * dout1).astype(BF), y0))
+    q0_far = section(after(q0, dbranch1))
+    p1 = line(after(p_sides[1], q0, dbranch1))
     a0_far = section(after(a0, y0))
-    gate0, gated0_near, gated0_far = gate_product(a0, after(y0, dbranch1), q0, q0_far, n_rows)
-    branch0 = scatter(branch_product(gated0_near, gated0_far, q0, q0_far, n_rows))
+    gate0, gated0_near, gated0_far = gate_product(a0, y0, q0, q0_far, n_rows)
+    branch0 = scatter(branch_product(gated0_near, gated0_far, q0, q0_far, n_rows))[0]
     h1 = (h0 + valid * branch0).astype(BF).astype(F32)
 
+    p1_far = section(after(p1, h1))
     q1 = line(after(q_sides[1], p1, h1))
-    q1_far = section(q1)
     a1 = group((h1 * rms_of(h1)).astype(BF))
-    dbranch1_far = section(after(dbranch1, h1))
     x1, act1, part1, cat1, wdt1, vec1 = first_products(n_grp, a1, masks, p1, p1_far, n_rows)
     parts1 = [part1] + peers(part1)
     a1_far = section(after(a1, part1))
     y1 = rec(parts1, act1, None, wdt1, vec1, masks, True)
+    q1_far = section(after(q1, y1))
+    dbranch1_far = section(after(dbranch1, y1))
     gate1, gated1_near, gated1_far = gate_product(a1, y1, q1, q1_far, n_rows)
 
     dy1, dgate1_near, dgate1_far = dgated_product(dbranch1, y1, gate1, q1, q1_far, n_rows)
@@ -1322,14 +1321,15 @@
     sq1 = summed(gq1)
     branch1 = branch_product(gated1_near, gated1_far, q1, q1_far, n_rows)
     lr1, dstate1, dpart1, ddt1, dvec1 = rec(parts1, act1, after(dy1, gq1, branch1), wdt1, vec1, masks, False)
-    out1 = h1 + valid * scatter(branch1)
+    out1 = h1 + valid * scatter(branch1)[0]
     dparts1 = [dpart1] + peers(dpart1)
     dstate1 = after(dstate1, out1)
     dx1_near, dx1_far, dsmall1, dconv1 = conv_bwd(dparts1, x1, act1, dstate1, masks, vec1, cat1)
     dnormed1 = dnormed_product(
         [dx1_near, dx1_far, dgate1_near, dgate1_far], p1, p1_far, q1, q1_far, n_rows)
-    dh1 = input_gradient(h1, dout1, scatter(dnormed1))
-    gp1 = gradient_p(a1, a1_far, after(dx1_near, dnormed1), dx1_far, dsmall1, ddt1, dconv1, dvec1)
+    scaled1, come1 = scatter(dnormed1)
+    dh1 = input_gradient(h1, dout1, scaled1)
+    gp1 = gradient_p(a1, a1_far, after(dx1_near, come1[0]), dx1_far, dsmall1, ddt1, dconv1, dvec1)
     sp1 = summed(after(gp1, sq1))
     dout0 = dh1.astype(BF).astype(F32)
     dbranch0 = group((valid * dout0).astype(BF))
@@ -1346,10 +1346,11 @@
     dx0_near, dx0_far, dsmall0, dconv0 = conv_bwd(dparts0, x0, act0, dstate0, masks, vec0, cat0)
     gp0 = gradient_p(a0, a0_far, dx0_near, dx0_far, dsmall0, ddt0, dconv0, dvec0)
     sp0 = summed(after(gp0, sq0))
+    q_parts0 = collected(0, sq0)
     dnormed0 = dnormed_product(
         [after(dx0_near, gp0), dx0_far, dgate0_near, dgate0_far], p0, p0_far, q0, q0_far, n_rows)
-    dh0 = input_gradient(h0, dout0, scatter(dnormed0))
-    q_parts0, p_parts0 = collected(0, sq0), collected(0, sp0)
+    p_parts0 = collected(0, after(sp0, dnormed0, *q_parts0))
+    dh0 = input_gradient(h0, dout0, after(scatter(dnormed0)[0], p_parts0[0]))
 
     out_far = directed(out1, "section", [(0, 1)])
     dh_far = directed(dh0, "section", [(1, 0)])

time: 795 us -> 752 us (0.946)
  waiting for transfers between devices: 320 us -> 291 us
  Pallas kernels: 278 us -> 261 us
    all_gather x4, waiting for transfers between devices: 103 us -> 36 us  [line(): return lax.all_gather(value, 'dp', axis=0)]
    ppermute x58, waiting for transfers between devices: 179 us -> 202 us  [swap(): lax.ppermute(value, axis, [(i, i ^ shift) for i in range(lax.axis_size(ax...]
    ppermute x18, waiting for transfers between devices: 38.2 us -> 53.7 us  [directed(): return lax.ppermute(value, axis, pairs)]
    unnamed x182 -> x216, local copies, waits for them, and re-layouts: 41.9 us -> 44.8 us
  transfers between devices with their start and end apart: 84 -> 84, of which waited for: 37 -> 40; matrix products, arithmetic and copies ran while one was open for 5% -> 5% of each run, Pallas kernels for 34% -> 32%
where the time goes in v4:
time: 752 us; the launch traced here: 743 us
  waiting for transfers between devices  291 us (39%)
  Pallas kernels  261 us (35%)
  starting transfers between devices  92.9 us (12%)
  local copies, waits for them, and re-layouts  50.3 us (7%)
  other arithmetic  30.7 us (4%)
  between operations  15.8 us (2%)
    ppermute x58, waiting for transfers between devices, swap(): lax.ppermute(value, axis, [(i, i ^ shift) for i in range(lax.axis_size(ax...  202 us
    pallas_call x2, Pallas kernels, rec(): call(partial(rec_body, True, keep_y, n_slots, length, width), tuple(outs)...  90.9 us
    pallas_call x10, Pallas kernels, flat_call(): call(body, out_shape, grid=(1,), in_specs=[(specs or {}).get(n, whole(v))...  65.8 us
    ppermute x18, waiting for transfers between devices, directed(): return lax.ppermute(value, axis, pairs)  53.7 us
    ppermute x58, starting transfers between devices, swap(): lax.ppermute(value, axis, [(i, i ^ shift) for i in range(lax.axis_size(ax...  49.5 us
    unnamed x216, local copies, waits for them, and re-layouts  44.8 us
    ppermute x18, starting transfers between devices, directed(): return lax.ppermute(value, axis, pairs)  42.8 us
    all_gather x4, waiting for transfers between devices, line(): return lax.all_gather(value, 'dp', axis=0)  36 us
  transfers between devices with their start and end apart: 84, of which 40 were waited for; matrix products, arithmetic and copies ran while one was open for 5% of the time, Pallas kernels for 32%

profile of v4, /device:TPU:0, one launch (start us, length us, event | category | flops | bytes accessed | tf_op | source)
XLA Modules:
  0.0 742.5 jit_solution(15746204844946957009)
XLA Ops:
  41.2 9.5 %collective-permute-done.6 = bf16[128,2048]{1,0:T(8,128)(2,1)S(1)} collective-permute-done((bf16[128,2048]{1,0:T(8,128)(2,1)S(1)}, bf16[128,2048]{1,0:T(8,128)(2,1)S(1)}, u32[]{:S(2)}, u32[]{:S(2)}) %collective-permute-start.6) | collective-permute-done | bytes 524320 | tf_op jit(solution)/shard_map/ppermute | solution.py:31
  50.6 10.5 %collective-permute-done.5 = bf16[128,2048]{1,0:T(8,128)(2,1)S(1)} collective-permute-done((bf16[128,2048]{1,0:T(8,128)(2,1)S(1)}, bf16[128,2048]{1,0:T(8,128)(2,1)S(1)}, u32[]{:S(2)}, u32[]{:S(2)}) %collective-permute-start.5) | collective-permute-done | bytes 524320 | tf_op jit(solution)/shard_map/ppermute | solution.py:31
  62.0 16.3 %all-gather.9.cloned.1.call-done = bf16[2496,512]{1,0:T(8,128)(2,1)} async-done(((bf16[624,512]{1,0:T(8,128)(2,1)}), bf16[2496,512]{1,0:T(8,128)(2,1)}) %all-gather.9.cloned.1.call-update) | async-done | bytes 2555920 | tf_op jit(solution)/shard_map/all_gather | solution.py:1252
  83.4 7.5 %shard_map.205 = (f32[512,1024]{1,0:T(8,128)S(1)}, bf16[512,1024]{1,0:T(8,128)(2,1)S(1)}, bf16[512,256]{1,0:T(8,128)(2,1)S(1)}, bf16[256,1024]{1,0:T(8,128)(2,1)...) custom-call(bf16[512,2048]{1,0:T(8,128)(2,1)} %pad_maximum_fusion.a_ref, f32[512,512]{1,0:T(8,128)S(1)} %bitcast.68, ...), custom_call_target="tpu_custom_call" | custom-call | flops 8000000000 | tf_op jit(solution)/shard_map/pallas_call | solution.py:659
  108.1 15.0 %shard_map.206.y_ref = f32[512,1024]{1,0:T(8,128)S(1)} custom-call(bf16[512,256]{1,0:T(8,128)(2,1)S(1)} %get-tuple-element.100.refs_0_, bf16[512,256]{1,0:T(8,128)(2,1)S(1)} %collective-permute-done.10.refs_1_, bf16[512,256]{1,0:T(8,128)(2,1)S(1)} %collective-permute-done.11.refs_2_, bf16[512,256]{1,0:T(8,128)(2,1)S(1)} %collective-permute-done.12.refs_3_, ...), custom_call_target="tpu_custom_call" | custom-call | flops 20000000000 | tf_op jit(solution)/shard_map/pallas_call | solution.py:410
  128.9 10.5 %collective-permute-done.13 = bf16[128,2048]{1,0:T(8,128)(2,1)S(1)} collective-permute-done((bf16[128,2048]{1,0:T(8,128)(2,1)S(1)}, bf16[128,2048]{1,0:T(8,128)(2,1)S(1)}, u32[]{:S(2)}, u32[]{:S(2)}) %collective-permute-start.13) | collective-permute-done | bytes 524320 | tf_op jit(solution)/shard_map/ppermute | solution.py:31
  140.2 10.7 %collective-permute-done.14 = bf16[128,2048]{1,0:T(8,128)(2,1)S(1)} collective-permute-done((bf16[128,2048]{1,0:T(8,128)(2,1)S(1)}, bf16[128,2048]{1,0:T(8,128)(2,1)S(1)}, u32[]{:S(2)}, u32[]{:S(2)}) %collective-permute-start.14) | collective-permute-done | bytes 524320 | tf_op jit(solution)/shard_map/ppermute | solution.py:31
  152.6 8.7 %all-gather.11.cloned.1.call-done = bf16[4096,512]{1,0:T(8,128)(2,1)} async-done(((bf16[1024,512]{1,0:T(8,128)(2,1)}), bf16[4096,512]{1,0:T(8,128)(2,1)}) %all-gather.11.cloned.1.call-update) | async-done | bytes 4194320 | tf_op jit(solution)/shard_map/all_gather | solution.py:1252
  186.0 11.3 %collective-permute-done.17 = bf16[128,2048]{1,0:T(8,128)(2,1)S(1)} collective-permute-done((bf16[128,2048]{1,0:T(8,128)(2,1)S(1)}, bf16[128,2048]{1,0:T(8,128)(2,1)S(1)}, u32[]{:S(2)}, u32[]{:S(2)}) %collective-permute-start.17) | collective-permute-done | bytes 524320 | tf_op jit(solution)/shard_map/ppermute | solution.py:31
  197.2 11.6 %collective-permute-done.19 = bf16[128,2048]{1,0:T(8,128)(2,1)S(1)} collective-permute-done((bf16[128,2048]{1,0:T(8,128)(2,1)S(1)}, bf16[128,2048]{1,0:T(8,128)(2,1)S(1)}, u32[]{:S(2)}, u32[]{:S(2)}) %collective-permute-start.19) | collective-permute-done | bytes 524320 | tf_op jit(solution)/shard_map/ppermute | solution.py:31
  219.0 12.2 %collective-permute-done.22 = bf16[128,2048]{1,0:T(8,128)(2,1)S(1)} collective-permute-done((bf16[128,2048]{1,0:T(8,128)(2,1)S(1)}, bf16[128,2048]{1,0:T(8,128)(2,1)S(1)}, u32[]{:S(2)}, u32[]{:S(2)}) %collective-permute-start.22) | collective-permute-done | bytes 524320 | tf_op jit(solution)/shard_map/ppermute | solution.py:31
  231.2 10.8 %collective-permute-done.21 = bf16[128,2048]{1,0:T(8,128)(2,1)S(1)} collective-permute-done((bf16[128,2048]{1,0:T(8,128)(2,1)S(1)}, bf16[128,2048]{1,0:T(8,128)(2,1)S(1)}, u32[]{:S(2)}, u32[]{:S(2)}) %collective-permute-start.21) | collective-permute-done | bytes 524320 | tf_op jit(solution)/shard_map/ppermute | solution.py:31
  245.1 7.5 %shard_map.209 = (f32[512,1024]{1,0:T(8,128)S(1)}, bf16[512,1024]{1,0:T(8,128)(2,1)S(1)}, bf16[512,256]{1,0:T(8,128)(2,1)S(1)}, bf16[256,1024]{1,0:T(8,128)(2,1)...) custom-call(bf16[512,2048]{1,0:T(8,128)(2,1)} %pad_maximum_fusion.1.a_ref, f32[512,512]{1,0:T(8,128)S(1)} %bitcast.70, ...), custom_call_target="tpu_custom_call" | custom-call | flops 8000000000 | tf_op jit(solution)/shard_map/pallas_call | solution.py:659
  269.7 15.2 %shard_map.210.y_ref = f32[512,1024]{1,0:T(8,128)S(1)} custom-call(bf16[512,256]{1,0:T(8,128)(2,1)S(1)} %get-tuple-element.111.refs_0_, bf16[512,256]{1,0:T(8,128)(2,1)S(1)} %collective-permute-done.24.refs_1_, bf16[512,256]{1,0:T(8,128)(2,1)S(1)} %collective-permute-done.25.refs_2_, bf16[512,256]{1,0:T(8,128)(2,1)S(1)} %collective-permute-done.26.refs_3_, ...), custom_call_target="tpu_custom_call" | custom-call | flops 20000000000 | tf_op jit(solution)/shard_map/pallas_call | solution.py:410
  297.2 12.8 %collective-permute-done.27.far_ref.q_far = bf16[4,1024,512]{2,1,0:T(8,128)(2,1)S(1)} collective-permute-done((bf16[4,1024,512]{2,1,0:T(8,128)(2,1)}, bf16[4,1024,512]{2,1,0:T(8,128)(2,1)S(1)}, u32[]{:S(2)}, u32[]{:S(2)}) %collective-permute-start.27) | collective-permute-done | bytes 4194336 | tf_op jit(solution)/shard_map/ppermute | solution.py:31
  335.2 8.8 %shard_map.213 = bf16[4,1024,512]{2,1,0:T(8,128)(2,1)} custom-call(bf16[512,2048]{1,0:T(8,128)(2,1)S(1)} %copy-done.10, bf16[512,2048]{1,0:T(8,128)(2,1)} %copy-done.102, bf16[512,512]{1,0:T(8,128)(2,1)S(1)} %get-tuple-element.120.dg_ref.dg_near, bf16[512,512]{1,0:T(8,128)(2,1)S(1)} %collective-permute-done.29.dg_come, ...), custom_call_target="tpu_custom_call" | custom-call | flops 8000000000 | tf_op jit(solution)/shard_map/pallas_call | solution.py:873
  350.2 45.5 %shard_map.215 = (bf16[512,128]{1,0:T(8,128)(2,1)}, f32[512,1024]{1,0:T(8,128)}, bf16[512,256]{1,0:T(8,128)(2,1)}, f32[128,1024]{1,0:T(8,128)}, f32[8,1024]{1,0:T(8,128)}) custom-call(bf16[512,256]{1,0:T(8,128)(2,1)} %copy-done.52, bf16[512,256]{1,0:T(8,128)(2,1)} %copy-done.55, bf16[512,256]{1,0:T(8,128)(2,1)} %copy-done.54, bf16[512,256]{1,0:T(8,128)(2,1)} %copy-done.53, ...), custom_call_target="tpu_custom_call" | custom-call | flops 54999998464 | tf_op jit(solution)/shard_map/pallas_call | solution.py:437
  410.2 7.8 %shard_map.216 = (bf16[512,512]{1,0:T(8,128)(2,1)S(1)}, bf16[512,512]{1,0:T(8,128)(2,1)S(1)}, f32[256,1024]{1,0:T(8,128)S(1)}, f32[8,1024]{1,0:T(8,128)S(1)}) custom-call(bf16[512,256]{1,0:T(8,128)(2,1)S(1)} %copy-done.26, bf16[512,256]{1,0:T(8,128)(2,1)S(1)} %collective-permute-done.32.p1, bf16[512,256]{1,0:T(8,128)(2,1)S(1)} %collective-permute-done.33.p2, ...), custom_call_target="tpu_custom_call" | custom-call | tf_op jit(solution)/shard_map/pallas_call | solution.py:534
  418.2 8.3 %shard_map.217 = bf16[512,2048]{1,0:T(8,128)(2,1)S(1)} custom-call(bf16[512,512]{1,0:T(8,128)(2,1)S(1)} %get-tuple-element.133.dx_near.dx_ref, bf16[512,512]{1,0:T(8,128)(2,1)S(1)} %get-tuple-element.132.dx_far, bf16[512,512]{1,0:T(8,128)(2,1)S(1)} %copy-done.74, bf16[512,512]{1,0:T(8,128)(2,1)S(1)} %copy-done.41, bf16[4,624,512]{2,1,0:T(8,128)(2,1)} %bitcast.117, ...), custom_call_target="tpu_custom_call" | custom-call | flops 8000000000 | tf_op jit(solution)/shard_map/pallas_call | solution.py:659
  431.5 10.8 %collective-permute-done.38 = bf16[128,2048]{1,0:T(8,128)(2,1)S(1)} collective-permute-done((bf16[128,2048]{1,0:T(8,128)(2,1)S(1)}, bf16[128,2048]{1,0:T(8,128)(2,1)S(1)}, u32[]{:S(2)}, u32[]{:S(2)}) %collective-permute-start.38) | collective-permute-done | bytes 524320 | tf_op jit(solution)/shard_map/ppermute | solution.py:31
  464.7 12.3 %collective-permute-done.43 = bf16[128,2048]{1,0:T(8,128)(2,1)S(1)} collective-permute-done((bf16[128,2048]{1,0:T(8,128)(2,1)S(1)}, bf16[128,2048]{1,0:T(8,128)(2,1)S(1)}, u32[]{:S(2)}, u32[]{:S(2)}) %collective-permute-start.43) | collective-permute-done | bytes 524320 | tf_op jit(solution)/shard_map/ppermute | solution.py:31
  477.0 9.5 %collective-permute-done.42 = bf16[128,2048]{1,0:T(8,128)(2,1)S(1)} collective-permute-done((bf16[128,2048]{1,0:T(8,128)(2,1)S(1)}, bf16[128,2048]{1,0:T(8,128)(2,1)S(1)}, u32[]{:S(2)}, u32[]{:S(2)}) %collective-permute-start.42) | collective-permute-done | bytes 524320 | tf_op jit(solution)/shard_map/ppermute | solution.py:31
  503.3 8.8 %shard_map.221 = bf16[4,1024,512]{2,1,0:T(8,128)(2,1)} custom-call(bf16[512,2048]{1,0:T(8,128)(2,1)S(1)} %copy-done.8, bf16[512,2048]{1,0:T(8,128)(2,1)} %copy-done.101, bf16[512,512]{1,0:T(8,128)(2,1)S(1)} %get-tuple-element.144.dg_ref.dg_near, bf16[512,512]{1,0:T(8,128)(2,1)S(1)} %collective-permute-done.47.dg_come, bf16[512,512]{1,0:T(8,128)(2,1)S(1)} %copy-done.70, ...), custom_call_target="tpu_custom_call" | custom-call | flops 8000000000 | tf_op jit(solution)/shard_map/pallas_call | solution.py:873
  526.9 45.4 %shard_map.222 = (bf16[512,128]{1,0:T(8,128)(2,1)}, f32[512,1024]{1,0:T(8,128)}, bf16[512,256]{1,0:T(8,128)(2,1)}, f32[128,1024]{1,0:T(8,128)}, f32[8,1024]{1,0:T(8,128)}) custom-call(bf16[512,256]{1,0:T(8,128)(2,1)} %copy-done.48, bf16[512,256]{1,0:T(8,128)(2,1)} %copy-done.51, bf16[512,256]{1,0:T(8,128)(2,1)} %copy-done.50, bf16[512,256]{1,0:T(8,128)(2,1)} %copy-done.49, ...), custom_call_target="tpu_custom_call" | custom-call | flops 54999998464 | tf_op jit(solution)/shard_map/pallas_call | solution.py:437
  580.3 8.1 %collective-permute-done.51.p2 = bf16[512,256]{1,0:T(8,128)(2,1)S(1)} collective-permute-done((bf16[512,256]{1,0:T(8,128)(2,1)}, bf16[512,256]{1,0:T(8,128)(2,1)S(1)}, u32[]{:S(2)}, u32[]{:S(2)}) %collective-permute-start.51) | collective-permute-done | bytes 262176 | tf_op jit(solution)/shard_map/ppermute | solution.py:31
  590.6 7.6 %shard_map.223 = (bf16[512,512]{1,0:T(8,128)(2,1)S(1)}, bf16[512,512]{1,0:T(8,128)(2,1)S(1)}, f32[256,1024]{1,0:T(8,128)S(1)}, f32[8,1024]{1,0:T(8,128)S(1)}) custom-call(bf16[512,256]{1,0:T(8,128)(2,1)S(1)} %copy-done.27, bf16[512,256]{1,0:T(8,128)(2,1)S(1)} %collective-permute-done.50.p1, bf16[512,256]{1,0:T(8,128)(2,1)S(1)} %collective-permute-done.51.p2, ...), custom_call_target="tpu_custom_call" | custom-call | tf_op jit(solution)/shard_map/pallas_call | solution.py:534
  622.1 8.3 %shard_map.226 = bf16[512,2048]{1,0:T(8,128)(2,1)S(1)} custom-call(bf16[512,512]{1,0:T(8,128)(2,1)S(1)} %copy-done.43, bf16[512,512]{1,0:T(8,128)(2,1)S(1)} %copy-done.45, bf16[512,512]{1,0:T(8,128)(2,1)S(1)} %copy-done.72, bf16[512,512]{1,0:T(8,128)(2,1)S(1)} %copy-done.39, bf16[4,624,512]{2,1,0:T(8,128)(2,1)} %bitcast.114, ...), custom_call_target="tpu_custom_call" | custom-call | flops 8000000000 | tf_op jit(solution)/shard_map/pallas_call | solution.py:659
  633.7 19.0 %collective-permute-done.69.refs_3_ = bf16[2,1024,512]{2,1,0:T(8,128)(2,1)S(1)} collective-permute-done((bf16[2,1024,512]{2,1,0:T(8,128)(2,1)S(1)}, bf16[2,1024,512]{2,1,0:T(8,128)(2,1)S(1)}, u32[]{:S(2)}, u32[]{:S(2)}) %collective-permute-start.69) | collective-permute-done | bytes 2097184 | tf_op jit(solution)/shard_map/ppermute | solution.py:35
  653.4 21.7 %collective-permute-done.68.refs_2_ = bf16[2,1024,512]{2,1,0:T(8,128)(2,1)S(1)} collective-permute-done((bf16[2,1024,512]{2,1,0:T(8,128)(2,1)S(1)}, bf16[2,1024,512]{2,1,0:T(8,128)(2,1)S(1)}, u32[]{:S(2)}, u32[]{:S(2)}) %collective-permute-start.68) | collective-permute-done | bytes 2097184 | tf_op jit(solution)/shard_map/ppermute | solution.py:35
  700.5 13.1 %shard_map.227 = (f32[512,8192]{1,0:T(8,128)}, f32[512,128]{1,0:T(8,128)S(1)}, f32[1024,2048]{1,0:T(8,128)}) custom-call(s32[2]{0:T(128)S(1)} %copy-done.33, bf16[512,8192]{1,0:T(8,128)(2,1)} %bitcast.82, f32[512,1]{1,0:T(8,128)S(1)} %copy-done.6, bf16[2,1024,512]{2,1,0:T(8,128)(2,1)S(1)} %pad_maximum_fusion.4.refs_0_, bf16[2,1024,512]{2,1,0:T(8,128)(2,1)S(1)} %copy-done.35, ...), custom_call_target="tpu_custom_call" | custom-call | flops 8000000000 | tf_op jit(solution)/shard_map/pallas_call | solution.py:976
  715.3 9.7 %collective-permute-done.74.refs_2_ = bf16[2,624,512]{2,1,0:T(8,128)(2,1)S(1)} collective-permute-done((bf16[2,624,512]{2,1,0:T(8,128)(2,1)S(1)}, bf16[2,624,512]{2,1,0:T(8,128)(2,1)S(1)}, u32[]{:S(2)}, u32[]{:S(2)}) %collective-permute-start.74) | collective-permute-done | bytes 1277984 | tf_op jit(solution)/shard_map/ppermute | solution.py:35
  725.0 9.5 %shard_map.228 = (f32[512,8192]{1,0:T(8,128)}, f32[512,128]{1,0:T(8,128)S(1)}, f32[1024,128]{1,0:T(8,128)}, f32[32,1024]{1,0:T(8,128)}, f32[128,1024]{1,0:T(8,12...) custom-call(s32[2]{0:T(128)S(1)} %copy-done.33, ...), custom_call_target="tpu_custom_call", output_to_operand_aliasing={{0}: (11, {})} | custom-call | flops 8000000000 | tf_op jit(solution)/shard_map/pallas_call | solution.py:976
  (436 shorter events, 302.3 us)
Async XLA Ops:
  7.2 71.1 %all-gather.9.cloned.1.call-start = ((), (), s32[]{:S(2)}) async-start(), calls=%async_computation.8 | async-start | bytes 3194880 | tf_op jit(solution)/shard_map/all_gather | solution.py:1252
  21.8 139.5 %all-gather.11.cloned.1.call-start = ((), (), s32[]{:S(2)}) async-start(), calls=%async_computation.9 | async-start | bytes 5242880 | tf_op jit(solution)/shard_map/all_gather | solution.py:1252
  81.4 133.7 %all-gather.13.cloned.1.call-start = ((), (), s32[]{:S(2)}) async-start(), calls=%async_computation.10 | async-start | bytes 3194880 | tf_op jit(solution)/shard_map/all_gather | solution.py:1252
  126.0 24.9 %collective-permute-start.14 = (bf16[128,2048]{1,0:T(8,128)(2,1)S(1)}, bf16[128,2048]{1,0:T(8,128)(2,1)S(1)}, u32[]{:S(2)}, u32[]{:S(2)}) collective-permute-start(bf16[128,2048]{1,0:T(8,128)(2,1)S(1)} %copy-done.89), channel_id=1, source_target_pairs={{0,8},{4,12},{8,0},{12,4},{1,9},{5,13},{9,1},{13,5},{2,10},{6,14},... | collective-permute-start | bytes 1572872 | tf_op jit(solution)/shard_map/ppermute | solution.py:31
  126.8 24.9 %collective-permute-start.15 = (bf16[128,2048]{1,0:T(8,128)(2,1)S(1)}, bf16[128,2048]{1,0:T(8,128)(2,1)S(1)}, u32[]{:S(2)}, u32[]{:S(2)}) collective-permute-start(bf16[128,2048]{1,0:T(8,128)(2,1)S(1)} %copy-done.89), channel_id=1, source_target_pairs={{0,12},{4,8},{8,4},{12,0},{1,13},{5,9},{9,5},{13,1},{2,14},{6,10},... | collective-permute-start | bytes 1572872 | tf_op jit(solution)/shard_map/ppermute | solution.py:31
  161.3 135.4 %all-gather.15.cloned.1.call-start = ((), (), s32[]{:S(2)}) async-start(), calls=%async_computation.11 | async-start | bytes 5242880 | tf_op jit(solution)/shard_map/all_gather | solution.py:1252
  215.1 232.8 %reduce-scatter.5.cloned.1.call-start = ((), (), s32[]{:S(2)}) async-start(), calls=%async_computation.4 | async-start | bytes 5242880 | tf_op jit(solution)/shard_map/reduce_scatter | solution.py:1279
  215.2 28.4 %collective-permute-start.23 = (bf16[4,624,512]{2,1,0:T(8,128)(2,1)}, bf16[4,624,512]{2,1,0:T(8,128)(2,1)S(1)}, u32[]{:S(2)}, u32[]{:S(2)}) collective-permute-start(bf16[4,624,512]{2,1,0:T(8,128)(2,1)} %bitcast.115), channel_id=1, source_target_pairs={{0,16},{16,0},{1,17},{17,1},{2,18},{18,2},{3,19},{19,3},{4,20},{20... | collective-permute-start | bytes 7667720 | tf_op jit(solution)/shard_map/ppermute | solution.py:31
  296.7 37.1 %collective-permute-start.28 = (bf16[512,2048]{1,0:T(8,128)(2,1)S(1)}, bf16[512,2048]{1,0:T(8,128)(2,1)S(1)}, u32[]{:S(2)}, u32[]{:S(2)}) collective-permute-start(bf16[512,2048]{1,0:T(8,128)(2,1)S(1)} %copy-done.10), channel_id=1, source_target_pairs={{0,16},{16,0},{1,17},{17,1},{2,18},{18,2},{3,19},{19,3},{4,20},{20... | collective-permute-start | bytes 6291464 | tf_op jit(solution)/shard_map/ppermute | solution.py:31
  297.2 36.6 %collective-permute-start.31 = (bf16[512,2048]{1,0:T(8,128)(2,1)}, bf16[512,2048]{1,0:T(8,128)(2,1)}, u32[]{:S(2)}, u32[]{:S(2)}) collective-permute-start(bf16[512,2048]{1,0:T(8,128)(2,1)} %constant_dynamic-update-slice_fusion.d_ref.db_ref), channel_id=1, source_target_pairs={{0,16},{16,0},{1,17},{17,1},{2,18},{18,2},{3,19},{19,3},{4,20},{20... | collective-permute-start | bytes 6291464 | tf_op jit(solution)/shard_map/ppermute | solution.py:31
  344.0 168.1 %reduce-scatter.7.cloned.1.call-start = ((), (), s32[]{:S(2)}) async-start(), calls=%async_computation.5 | async-start | bytes 3194880 | tf_op jit(solution)/shard_map/reduce_scatter | solution.py:1279
  346.7 52.1 %collective-permute-start.35 = (bf16[128,2048]{1,0:T(8,128)(2,1)}, bf16[128,2048]{1,0:T(8,128)(2,1)S(1)}, u32[]{:S(2)}, u32[]{:S(2)}) collective-permute-start(bf16[128,2048]{1,0:T(8,128)(2,1)} %get-tuple-element.237), channel_id=1, source_target_pairs={{0,4},{4,0},{8,12},{12,8},{1,5},{5,1},{9,13},{13,9},{2,6},{6,2},{1... | collective-permute-start | bytes 1572872 | tf_op jit(solution)/shard_map/ppermute | solution.py:31
  348.2 51.1 %collective-permute-start.37 = (bf16[128,2048]{1,0:T(8,128)(2,1)}, bf16[128,2048]{1,0:T(8,128)(2,1)}, u32[]{:S(2)}, u32[]{:S(2)}) collective-permute-start(bf16[128,2048]{1,0:T(8,128)(2,1)} %get-tuple-element.238), channel_id=1, source_target_pairs={{0,12},{4,8},{8,4},{12,0},{1,13},{5,9},{9,5},{13,1},{2,14},{6,10},... | collective-permute-start | bytes 1572872 | tf_op jit(solution)/shard_map/ppermute | solution.py:31
  349.7 49.7 %collective-permute-start.36 = (bf16[128,2048]{1,0:T(8,128)(2,1)S(1)}, bf16[128,2048]{1,0:T(8,128)(2,1)}, u32[]{:S(2)}, u32[]{:S(2)}) collective-permute-start(bf16[128,2048]{1,0:T(8,128)(2,1)S(1)} %get-tuple-element.239), channel_id=1, source_target_pairs={{0,8},{4,12},{8,0},{12,4},{1,9},{5,13},{9,1},{13,5},{2,10},{6,14},... | collective-permute-start | bytes 1572872 | tf_op jit(solution)/shard_map/ppermute | solution.py:31
  430.9 25.5 %collective-permute-start.39 = (bf16[128,2048]{1,0:T(8,128)(2,1)}, bf16[128,2048]{1,0:T(8,128)(2,1)}, u32[]{:S(2)}, u32[]{:S(2)}) collective-permute-start(bf16[128,2048]{1,0:T(8,128)(2,1)} %get-tuple-element.236), channel_id=1, source_target_pairs={{0,8},{4,12},{8,0},{12,4},{1,9},{5,13},{9,1},{13,5},{2,10},{6,14},... | collective-permute-start | bytes 1572872 | tf_op jit(solution)/shard_map/ppermute | solution.py:31
  447.9 158.5 %reduce-scatter.9.cloned.1.call-start = ((), (), s32[]{:S(2)}) async-start(), calls=%async_computation.6 | async-start | bytes 5242880 | tf_op jit(solution)/shard_map/reduce_scatter | solution.py:1279
  464.7 36.6 %collective-permute-start.46 = (bf16[512,2048]{1,0:T(8,128)(2,1)S(1)}, bf16[512,2048]{1,0:T(8,128)(2,1)S(1)}, u32[]{:S(2)}, u32[]{:S(2)}) collective-permute-start(bf16[512,2048]{1,0:T(8,128)(2,1)S(1)} %copy-done.8), channel_id=1, source_target_pairs={{0,16},{16,0},{1,17},{17,1},{2,18},{18,2},{3,19},{19,3},{4,20},{20... | collective-permute-start | bytes 6291464 | tf_op jit(solution)/shard_map/ppermute | solution.py:31
  499.2 25.9 %collective-permute-start.56 = (bf16[2,1024,512]{2,1,0:T(8,128)(2,1)}, bf16[2,1024,512]{2,1,0:T(8,128)(2,1)}, u32[]{:S(2)}, u32[]{:S(2)}) collective-permute-start(bf16[2,1024,512]{2,1,0:T(8,128)(2,1)} %pad_maximum_fusion.3.refs_4_), channel_id=1, source_target_pairs={{16,28},{20,24},{24,20},{28,16},{17,29},{21,25},{25,21},{29,17},{1... | collective-permute-start | bytes 6291464 | tf_op jit(solution)/shard_map/ppermute | solution.py:35
  512.2 165.6 %reduce-scatter.11.cloned.1.call-start = ((), (), s32[]{:S(2)}) async-start(), calls=%async_computation.7 | async-start | bytes 3194880 | tf_op jit(solution)/shard_map/reduce_scatter | solution.py:1279
  516.3 55.9 %collective-permute-start.55 = (bf16[2,1024,512]{2,1,0:T(8,128)(2,1)}, bf16[2,1024,512]{2,1,0:T(8,128)(2,1)}, u32[]{:S(2)}, u32[]{:S(2)}) collective-permute-start(bf16[2,1024,512]{2,1,0:T(8,128)(2,1)} %pad_maximum_fusion.3.refs_4_), channel_id=1, source_target_pairs={{16,24},{20,28},{24,16},{28,20},{17,25},{21,29},{25,17},{29,21},{1... | collective-permute-start | bytes 6291464 | tf_op jit(solution)/shard_map/ppermute | solution.py:35
  518.3 55.4 %collective-permute-start.54 = (bf16[2,1024,512]{2,1,0:T(8,128)(2,1)}, bf16[2,1024,512]{2,1,0:T(8,128)(2,1)}, u32[]{:S(2)}, u32[]{:S(2)}) collective-permute-start(bf16[2,1024,512]{2,1,0:T(8,128)(2,1)} %pad_maximum_fusion.3.refs_4_), channel_id=1, source_target_pairs={{16,20},{20,16},{24,28},{28,24},{17,21},{21,17},{25,29},{29,25},{1... | collective-permute-start | bytes 6291464 | tf_op jit(solution)/shard_map/ppermute | solution.py:35
  521.6 52.8 %collective-permute-start.60 = (bf16[2,624,512]{2,1,0:T(8,128)(2,1)}, bf16[2,624,512]{2,1,0:T(8,128)(2,1)}, u32[]{:S(2)}, u32[]{:S(2)}) collective-permute-start(bf16[2,624,512]{2,1,0:T(8,128)(2,1)} %pad_maximum_fusion.5.refs_4_), channel_id=1, source_target_pairs={{16,28},{20,24},{24,20},{28,16},{17,29},{21,25},{25,21},{29,17},{1... | collective-permute-start | bytes 3833864 | tf_op jit(solution)/shard_map/ppermute | solution.py:35
  523.4 52.3 %collective-permute-start.59 = (bf16[2,624,512]{2,1,0:T(8,128)(2,1)}, bf16[2,624,512]{2,1,0:T(8,128)(2,1)}, u32[]{:S(2)}, u32[]{:S(2)}) collective-permute-start(bf16[2,624,512]{2,1,0:T(8,128)(2,1)} %pad_maximum_fusion.5.refs_4_), channel_id=1, source_target_pairs={{16,24},{20,28},{24,16},{28,20},{17,25},{21,29},{25,17},{29,21},{1... | collective-permute-start | bytes 3833864 | tf_op jit(solution)/shard_map/ppermute | solution.py:35
  525.2 50.6 %collective-permute-start.58 = (bf16[2,624,512]{2,1,0:T(8,128)(2,1)}, bf16[2,624,512]{2,1,0:T(8,128)(2,1)}, u32[]{:S(2)}, u32[]{:S(2)}) collective-permute-start(bf16[2,624,512]{2,1,0:T(8,128)(2,1)} %pad_maximum_fusion.5.refs_4_), channel_id=1, source_target_pairs={{16,20},{20,16},{24,28},{28,24},{17,21},{21,17},{25,29},{29,25},{1... | collective-permute-start | bytes 3833864 | tf_op jit(solution)/shard_map/ppermute | solution.py:35
  612.5 40.3 %collective-permute-start.69 = (bf16[2,1024,512]{2,1,0:T(8,128)(2,1)S(1)}, bf16[2,1024,512]{2,1,0:T(8,128)(2,1)S(1)}, u32[]{:S(2)}, u32[]{:S(2)}) collective-permute-start(bf16[2,1024,512]{2,1,0:T(8,128)(2,1)S(1)} %pad_maximum_fusion.4.refs_0_), channel_id=1, source_target_pairs={{0,12},{4,8},{8,4},{12,0},{1,13},{5,9},{9,5},{13,1},{2,14},{6,10},... | collective-permute-start | bytes 6291464 | tf_op jit(solution)/shard_map/ppermute | solution.py:35
  616.0 59.1 %collective-permute-start.68 = (bf16[2,1024,512]{2,1,0:T(8,128)(2,1)S(1)}, bf16[2,1024,512]{2,1,0:T(8,128)(2,1)S(1)}, u32[]{:S(2)}, u32[]{:S(2)}) collective-permute-start(bf16[2,1024,512]{2,1,0:T(8,128)(2,1)S(1)} %pad_maximum_fusion.4.refs_0_), channel_id=1, source_target_pairs={{0,8},{4,12},{8,0},{12,4},{1,9},{5,13},{9,1},{13,5},{2,10},{6,14},... | collective-permute-start | bytes 6291464 | tf_op jit(solution)/shard_map/ppermute | solution.py:35
  618.5 57.9 %collective-permute-start.67 = (bf16[2,1024,512]{2,1,0:T(8,128)(2,1)S(1)}, bf16[2,1024,512]{2,1,0:T(8,128)(2,1)S(1)}, u32[]{:S(2)}, u32[]{:S(2)}) collective-permute-start(bf16[2,1024,512]{2,1,0:T(8,128)(2,1)S(1)} %pad_maximum_fusion.4.refs_0_), channel_id=1, source_target_pairs={{0,4},{4,0},{8,12},{12,8},{1,5},{5,1},{9,13},{13,9},{2,6},{6,2},{1... | collective-permute-start | bytes 6291464 | tf_op jit(solution)/shard_map/ppermute | solution.py:35
  631.6 50.7 %collective-permute-start.63 = (bf16[128,2048]{1,0:T(8,128)(2,1)}, bf16[128,2048]{1,0:T(8,128)(2,1)}, u32[]{:S(2)}, u32[]{:S(2)}) collective-permute-start(bf16[128,2048]{1,0:T(8,128)(2,1)} %get-tuple-element.231), channel_id=1, source_target_pairs={{0,4},{4,0},{8,12},{12,8},{1,5},{5,1},{9,13},{13,9},{2,6},{6,2},{1... | collective-permute-start | bytes 1572872 | tf_op jit(solution)/shard_map/ppermute | solution.py:31
  632.3 54.3 %collective-permute-start.65 = (bf16[128,2048]{1,0:T(8,128)(2,1)}, bf16[128,2048]{1,0:T(8,128)(2,1)}, u32[]{:S(2)}, u32[]{:S(2)}) collective-permute-start(bf16[128,2048]{1,0:T(8,128)(2,1)} %get-tuple-element.232), channel_id=1, source_target_pairs={{0,12},{4,8},{8,4},{12,0},{1,13},{5,9},{9,5},{13,1},{2,14},{6,10},... | collective-permute-start | bytes 1572872 | tf_op jit(solution)/shard_map/ppermute | solution.py:31
  652.8 33.8 %collective-permute-start.64 = (bf16[128,2048]{1,0:T(8,128)(2,1)}, bf16[128,2048]{1,0:T(8,128)(2,1)}, u32[]{:S(2)}, u32[]{:S(2)}) collective-permute-start(bf16[128,2048]{1,0:T(8,128)(2,1)} %get-tuple-element.233), channel_id=1, source_target_pairs={{0,8},{4,12},{8,0},{12,4},{1,9},{5,13},{9,1},{13,5},{2,10},{6,14},... | collective-permute-start | bytes 1572872 | tf_op jit(solution)/shard_map/ppermute | solution.py:31
  694.7 30.3 %collective-permute-start.74 = (bf16[2,624,512]{2,1,0:T(8,128)(2,1)S(1)}, bf16[2,624,512]{2,1,0:T(8,128)(2,1)S(1)}, u32[]{:S(2)}, u32[]{:S(2)}) collective-permute-start(bf16[2,624,512]{2,1,0:T(8,128)(2,1)S(1)} %pad_maximum_fusion.6.refs_0_), channel_id=1, source_target_pairs={{0,8},{4,12},{8,0},{12,4},{1,9},{5,13},{9,1},{13,5},{2,10},{6,14},... | collective-permute-start | bytes 3833864 | tf_op jit(solution)/shard_map/ppermute | solution.py:35
  697.2 27.8 %collective-permute-start.73 = (bf16[2,624,512]{2,1,0:T(8,128)(2,1)S(1)}, bf16[2,624,512]{2,1,0:T(8,128)(2,1)S(1)}, u32[]{:S(2)}, u32[]{:S(2)}) collective-permute-start(bf16[2,624,512]{2,1,0:T(8,128)(2,1)S(1)} %pad_maximum_fusion.6.refs_0_), channel_id=1, source_target_pairs={{0,4},{4,0},{8,12},{12,8},{1,5},{5,1},{9,13},{13,9},{2,6},{6,2},{1... | collective-permute-start | bytes 3833864 | tf_op jit(solution)/shard_map/ppermute | solution.py:35
  (158 other events, 2224.0 us)
Sparse Core Ops, SparseCore 0:
  21.9 56.3 all-gather.8
  81.5 79.6 all-gather.10
  162.8 52.2 all-gather.12
  217.1 79.5 all-gather.14
  344.2 75.2 reduce-scatter.4
  448.0 49.5 reduce-scatter.6
  512.3 75.8 reduce-scatter.8
  606.6 49.1 reduce-scatter.10

commit v5 on v4

--- a/solution.py
+++ b/solution.py
@@ -382,7 +382,10 @@
             ]
             dkq = dk + pltpu.roll(dq, STATE, axis=1)
             dkq = dkq - jnp.where(lane < STATE, 2.0 * kq_n[rows, :] * corr_n[rows, :], 0.0)
-            dpart_out[rows, :] = pack(dlr_n[rows, :], dkq)
+            dpart_out[rows, :] = dlr_n[rows, :].astype(BF)
+            dkq = jnp.where(lane < 2 * STATE, dkq, 0.0)
+            packed = dkq if j == 0 else packed + pltpu.roll(dkq, 2 * STATE * j, axis=1)
+        dpart_out[n_slots * length :, :] = packed.astype(BF)
 
 
 def rec(parts, inner, dy, wdt, vec, masks, keep_y):
@@ -429,7 +432,7 @@
         pltpu.VMEM((rows, width), BF),
     ]
     lr_like = shape((rows, RANK), BF)
-    part_like = shape((rows, 2 * LANES), BF)
+    part_like = shape((rows + length, LANES), BF)
     outs = [lr_like, y_like, part_like, shape((RANK, channels), F32), shape((ROWS, channels), F32)]
     specs = [whole(lr_like), block(rows), whole(part_like), block(RANK), block(ROWS)]
     if keep_y:
@@ -491,9 +494,12 @@
     kq = jnp.zeros((length, LANES), F32)
     for d, part in enumerate((p0, p1, p2, p3)):
         rows = pl.ds(pl.multiple_of((j ^ d) * length, length), length)
-        low_rank = low_rank + part[rows, :RANK].astype(F32)
-        kq = kq + part[rows, RANK:].astype(F32)
-    kq = kq + pltpu.roll(kq, 64, axis=1)
+        low_rank = low_rank + part[rows, :].astype(F32)
+        packed = part[n_slots * length :, :].astype(F32)
+        mine = packed
+        for n in range(1, n_slots):
+            mine = jnp.where((j ^ d) == n, pltpu.roll(packed, LANES - 2 * STATE * n, axis=1), mine)
+        kq = kq + mine
     dcat[:, :RANK] = low_rank.astype(BF)
     dcat[:, RANK:] = jnp.where(lane < 2 * STATE, kq, 0.0).astype(BF)
     dsmall_out[...] += dot(dcat[...], inner[...], 0, 0)
@@ -609,6 +615,7 @@
             + [pltpu.SemaphoreType.DMA((7,))],
         ),
         cost_estimate=cost(3e9),
+        vmem=62,
     )(where, weight, gain, *smalls)
 
 
@@ -808,21 +815,25 @@
 
 
 def dnormed_body(rows, dx_near, dx_far, dg_near, dg_far, p_near, p_far, q_near, q_far, out_ref):
-    for p in range(p_near.shape[0]):
-        total = dot(dx_near[...], p_near[p, 0:rows, :], 1, 1) + dot(dx_far[...], p_far[p, 0:rows, :], 1, 1)
-        total = total + dot(dg_near[...], q_near[p], 1, 1) + dot(dg_far[...], q_far[p], 1, 1)
-        out_ref[:, p * rows : (p + 1) * rows] = total.astype(BF)
+    total = dot(dx_near[...], p_near[0, 0:rows, :], 1, 1) + dot(dx_far[...], p_far[0, 0:rows, :], 1, 1)
+    total = total + dot(dg_near[...], q_near[0], 1, 1) + dot(dg_far[...], q_far[0], 1, 1)
+    out_ref[...] = total.astype(BF)
 
 
 def dnormed_product(lefts, p_near, p_far, q_near, q_far, rows):
-    n_dp = p_near.shape[0]
-    return flat_call(
+    n_dp, _, half = p_near.shape
+    n = lefts[0].shape[0]
+    left = pl.BlockSpec((n, half), lambda i: (0, 0))
+    p_spec = pl.BlockSpec((1, p_near.shape[1], half), lambda i: (i, 0, 0))
+    q_spec = pl.BlockSpec((1, rows, half), lambda i: (i, 0, 0))
+    return call(
         partial(dnormed_body, rows),
-        shape((lefts[0].shape[0], n_dp * rows), BF),
-        [*lefts, p_near, p_far, q_near, q_far],
-        specs={6: q_block(q_near, 0, rows), 7: q_block(q_far, 0, rows)},
-        flops=8e9,
-    )
+        shape((n, n_dp * rows), BF),
+        grid=(n_dp,),
+        in_specs=[left] * 4 + [p_spec] * 2 + [q_spec] * 2,
+        out_specs=pl.BlockSpec((n, rows), lambda i: (0, i)),
+        cost_estimate=cost(8e9),
+    )(*lefts, p_near, p_far, q_near, q_far)
 
 
 def grad_p_body(a_ref, a_far, dx_ref, dx_come, small_ref, small_come, out_ref):

time: 752 us -> 741 us (0.985)
  waiting for transfers between devices: 291 us -> 283 us
    pallas_call x10 -> x8, Pallas kernels: 65.8 us -> 49.2 us  [flat_call(): call(body, out_shape, grid=(1,), in_specs=[(specs or {}).get(n, whole(v))...]
    pallas_call x0 -> x2, Pallas kernels: none -> 14.5 us  [dnormed_product(): call(partial(dnormed_body, rows), shape((n, n_dp * rows), BF), grid=(n_dp...]
    ppermute x58, waiting for transfers between devices: 202 us -> 192 us  [swap(): lax.ppermute(value, axis, [(i, i ^ shift) for i in range(lax.axis_size(ax...]
    unnamed x216 -> x202, local copies, waits for them, and re-layouts: 44.8 us -> 38.6 us
where the time goes in v5:
time: 741 us; the launch traced here: 731 us
  waiting for transfers between devices  283 us (38%)
  Pallas kernels  261 us (35%)
  starting transfers between devices  95.1 us (13%)
  local copies, waits for them, and re-layouts  44.9 us (6%)
  other arithmetic  30.6 us (4%)
  between operations  15.8 us (2%)
    ppermute x58, waiting for transfers between devices, swap(): lax.ppermute(value, axis, [(i, i ^ shift) for i in range(lax.axis_size(ax...  192 us
    pallas_call x2, Pallas kernels, rec(): call(partial(rec_body, True, keep_y, n_slots, length, width), tuple(outs)...  90.5 us
    ppermute x18, waiting for transfers between devices, directed(): return lax.ppermute(value, axis, pairs)  54.8 us
    ppermute x58, starting transfers between devices, swap(): lax.ppermute(value, axis, [(i, i ^ shift) for i in range(lax.axis_size(ax...  51.3 us
    pallas_call x8, Pallas kernels, flat_call(): call(body, out_shape, grid=(1,), in_specs=[(specs or {}).get(n, whole(v))...  49.2 us
    ppermute x18, starting transfers between devices, directed(): return lax.ppermute(value, axis, pairs)  43.1 us
    unnamed x202, local copies, waits for them, and re-layouts  38.6 us
    all_gather x4, waiting for transfers between devices, line(): return lax.all_gather(value, 'dp', axis=0)  36.7 us
  transfers between devices with their start and end apart: 84, of which 40 were waited for; matrix products, arithmetic and copies ran while one was open for 5% of the time, Pallas kernels for 32%

profile of v5, /device:TPU:0, one launch (start us, length us, event | category | flops | bytes accessed | tf_op | source)
XLA Modules:
  0.0 730.9 jit_solution(15230461731379774751)
XLA Ops:
  38.3 9.5 %collective-permute-done.6 = bf16[128,2048]{1,0:T(8,128)(2,1)S(1)} collective-permute-done((bf16[128,2048]{1,0:T(8,128)(2,1)S(1)}, bf16[128,2048]{1,0:T(8,128)(2,1)S(1)}, u32[]{:S(2)}, u32[]{:S(2)}) %collective-permute-start.6) | collective-permute-done | bytes 524320 | tf_op jit(solution)/shard_map/ppermute | solution.py:31
  47.8 10.5 %collective-permute-done.5 = bf16[128,2048]{1,0:T(8,128)(2,1)S(1)} collective-permute-done((bf16[128,2048]{1,0:T(8,128)(2,1)S(1)}, bf16[128,2048]{1,0:T(8,128)(2,1)S(1)}, u32[]{:S(2)}, u32[]{:S(2)}) %collective-permute-start.5) | collective-permute-done | bytes 524320 | tf_op jit(solution)/shard_map/ppermute | solution.py:31
  59.1 17.0 %all-gather.9.cloned.1.call-done = bf16[2496,512]{1,0:T(8,128)(2,1)} async-done(((bf16[624,512]{1,0:T(8,128)(2,1)}), bf16[2496,512]{1,0:T(8,128)(2,1)}) %all-gather.9.cloned.1.call-update) | async-done | bytes 2555920 | tf_op jit(solution)/shard_map/all_gather | solution.py:1263
  81.3 7.5 %shard_map.205 = (f32[512,1024]{1,0:T(8,128)S(1)}, bf16[512,1024]{1,0:T(8,128)(2,1)S(1)}, bf16[512,256]{1,0:T(8,128)(2,1)S(1)}, bf16[256,1024]{1,0:T(8,128)(2,1)...) custom-call(bf16[512,2048]{1,0:T(8,128)(2,1)} %pad_maximum_fusion.a_ref, f32[512,512]{1,0:T(8,128)S(1)} %bitcast.68, ...), custom_call_target="tpu_custom_call" | custom-call | flops 8000000000 | tf_op jit(solution)/shard_map/pallas_call | solution.py:666
  105.9 15.0 %shard_map.206.y_ref = f32[512,1024]{1,0:T(8,128)S(1)} custom-call(bf16[512,256]{1,0:T(8,128)(2,1)S(1)} %get-tuple-element.100.refs_0_, bf16[512,256]{1,0:T(8,128)(2,1)S(1)} %collective-permute-done.10.refs_1_, bf16[512,256]{1,0:T(8,128)(2,1)S(1)} %collective-permute-done.11.refs_2_, bf16[512,256]{1,0:T(8,128)(2,1)S(1)} %collective-permute-done.12.refs_3_, ...), custom_call_target="tpu_custom_call" | custom-call | flops 20000000000 | tf_op jit(solution)/shard_map/pallas_call | solution.py:413
  126.7 10.5 %collective-permute-done.13 = bf16[128,2048]{1,0:T(8,128)(2,1)S(1)} collective-permute-done((bf16[128,2048]{1,0:T(8,128)(2,1)S(1)}, bf16[128,2048]{1,0:T(8,128)(2,1)S(1)}, u32[]{:S(2)}, u32[]{:S(2)}) %collective-permute-start.13) | collective-permute-done | bytes 524320 | tf_op jit(solution)/shard_map/ppermute | solution.py:31
  138.1 10.7 %collective-permute-done.14 = bf16[128,2048]{1,0:T(8,128)(2,1)S(1)} collective-permute-done((bf16[128,2048]{1,0:T(8,128)(2,1)S(1)}, bf16[128,2048]{1,0:T(8,128)(2,1)S(1)}, u32[]{:S(2)}, u32[]{:S(2)}) %collective-permute-start.14) | collective-permute-done | bytes 524320 | tf_op jit(solution)/shard_map/ppermute | solution.py:31
  150.5 8.7 %all-gather.11.cloned.1.call-done = bf16[4096,512]{1,0:T(8,128)(2,1)} async-done(((bf16[1024,512]{1,0:T(8,128)(2,1)}), bf16[4096,512]{1,0:T(8,128)(2,1)}) %all-gather.11.cloned.1.call-update) | async-done | bytes 4194320 | tf_op jit(solution)/shard_map/all_gather | solution.py:1263
  159.4 7.3 collective-permute-done.16.far_ref.q_far
  183.8 11.3 %collective-permute-done.17 = bf16[128,2048]{1,0:T(8,128)(2,1)S(1)} collective-permute-done((bf16[128,2048]{1,0:T(8,128)(2,1)S(1)}, bf16[128,2048]{1,0:T(8,128)(2,1)S(1)}, u32[]{:S(2)}, u32[]{:S(2)}) %collective-permute-start.17) | collective-permute-done | bytes 524320 | tf_op jit(solution)/shard_map/ppermute | solution.py:31
  195.1 11.6 %collective-permute-done.19 = bf16[128,2048]{1,0:T(8,128)(2,1)S(1)} collective-permute-done((bf16[128,2048]{1,0:T(8,128)(2,1)S(1)}, bf16[128,2048]{1,0:T(8,128)(2,1)S(1)}, u32[]{:S(2)}, u32[]{:S(2)}) %collective-permute-start.19) | collective-permute-done | bytes 524320 | tf_op jit(solution)/shard_map/ppermute | solution.py:31
  216.9 12.2 %collective-permute-done.22 = bf16[128,2048]{1,0:T(8,128)(2,1)S(1)} collective-permute-done((bf16[128,2048]{1,0:T(8,128)(2,1)S(1)}, bf16[128,2048]{1,0:T(8,128)(2,1)S(1)}, u32[]{:S(2)}, u32[]{:S(2)}) %collective-permute-start.22) | collective-permute-done | bytes 524320 | tf_op jit(solution)/shard_map/ppermute | solution.py:31
  229.0 10.8 %collective-permute-done.21 = bf16[128,2048]{1,0:T(8,128)(2,1)S(1)} collective-permute-done((bf16[128,2048]{1,0:T(8,128)(2,1)S(1)}, bf16[128,2048]{1,0:T(8,128)(2,1)S(1)}, u32[]{:S(2)}, u32[]{:S(2)}) %collective-permute-start.21) | collective-permute-done | bytes 524320 | tf_op jit(solution)/shard_map/ppermute | solution.py:31
  243.0 7.5 %shard_map.209 = (f32[512,1024]{1,0:T(8,128)S(1)}, bf16[512,1024]{1,0:T(8,128)(2,1)S(1)}, bf16[512,256]{1,0:T(8,128)(2,1)S(1)}, bf16[256,1024]{1,0:T(8,128)(2,1)...) custom-call(bf16[512,2048]{1,0:T(8,128)(2,1)} %pad_maximum_fusion.1.a_ref, f32[512,512]{1,0:T(8,128)S(1)} %bitcast.70, ...), custom_call_target="tpu_custom_call" | custom-call | flops 8000000000 | tf_op jit(solution)/shard_map/pallas_call | solution.py:666
  267.6 15.2 %shard_map.210.y_ref = f32[512,1024]{1,0:T(8,128)S(1)} custom-call(bf16[512,256]{1,0:T(8,128)(2,1)S(1)} %get-tuple-element.111.refs_0_, bf16[512,256]{1,0:T(8,128)(2,1)S(1)} %collective-permute-done.24.refs_1_, bf16[512,256]{1,0:T(8,128)(2,1)S(1)} %collective-permute-done.25.refs_2_, bf16[512,256]{1,0:T(8,128)(2,1)S(1)} %collective-permute-done.26.refs_3_, ...), custom_call_target="tpu_custom_call" | custom-call | flops 20000000000 | tf_op jit(solution)/shard_map/pallas_call | solution.py:413
  295.1 12.8 %collective-permute-done.27.far_ref.q_far = bf16[4,1024,512]{2,1,0:T(8,128)(2,1)S(1)} collective-permute-done((bf16[4,1024,512]{2,1,0:T(8,128)(2,1)}, bf16[4,1024,512]{2,1,0:T(8,128)(2,1)S(1)}, u32[]{:S(2)}, u32[]{:S(2)}) %collective-permute-start.27) | collective-permute-done | bytes 4194336 | tf_op jit(solution)/shard_map/ppermute | solution.py:31
  332.9 8.8 %shard_map.213 = bf16[4,1024,512]{2,1,0:T(8,128)(2,1)} custom-call(bf16[512,2048]{1,0:T(8,128)(2,1)S(1)} %copy-done.12, bf16[512,2048]{1,0:T(8,128)(2,1)} %copy-done.95, bf16[512,512]{1,0:T(8,128)(2,1)S(1)} %get-tuple-element.120.dg_ref.dg_near, bf16[512,512]{1,0:T(8,128)(2,1)S(1)} %collective-permute-done.29.dg_come, ...), custom_call_target="tpu_custom_call" | custom-call | flops 8000000000 | tf_op jit(solution)/shard_map/pallas_call | solution.py:884
  348.0 45.5 %shard_map.215 = (bf16[512,128]{1,0:T(8,128)(2,1)}, f32[512,1024]{1,0:T(8,128)}, bf16[640,128]{1,0:T(8,128)(2,1)}, f32[128,1024]{1,0:T(8,128)}, f32[8,1024]{1,0:T(8,128)}) custom-call(bf16[512,256]{1,0:T(8,128)(2,1)} %copy-done.50, bf16[512,256]{1,0:T(8,128)(2,1)} %copy-done.53, bf16[512,256]{1,0:T(8,128)(2,1)} %copy-done.52, bf16[512,256]{1,0:T(8,128)(2,1)} %copy-done.51, ...), custom_call_target="tpu_custom_call" | custom-call | flops 54999998464 | tf_op jit(solution)/shard_map/pallas_call | solution.py:440
  403.7 8.0 %shard_map.216 = (bf16[512,512]{1,0:T(8,128)(2,1)S(1)}, bf16[512,512]{1,0:T(8,128)(2,1)S(1)}, f32[256,1024]{1,0:T(8,128)S(1)}, f32[8,1024]{1,0:T(8,128)S(1)}) custom-call(bf16[640,128]{1,0:T(8,128)(2,1)S(1)} %copy-done.26, bf16[640,128]{1,0:T(8,128)(2,1)S(1)} %collective-permute-done.32.p1, bf16[640,128]{1,0:T(8,128)(2,1)S(1)} %collective-permute-done.33.p2, ...), custom_call_target="tpu_custom_call" | custom-call | tf_op jit(solution)/shard_map/pallas_call | solution.py:540
  411.8 7.3 shard_map.217
  424.1 10.8 %collective-permute-done.38 = bf16[128,2048]{1,0:T(8,128)(2,1)S(1)} collective-permute-done((bf16[128,2048]{1,0:T(8,128)(2,1)S(1)}, bf16[128,2048]{1,0:T(8,128)(2,1)S(1)}, u32[]{:S(2)}, u32[]{:S(2)}) %collective-permute-start.38) | collective-permute-done | bytes 524320 | tf_op jit(solution)/shard_map/ppermute | solution.py:31
  457.1 12.3 %collective-permute-done.43 = bf16[128,2048]{1,0:T(8,128)(2,1)S(1)} collective-permute-done((bf16[128,2048]{1,0:T(8,128)(2,1)S(1)}, bf16[128,2048]{1,0:T(8,128)(2,1)S(1)}, u32[]{:S(2)}, u32[]{:S(2)}) %collective-permute-start.43) | collective-permute-done | bytes 524320 | tf_op jit(solution)/shard_map/ppermute | solution.py:31
  469.5 9.3 %collective-permute-done.42 = bf16[128,2048]{1,0:T(8,128)(2,1)S(1)} collective-permute-done((bf16[128,2048]{1,0:T(8,128)(2,1)S(1)}, bf16[128,2048]{1,0:T(8,128)(2,1)S(1)}, u32[]{:S(2)}, u32[]{:S(2)}) %collective-permute-start.42) | collective-permute-done | bytes 524320 | tf_op jit(solution)/shard_map/ppermute | solution.py:31
  495.6 8.8 %shard_map.221 = bf16[4,1024,512]{2,1,0:T(8,128)(2,1)} custom-call(bf16[512,2048]{1,0:T(8,128)(2,1)S(1)} %copy-done.10, bf16[512,2048]{1,0:T(8,128)(2,1)} %copy-done.94, bf16[512,512]{1,0:T(8,128)(2,1)S(1)} %get-tuple-element.144.dg_ref.dg_near, bf16[512,512]{1,0:T(8,128)(2,1)S(1)} %collective-permute-done.47.dg_come, bf16[512,512]{1,0:T(8,128)(2,1)S(1)} %copy-done.63, ...), custom_call_target="tpu_custom_call" | custom-call | flops 8000000000 | tf_op jit(solution)/shard_map/pallas_call | solution.py:884
  519.5 45.1 %shard_map.222 = (bf16[512,128]{1,0:T(8,128)(2,1)}, f32[512,1024]{1,0:T(8,128)}, bf16[640,128]{1,0:T(8,128)(2,1)}, f32[128,1024]{1,0:T(8,128)}, f32[8,1024]{1,0:T(8,128)}) custom-call(bf16[512,256]{1,0:T(8,128)(2,1)} %copy-done.46, bf16[512,256]{1,0:T(8,128)(2,1)} %copy-done.49, bf16[512,256]{1,0:T(8,128)(2,1)} %copy-done.48, bf16[512,256]{1,0:T(8,128)(2,1)} %copy-done.47, ...), custom_call_target="tpu_custom_call" | custom-call | flops 54999998464 | tf_op jit(solution)/shard_map/pallas_call | solution.py:440
  577.7 8.0 %shard_map.223 = (bf16[512,512]{1,0:T(8,128)(2,1)S(1)}, bf16[512,512]{1,0:T(8,128)(2,1)S(1)}, f32[256,1024]{1,0:T(8,128)S(1)}, f32[8,1024]{1,0:T(8,128)S(1)}) custom-call(bf16[640,128]{1,0:T(8,128)(2,1)S(1)} %copy-done.27, bf16[640,128]{1,0:T(8,128)(2,1)S(1)} %collective-permute-done.50.p1, bf16[640,128]{1,0:T(8,128)(2,1)S(1)} %collective-permute-done.51.p2, ...), custom_call_target="tpu_custom_call" | custom-call | tf_op jit(solution)/shard_map/pallas_call | solution.py:540
  610.5 7.2 shard_map.226
  621.0 20.1 %collective-permute-done.69.refs_3_ = bf16[2,1024,512]{2,1,0:T(8,128)(2,1)S(1)} collective-permute-done((bf16[2,1024,512]{2,1,0:T(8,128)(2,1)S(1)}, bf16[2,1024,512]{2,1,0:T(8,128)(2,1)S(1)}, u32[]{:S(2)}, u32[]{:S(2)}) %collective-permute-start.69) | collective-permute-done | bytes 2097184 | tf_op jit(solution)/shard_map/ppermute | solution.py:35
  641.7 21.7 %collective-permute-done.68.refs_2_ = bf16[2,1024,512]{2,1,0:T(8,128)(2,1)S(1)} collective-permute-done((bf16[2,1024,512]{2,1,0:T(8,128)(2,1)S(1)}, bf16[2,1024,512]{2,1,0:T(8,128)(2,1)S(1)}, u32[]{:S(2)}, u32[]{:S(2)}) %collective-permute-start.68) | collective-permute-done | bytes 2097184 | tf_op jit(solution)/shard_map/ppermute | solution.py:35
  688.9 13.1 %shard_map.227 = (f32[512,8192]{1,0:T(8,128)}, f32[512,128]{1,0:T(8,128)S(1)}, f32[1024,2048]{1,0:T(8,128)}) custom-call(s32[2]{0:T(128)S(1)} %copy-done.33, bf16[512,8192]{1,0:T(8,128)(2,1)} %bitcast.78, f32[512,1]{1,0:T(8,128)S(1)} %copy-done.6, bf16[2,1024,512]{2,1,0:T(8,128)(2,1)S(1)} %pad_maximum_fusion.4.refs_0_, bf16[2,1024,512]{2,1,0:T(8,128)(2,1)S(1)} %copy-done.35, ...), custom_call_target="tpu_custom_call" | custom-call | flops 8000000000 | tf_op jit(solution)/shard_map/pallas_call | solution.py:987
  703.7 9.7 %collective-permute-done.74.refs_2_ = bf16[2,624,512]{2,1,0:T(8,128)(2,1)S(1)} collective-permute-done((bf16[2,624,512]{2,1,0:T(8,128)(2,1)S(1)}, bf16[2,624,512]{2,1,0:T(8,128)(2,1)S(1)}, u32[]{:S(2)}, u32[]{:S(2)}) %collective-permute-start.74) | collective-permute-done | bytes 1277984 | tf_op jit(solution)/shard_map/ppermute | solution.py:35
  713.4 9.5 %shard_map.228 = (f32[512,8192]{1,0:T(8,128)}, f32[512,128]{1,0:T(8,128)S(1)}, f32[1024,128]{1,0:T(8,128)}, f32[32,1024]{1,0:T(8,128)}, f32[128,1024]{1,0:T(8,12...) custom-call(s32[2]{0:T(128)S(1)} %copy-done.33, ...), custom_call_target="tpu_custom_call", output_to_operand_aliasing={{0}: (11, {})} | custom-call | flops 8000000000 | tf_op jit(solution)/shard_map/pallas_call | solution.py:987
  (422 shorter events, 291.9 us)
Async XLA Ops:
  7.2 69.0 %all-gather.9.cloned.1.call-start = ((), (), s32[]{:S(2)}) async-start(), calls=%async_computation.8 | async-start | bytes 3194880 | tf_op jit(solution)/shard_map/all_gather | solution.py:1263
  19.6 139.5 %all-gather.11.cloned.1.call-start = ((), (), s32[]{:S(2)}) async-start(), calls=%async_computation.9 | async-start | bytes 5242880 | tf_op jit(solution)/shard_map/all_gather | solution.py:1263
  79.3 133.7 %all-gather.13.cloned.1.call-start = ((), (), s32[]{:S(2)}) async-start(), calls=%async_computation.10 | async-start | bytes 3194880 | tf_op jit(solution)/shard_map/all_gather | solution.py:1263
  123.9 24.9 %collective-permute-start.14 = (bf16[128,2048]{1,0:T(8,128)(2,1)S(1)}, bf16[128,2048]{1,0:T(8,128)(2,1)S(1)}, u32[]{:S(2)}, u32[]{:S(2)}) collective-permute-start(bf16[128,2048]{1,0:T(8,128)(2,1)S(1)} %copy-done.82), channel_id=1, source_target_pairs={{0,8},{4,12},{8,0},{12,4},{1,9},{5,13},{9,1},{13,5},{2,10},{6,14},... | collective-permute-start | bytes 1572872 | tf_op jit(solution)/shard_map/ppermute | solution.py:31
  124.7 24.9 %collective-permute-start.15 = (bf16[128,2048]{1,0:T(8,128)(2,1)S(1)}, bf16[128,2048]{1,0:T(8,128)(2,1)S(1)}, u32[]{:S(2)}, u32[]{:S(2)}) collective-permute-start(bf16[128,2048]{1,0:T(8,128)(2,1)S(1)} %copy-done.82), channel_id=1, source_target_pairs={{0,12},{4,8},{8,4},{12,0},{1,13},{5,9},{9,5},{13,1},{2,14},{6,10},... | collective-permute-start | bytes 1572872 | tf_op jit(solution)/shard_map/ppermute | solution.py:31
  159.1 135.4 %all-gather.15.cloned.1.call-start = ((), (), s32[]{:S(2)}) async-start(), calls=%async_computation.11 | async-start | bytes 5242880 | tf_op jit(solution)/shard_map/all_gather | solution.py:1263
  213.0 227.4 %reduce-scatter.5.cloned.1.call-start = ((), (), s32[]{:S(2)}) async-start(), calls=%async_computation.4 | async-start | bytes 5242880 | tf_op jit(solution)/shard_map/reduce_scatter | solution.py:1290
  213.1 28.4 %collective-permute-start.23 = (bf16[4,624,512]{2,1,0:T(8,128)(2,1)}, bf16[4,624,512]{2,1,0:T(8,128)(2,1)S(1)}, u32[]{:S(2)}, u32[]{:S(2)}) collective-permute-start(bf16[4,624,512]{2,1,0:T(8,128)(2,1)} %bitcast.111), channel_id=1, source_target_pairs={{0,16},{16,0},{1,17},{17,1},{2,18},{18,2},{3,19},{19,3},{4,20},{20... | collective-permute-start | bytes 7667720 | tf_op jit(solution)/shard_map/ppermute | solution.py:31
  294.6 37.0 %collective-permute-start.28 = (bf16[512,2048]{1,0:T(8,128)(2,1)S(1)}, bf16[512,2048]{1,0:T(8,128)(2,1)S(1)}, u32[]{:S(2)}, u32[]{:S(2)}) collective-permute-start(bf16[512,2048]{1,0:T(8,128)(2,1)S(1)} %copy-done.12), channel_id=1, source_target_pairs={{0,16},{16,0},{1,17},{17,1},{2,18},{18,2},{3,19},{19,3},{4,20},{20... | collective-permute-start | bytes 6291464 | tf_op jit(solution)/shard_map/ppermute | solution.py:31
  295.1 36.5 %collective-permute-start.31 = (bf16[512,2048]{1,0:T(8,128)(2,1)}, bf16[512,2048]{1,0:T(8,128)(2,1)}, u32[]{:S(2)}, u32[]{:S(2)}) collective-permute-start(bf16[512,2048]{1,0:T(8,128)(2,1)} %constant_dynamic-update-slice_fusion.d_ref.db_ref), channel_id=1, source_target_pairs={{0,16},{16,0},{1,17},{17,1},{2,18},{18,2},{3,19},{19,3},{4,20},{20... | collective-permute-start | bytes 6291464 | tf_op jit(solution)/shard_map/ppermute | solution.py:31
  341.8 162.7 %reduce-scatter.7.cloned.1.call-start = ((), (), s32[]{:S(2)}) async-start(), calls=%async_computation.5 | async-start | bytes 3194880 | tf_op jit(solution)/shard_map/reduce_scatter | solution.py:1290
  344.5 52.0 %collective-permute-start.35 = (bf16[128,2048]{1,0:T(8,128)(2,1)}, bf16[128,2048]{1,0:T(8,128)(2,1)S(1)}, u32[]{:S(2)}, u32[]{:S(2)}) collective-permute-start(bf16[128,2048]{1,0:T(8,128)(2,1)} %get-tuple-element.237), channel_id=1, source_target_pairs={{0,4},{4,0},{8,12},{12,8},{1,5},{5,1},{9,13},{13,9},{2,6},{6,2},{1... | collective-permute-start | bytes 1572872 | tf_op jit(solution)/shard_map/ppermute | solution.py:31
  346.0 51.1 %collective-permute-start.37 = (bf16[128,2048]{1,0:T(8,128)(2,1)}, bf16[128,2048]{1,0:T(8,128)(2,1)}, u32[]{:S(2)}, u32[]{:S(2)}) collective-permute-start(bf16[128,2048]{1,0:T(8,128)(2,1)} %get-tuple-element.238), channel_id=1, source_target_pairs={{0,12},{4,8},{8,4},{12,0},{1,13},{5,9},{9,5},{13,1},{2,14},{6,10},... | collective-permute-start | bytes 1572872 | tf_op jit(solution)/shard_map/ppermute | solution.py:31
  347.4 49.6 %collective-permute-start.36 = (bf16[128,2048]{1,0:T(8,128)(2,1)S(1)}, bf16[128,2048]{1,0:T(8,128)(2,1)}, u32[]{:S(2)}, u32[]{:S(2)}) collective-permute-start(bf16[128,2048]{1,0:T(8,128)(2,1)S(1)} %get-tuple-element.239), channel_id=1, source_target_pairs={{0,8},{4,12},{8,0},{12,4},{1,9},{5,13},{9,1},{13,5},{2,10},{6,14},... | collective-permute-start | bytes 1572872 | tf_op jit(solution)/shard_map/ppermute | solution.py:31
  423.5 25.4 %collective-permute-start.39 = (bf16[128,2048]{1,0:T(8,128)(2,1)}, bf16[128,2048]{1,0:T(8,128)(2,1)}, u32[]{:S(2)}, u32[]{:S(2)}) collective-permute-start(bf16[128,2048]{1,0:T(8,128)(2,1)} %get-tuple-element.236), channel_id=1, source_target_pairs={{0,8},{4,12},{8,0},{12,4},{1,9},{5,13},{9,1},{13,5},{2,10},{6,14},... | collective-permute-start | bytes 1572872 | tf_op jit(solution)/shard_map/ppermute | solution.py:31
  440.5 154.3 %reduce-scatter.9.cloned.1.call-start = ((), (), s32[]{:S(2)}) async-start(), calls=%async_computation.6 | async-start | bytes 5242880 | tf_op jit(solution)/shard_map/reduce_scatter | solution.py:1290
  457.1 36.4 %collective-permute-start.46 = (bf16[512,2048]{1,0:T(8,128)(2,1)S(1)}, bf16[512,2048]{1,0:T(8,128)(2,1)S(1)}, u32[]{:S(2)}, u32[]{:S(2)}) collective-permute-start(bf16[512,2048]{1,0:T(8,128)(2,1)S(1)} %copy-done.10), channel_id=1, source_target_pairs={{0,16},{16,0},{1,17},{17,1},{2,18},{18,2},{3,19},{19,3},{4,20},{20... | collective-permute-start | bytes 6291464 | tf_op jit(solution)/shard_map/ppermute | solution.py:31
  491.6 26.0 %collective-permute-start.56 = (bf16[2,1024,512]{2,1,0:T(8,128)(2,1)}, bf16[2,1024,512]{2,1,0:T(8,128)(2,1)}, u32[]{:S(2)}, u32[]{:S(2)}) collective-permute-start(bf16[2,1024,512]{2,1,0:T(8,128)(2,1)} %pad_maximum_fusion.3.refs_4_), channel_id=1, source_target_pairs={{16,28},{20,24},{24,20},{28,16},{17,29},{21,25},{25,21},{29,17},{1... | collective-permute-start | bytes 6291464 | tf_op jit(solution)/shard_map/ppermute | solution.py:35
  504.5 161.7 %reduce-scatter.11.cloned.1.call-start = ((), (), s32[]{:S(2)}) async-start(), calls=%async_computation.7 | async-start | bytes 3194880 | tf_op jit(solution)/shard_map/reduce_scatter | solution.py:1290
  508.8 55.8 %collective-permute-start.55 = (bf16[2,1024,512]{2,1,0:T(8,128)(2,1)}, bf16[2,1024,512]{2,1,0:T(8,128)(2,1)}, u32[]{:S(2)}, u32[]{:S(2)}) collective-permute-start(bf16[2,1024,512]{2,1,0:T(8,128)(2,1)} %pad_maximum_fusion.3.refs_4_), channel_id=1, source_target_pairs={{16,24},{20,28},{24,16},{28,20},{17,25},{21,29},{25,17},{29,21},{1... | collective-permute-start | bytes 6291464 | tf_op jit(solution)/shard_map/ppermute | solution.py:35
  510.7 55.3 %collective-permute-start.54 = (bf16[2,1024,512]{2,1,0:T(8,128)(2,1)}, bf16[2,1024,512]{2,1,0:T(8,128)(2,1)}, u32[]{:S(2)}, u32[]{:S(2)}) collective-permute-start(bf16[2,1024,512]{2,1,0:T(8,128)(2,1)} %pad_maximum_fusion.3.refs_4_), channel_id=1, source_target_pairs={{16,20},{20,16},{24,28},{28,24},{17,21},{21,17},{25,29},{29,25},{1... | collective-permute-start | bytes 6291464 | tf_op jit(solution)/shard_map/ppermute | solution.py:35
  514.0 52.6 %collective-permute-start.60 = (bf16[2,624,512]{2,1,0:T(8,128)(2,1)}, bf16[2,624,512]{2,1,0:T(8,128)(2,1)}, u32[]{:S(2)}, u32[]{:S(2)}) collective-permute-start(bf16[2,624,512]{2,1,0:T(8,128)(2,1)} %pad_maximum_fusion.5.refs_4_), channel_id=1, source_target_pairs={{16,28},{20,24},{24,20},{28,16},{17,29},{21,25},{25,21},{29,17},{1... | collective-permute-start | bytes 3833864 | tf_op jit(solution)/shard_map/ppermute | solution.py:35
  515.9 52.3 %collective-permute-start.59 = (bf16[2,624,512]{2,1,0:T(8,128)(2,1)}, bf16[2,624,512]{2,1,0:T(8,128)(2,1)}, u32[]{:S(2)}, u32[]{:S(2)}) collective-permute-start(bf16[2,624,512]{2,1,0:T(8,128)(2,1)} %pad_maximum_fusion.5.refs_4_), channel_id=1, source_target_pairs={{16,24},{20,28},{24,16},{28,20},{17,25},{21,29},{25,17},{29,21},{1... | collective-permute-start | bytes 3833864 | tf_op jit(solution)/shard_map/ppermute | solution.py:35
  517.6 50.6 %collective-permute-start.58 = (bf16[2,624,512]{2,1,0:T(8,128)(2,1)}, bf16[2,624,512]{2,1,0:T(8,128)(2,1)}, u32[]{:S(2)}, u32[]{:S(2)}) collective-permute-start(bf16[2,624,512]{2,1,0:T(8,128)(2,1)} %pad_maximum_fusion.5.refs_4_), channel_id=1, source_target_pairs={{16,20},{20,16},{24,28},{28,24},{17,21},{21,17},{25,29},{29,25},{1... | collective-permute-start | bytes 3833864 | tf_op jit(solution)/shard_map/ppermute | solution.py:35
  600.8 40.3 %collective-permute-start.69 = (bf16[2,1024,512]{2,1,0:T(8,128)(2,1)S(1)}, bf16[2,1024,512]{2,1,0:T(8,128)(2,1)S(1)}, u32[]{:S(2)}, u32[]{:S(2)}) collective-permute-start(bf16[2,1024,512]{2,1,0:T(8,128)(2,1)S(1)} %pad_maximum_fusion.4.refs_0_), channel_id=1, source_target_pairs={{0,12},{4,8},{8,4},{12,0},{1,13},{5,9},{9,5},{13,1},{2,14},{6,10},... | collective-permute-start | bytes 6291464 | tf_op jit(solution)/shard_map/ppermute | solution.py:35
  604.4 59.1 %collective-permute-start.68 = (bf16[2,1024,512]{2,1,0:T(8,128)(2,1)S(1)}, bf16[2,1024,512]{2,1,0:T(8,128)(2,1)S(1)}, u32[]{:S(2)}, u32[]{:S(2)}) collective-permute-start(bf16[2,1024,512]{2,1,0:T(8,128)(2,1)S(1)} %pad_maximum_fusion.4.refs_0_), channel_id=1, source_target_pairs={{0,8},{4,12},{8,0},{12,4},{1,9},{5,13},{9,1},{13,5},{2,10},{6,14},... | collective-permute-start | bytes 6291464 | tf_op jit(solution)/shard_map/ppermute | solution.py:35
  607.0 57.9 %collective-permute-start.67 = (bf16[2,1024,512]{2,1,0:T(8,128)(2,1)S(1)}, bf16[2,1024,512]{2,1,0:T(8,128)(2,1)S(1)}, u32[]{:S(2)}, u32[]{:S(2)}) collective-permute-start(bf16[2,1024,512]{2,1,0:T(8,128)(2,1)S(1)} %pad_maximum_fusion.4.refs_0_), channel_id=1, source_target_pairs={{0,4},{4,0},{8,12},{12,8},{1,5},{5,1},{9,13},{13,9},{2,6},{6,2},{1... | collective-permute-start | bytes 6291464 | tf_op jit(solution)/shard_map/ppermute | solution.py:35
  618.9 51.8 %collective-permute-start.63 = (bf16[128,2048]{1,0:T(8,128)(2,1)}, bf16[128,2048]{1,0:T(8,128)(2,1)}, u32[]{:S(2)}, u32[]{:S(2)}) collective-permute-start(bf16[128,2048]{1,0:T(8,128)(2,1)} %get-tuple-element.231), channel_id=1, source_target_pairs={{0,4},{4,0},{8,12},{12,8},{1,5},{5,1},{9,13},{13,9},{2,6},{6,2},{1... | collective-permute-start | bytes 1572872 | tf_op jit(solution)/shard_map/ppermute | solution.py:31
  619.7 55.2 %collective-permute-start.65 = (bf16[128,2048]{1,0:T(8,128)(2,1)}, bf16[128,2048]{1,0:T(8,128)(2,1)}, u32[]{:S(2)}, u32[]{:S(2)}) collective-permute-start(bf16[128,2048]{1,0:T(8,128)(2,1)} %get-tuple-element.232), channel_id=1, source_target_pairs={{0,12},{4,8},{8,4},{12,0},{1,13},{5,9},{9,5},{13,1},{2,14},{6,10},... | collective-permute-start | bytes 1572872 | tf_op jit(solution)/shard_map/ppermute | solution.py:31
  641.1 33.8 %collective-permute-start.64 = (bf16[128,2048]{1,0:T(8,128)(2,1)}, bf16[128,2048]{1,0:T(8,128)(2,1)}, u32[]{:S(2)}, u32[]{:S(2)}) collective-permute-start(bf16[128,2048]{1,0:T(8,128)(2,1)} %get-tuple-element.233), channel_id=1, source_target_pairs={{0,8},{4,12},{8,0},{12,4},{1,9},{5,13},{9,1},{13,5},{2,10},{6,14},... | collective-permute-start | bytes 1572872 | tf_op jit(solution)/shard_map/ppermute | solution.py:31
  683.1 30.3 %collective-permute-start.74 = (bf16[2,624,512]{2,1,0:T(8,128)(2,1)S(1)}, bf16[2,624,512]{2,1,0:T(8,128)(2,1)S(1)}, u32[]{:S(2)}, u32[]{:S(2)}) collective-permute-start(bf16[2,624,512]{2,1,0:T(8,128)(2,1)S(1)} %pad_maximum_fusion.6.refs_0_), channel_id=1, source_target_pairs={{0,8},{4,12},{8,0},{12,4},{1,9},{5,13},{9,1},{13,5},{2,10},{6,14},... | collective-permute-start | bytes 3833864 | tf_op jit(solution)/shard_map/ppermute | solution.py:35
  685.7 27.7 %collective-permute-start.73 = (bf16[2,624,512]{2,1,0:T(8,128)(2,1)S(1)}, bf16[2,624,512]{2,1,0:T(8,128)(2,1)S(1)}, u32[]{:S(2)}, u32[]{:S(2)}) collective-permute-start(bf16[2,624,512]{2,1,0:T(8,128)(2,1)S(1)} %pad_maximum_fusion.6.refs_0_), channel_id=1, source_target_pairs={{0,4},{4,0},{8,12},{12,8},{1,5},{5,1},{9,13},{13,9},{2,6},{6,2},{1... | collective-permute-start | bytes 3833864 | tf_op jit(solution)/shard_map/ppermute | solution.py:35
  (151 other events, 2136.7 us)
Sparse Core Ops, SparseCore 0:
  19.8 56.3 all-gather.8
  79.4 79.6 all-gather.10
  160.7 52.2 all-gather.12
  215.0 79.5 all-gather.14
  341.9 75.2 reduce-scatter.4
  440.6 49.5 reduce-scatter.6
  504.6 76.0 reduce-scatter.8
  595.0 49.4 reduce-scatter.10

commit v6 on v5

--- a/solution.py
+++ b/solution.py
@@ -293,7 +293,7 @@
                 y_i[b, now, :] = ys[b]
         return carry
 
-    lax.fori_loop(0, length, forward_step, 0, unroll=2)
+    lax.fori_loop(0, length, forward_step, 0, unroll=4)
 
     if y_out is not None:
         for j in range(n_slots):
@@ -338,7 +338,7 @@
             p_i[b, now, :] = b_sum[b]
         return carry
 
-    lax.fori_loop(0, length, backward_step, 0, unroll=2)
+    lax.fori_loop(0, length, backward_step, 0, unroll=4)
 
     source = lax.broadcasted_iota(jnp.int32, (STATE * LANES, LANES), 0) // LANES
     sums = jnp.where(source == lax.broadcasted_iota(jnp.int32, (STATE * LANES, LANES), 1), 1.0, 0.0).astype(BF)
@@ -939,10 +939,14 @@
     def _():
         sum_ref[...] = jnp.zeros(sum_ref.shape, F32)
 
+    total = None
     for at, value in join_values(n_grp, where_ref, parts):
         out_ref[:, at] = value[:rows] * gain_ref[...]
-        sum_ref[...] += value[:rows] * w_ref[:, at].astype(F32)
+        term = value[:rows] * w_ref[:, at].astype(F32)
+        total = term if total is None else total + term
         small[pl.ds(pl.multiple_of(i * part, 16), part), at] = value[rows:]
+
+    sum_ref[...] += total
 
     @pl.when(i == n_dp - 1)
     def _():

time: 741 us -> 740 us (level)
  no operation moved by 1% of the time
where the time goes in v6:
time: 740 us; the launch traced here: 730 us
  waiting for transfers between devices  286 us (39%)
  Pallas kernels  258 us (35%)
  starting transfers between devices  94.8 us (13%)
  local copies, waits for them, and re-layouts  44.9 us (6%)
  other arithmetic  30.6 us (4%)
  between operations  15.5 us (2%)
    ppermute x58, waiting for transfers between devices, swap(): lax.ppermute(value, axis, [(i, i ^ shift) for i in range(lax.axis_size(ax...  193 us
    pallas_call x2, Pallas kernels, rec(): call(partial(rec_body, True, keep_y, n_slots, length, width), tuple(outs)...  88.4 us
    ppermute x18, waiting for transfers between devices, directed(): return lax.ppermute(value, axis, pairs)  54.9 us
    ppermute x58, starting transfers between devices, swap(): lax.ppermute(value, axis, [(i, i ^ shift) for i in range(lax.axis_size(ax...  51.3 us
    pallas_call x8, Pallas kernels, flat_call(): call(body, out_shape, grid=(1,), in_specs=[(specs or {}).get(n, whole(v))...  49.2 us
    ppermute x18, starting transfers between devices, directed(): return lax.ppermute(value, axis, pairs)  42.6 us
    unnamed x202, local copies, waits for them, and re-layouts  38.6 us
    all_gather x4, waiting for transfers between devices, line(): return lax.all_gather(value, 'dp', axis=0)  38 us
  transfers between devices with their start and end apart: 84, of which 40 were waited for; matrix products, arithmetic and copies ran while one was open for 5% of the time, Pallas kernels for 32%

profile of v6, /device:TPU:0, one launch (start us, length us, event | category | flops | bytes accessed | tf_op | source)
XLA Modules:
  0.0 729.7 jit_solution(3024205661223178452)
XLA Ops:
  38.3 9.5 %collective-permute-done.6 = bf16[128,2048]{1,0:T(8,128)(2,1)S(1)} collective-permute-done((bf16[128,2048]{1,0:T(8,128)(2,1)S(1)}, bf16[128,2048]{1,0:T(8,128)(2,1)S(1)}, u32[]{:S(2)}, u32[]{:S(2)}) %collective-permute-start.6) | collective-permute-done | bytes 524320 | tf_op jit(solution)/shard_map/ppermute | solution.py:31
  47.8 10.5 %collective-permute-done.5 = bf16[128,2048]{1,0:T(8,128)(2,1)S(1)} collective-permute-done((bf16[128,2048]{1,0:T(8,128)(2,1)S(1)}, bf16[128,2048]{1,0:T(8,128)(2,1)S(1)}, u32[]{:S(2)}, u32[]{:S(2)}) %collective-permute-start.5) | collective-permute-done | bytes 524320 | tf_op jit(solution)/shard_map/ppermute | solution.py:31
  59.1 17.0 %all-gather.9.cloned.1.call-done = bf16[2496,512]{1,0:T(8,128)(2,1)} async-done(((bf16[624,512]{1,0:T(8,128)(2,1)}), bf16[2496,512]{1,0:T(8,128)(2,1)}) %all-gather.9.cloned.1.call-update) | async-done | bytes 2555920 | tf_op jit(solution)/shard_map/all_gather | solution.py:1267
  81.3 7.5 %shard_map.205 = (f32[512,1024]{1,0:T(8,128)S(1)}, bf16[512,1024]{1,0:T(8,128)(2,1)S(1)}, bf16[512,256]{1,0:T(8,128)(2,1)S(1)}, bf16[256,1024]{1,0:T(8,128)(2,1)...) custom-call(bf16[512,2048]{1,0:T(8,128)(2,1)} %pad_maximum_fusion.a_ref, f32[512,512]{1,0:T(8,128)S(1)} %bitcast.68, ...), custom_call_target="tpu_custom_call" | custom-call | flops 8000000000 | tf_op jit(solution)/shard_map/pallas_call | solution.py:666
  105.9 14.2 %shard_map.206.y_ref = f32[512,1024]{1,0:T(8,128)S(1)} custom-call(bf16[512,256]{1,0:T(8,128)(2,1)S(1)} %get-tuple-element.100.refs_0_, bf16[512,256]{1,0:T(8,128)(2,1)S(1)} %collective-permute-done.10.refs_1_, bf16[512,256]{1,0:T(8,128)(2,1)S(1)} %collective-permute-done.11.refs_2_, bf16[512,256]{1,0:T(8,128)(2,1)S(1)} %collective-permute-done.12.refs_3_, ...), custom_call_target="tpu_custom_call" | custom-call | flops 20000000000 | tf_op jit(solution)/shard_map/pallas_call | solution.py:413
  126.0 10.5 %collective-permute-done.13 = bf16[128,2048]{1,0:T(8,128)(2,1)S(1)} collective-permute-done((bf16[128,2048]{1,0:T(8,128)(2,1)S(1)}, bf16[128,2048]{1,0:T(8,128)(2,1)S(1)}, u32[]{:S(2)}, u32[]{:S(2)}) %collective-permute-start.13) | collective-permute-done | bytes 524320 | tf_op jit(solution)/shard_map/ppermute | solution.py:31
  137.3 10.7 %collective-permute-done.14 = bf16[128,2048]{1,0:T(8,128)(2,1)S(1)} collective-permute-done((bf16[128,2048]{1,0:T(8,128)(2,1)S(1)}, bf16[128,2048]{1,0:T(8,128)(2,1)S(1)}, u32[]{:S(2)}, u32[]{:S(2)}) %collective-permute-start.14) | collective-permute-done | bytes 524320 | tf_op jit(solution)/shard_map/ppermute | solution.py:31
  149.7 9.4 %all-gather.11.cloned.1.call-done = bf16[4096,512]{1,0:T(8,128)(2,1)} async-done(((bf16[1024,512]{1,0:T(8,128)(2,1)}), bf16[4096,512]{1,0:T(8,128)(2,1)}) %all-gather.11.cloned.1.call-update) | async-done | bytes 4194320 | tf_op jit(solution)/shard_map/all_gather | solution.py:1267
  159.4 7.2 collective-permute-done.16.far_ref.q_far
  183.8 11.3 %collective-permute-done.17 = bf16[128,2048]{1,0:T(8,128)(2,1)S(1)} collective-permute-done((bf16[128,2048]{1,0:T(8,128)(2,1)S(1)}, bf16[128,2048]{1,0:T(8,128)(2,1)S(1)}, u32[]{:S(2)}, u32[]{:S(2)}) %collective-permute-start.17) | collective-permute-done | bytes 524320 | tf_op jit(solution)/shard_map/ppermute | solution.py:31
  195.1 11.6 %collective-permute-done.19 = bf16[128,2048]{1,0:T(8,128)(2,1)S(1)} collective-permute-done((bf16[128,2048]{1,0:T(8,128)(2,1)S(1)}, bf16[128,2048]{1,0:T(8,128)(2,1)S(1)}, u32[]{:S(2)}, u32[]{:S(2)}) %collective-permute-start.19) | collective-permute-done | bytes 524320 | tf_op jit(solution)/shard_map/ppermute | solution.py:31
  216.9 12.2 %collective-permute-done.22 = bf16[128,2048]{1,0:T(8,128)(2,1)S(1)} collective-permute-done((bf16[128,2048]{1,0:T(8,128)(2,1)S(1)}, bf16[128,2048]{1,0:T(8,128)(2,1)S(1)}, u32[]{:S(2)}, u32[]{:S(2)}) %collective-permute-start.22) | collective-permute-done | bytes 524320 | tf_op jit(solution)/shard_map/ppermute | solution.py:31
  229.0 10.8 %collective-permute-done.21 = bf16[128,2048]{1,0:T(8,128)(2,1)S(1)} collective-permute-done((bf16[128,2048]{1,0:T(8,128)(2,1)S(1)}, bf16[128,2048]{1,0:T(8,128)(2,1)S(1)}, u32[]{:S(2)}, u32[]{:S(2)}) %collective-permute-start.21) | collective-permute-done | bytes 524320 | tf_op jit(solution)/shard_map/ppermute | solution.py:31
  243.0 7.5 %shard_map.209 = (f32[512,1024]{1,0:T(8,128)S(1)}, bf16[512,1024]{1,0:T(8,128)(2,1)S(1)}, bf16[512,256]{1,0:T(8,128)(2,1)S(1)}, bf16[256,1024]{1,0:T(8,128)(2,1)...) custom-call(bf16[512,2048]{1,0:T(8,128)(2,1)} %pad_maximum_fusion.1.a_ref, f32[512,512]{1,0:T(8,128)S(1)} %bitcast.70, ...), custom_call_target="tpu_custom_call" | custom-call | flops 8000000000 | tf_op jit(solution)/shard_map/pallas_call | solution.py:666
  267.6 14.6 %shard_map.210.y_ref = f32[512,1024]{1,0:T(8,128)S(1)} custom-call(bf16[512,256]{1,0:T(8,128)(2,1)S(1)} %get-tuple-element.111.refs_0_, bf16[512,256]{1,0:T(8,128)(2,1)S(1)} %collective-permute-done.24.refs_1_, bf16[512,256]{1,0:T(8,128)(2,1)S(1)} %collective-permute-done.25.refs_2_, bf16[512,256]{1,0:T(8,128)(2,1)S(1)} %collective-permute-done.26.refs_3_, ...), custom_call_target="tpu_custom_call" | custom-call | flops 20000000000 | tf_op jit(solution)/shard_map/pallas_call | solution.py:413
  295.1 12.8 %collective-permute-done.27.far_ref.q_far = bf16[4,1024,512]{2,1,0:T(8,128)(2,1)S(1)} collective-permute-done((bf16[4,1024,512]{2,1,0:T(8,128)(2,1)}, bf16[4,1024,512]{2,1,0:T(8,128)(2,1)S(1)}, u32[]{:S(2)}, u32[]{:S(2)}) %collective-permute-start.27) | collective-permute-done | bytes 4194336 | tf_op jit(solution)/shard_map/ppermute | solution.py:31
  332.9 8.8 %shard_map.213 = bf16[4,1024,512]{2,1,0:T(8,128)(2,1)} custom-call(bf16[512,2048]{1,0:T(8,128)(2,1)S(1)} %copy-done.12, bf16[512,2048]{1,0:T(8,128)(2,1)} %copy-done.95, bf16[512,512]{1,0:T(8,128)(2,1)S(1)} %get-tuple-element.120.dg_ref.dg_near, bf16[512,512]{1,0:T(8,128)(2,1)S(1)} %collective-permute-done.29.dg_come, ...), custom_call_target="tpu_custom_call" | custom-call | flops 8000000000 | tf_op jit(solution)/shard_map/pallas_call | solution.py:884
  348.0 44.3 %shard_map.215 = (bf16[512,128]{1,0:T(8,128)(2,1)}, f32[512,1024]{1,0:T(8,128)}, bf16[640,128]{1,0:T(8,128)(2,1)}, f32[128,1024]{1,0:T(8,128)}, f32[8,1024]{1,0:T(8,128)}) custom-call(bf16[512,256]{1,0:T(8,128)(2,1)} %copy-done.50, bf16[512,256]{1,0:T(8,128)(2,1)} %copy-done.53, bf16[512,256]{1,0:T(8,128)(2,1)} %copy-done.52, bf16[512,256]{1,0:T(8,128)(2,1)} %copy-done.51, ...), custom_call_target="tpu_custom_call" | custom-call | flops 54999998464 | tf_op jit(solution)/shard_map/pallas_call | solution.py:440
  402.6 8.0 %shard_map.216 = (bf16[512,512]{1,0:T(8,128)(2,1)S(1)}, bf16[512,512]{1,0:T(8,128)(2,1)S(1)}, f32[256,1024]{1,0:T(8,128)S(1)}, f32[8,1024]{1,0:T(8,128)S(1)}) custom-call(bf16[640,128]{1,0:T(8,128)(2,1)S(1)} %copy-done.26, bf16[640,128]{1,0:T(8,128)(2,1)S(1)} %collective-permute-done.32.p1, bf16[640,128]{1,0:T(8,128)(2,1)S(1)} %collective-permute-done.33.p2, ...), custom_call_target="tpu_custom_call" | custom-call | tf_op jit(solution)/shard_map/pallas_call | solution.py:540
  410.7 7.3 shard_map.217
  423.0 10.8 %collective-permute-done.38 = bf16[128,2048]{1,0:T(8,128)(2,1)S(1)} collective-permute-done((bf16[128,2048]{1,0:T(8,128)(2,1)S(1)}, bf16[128,2048]{1,0:T(8,128)(2,1)S(1)}, u32[]{:S(2)}, u32[]{:S(2)}) %collective-permute-start.38) | collective-permute-done | bytes 524320 | tf_op jit(solution)/shard_map/ppermute | solution.py:31
  456.2 12.3 %collective-permute-done.43 = bf16[128,2048]{1,0:T(8,128)(2,1)S(1)} collective-permute-done((bf16[128,2048]{1,0:T(8,128)(2,1)S(1)}, bf16[128,2048]{1,0:T(8,128)(2,1)S(1)}, u32[]{:S(2)}, u32[]{:S(2)}) %collective-permute-start.43) | collective-permute-done | bytes 524320 | tf_op jit(solution)/shard_map/ppermute | solution.py:31
  468.5 9.5 %collective-permute-done.42 = bf16[128,2048]{1,0:T(8,128)(2,1)S(1)} collective-permute-done((bf16[128,2048]{1,0:T(8,128)(2,1)S(1)}, bf16[128,2048]{1,0:T(8,128)(2,1)S(1)}, u32[]{:S(2)}, u32[]{:S(2)}) %collective-permute-start.42) | collective-permute-done | bytes 524320 | tf_op jit(solution)/shard_map/ppermute | solution.py:31
  494.8 8.8 %shard_map.221 = bf16[4,1024,512]{2,1,0:T(8,128)(2,1)} custom-call(bf16[512,2048]{1,0:T(8,128)(2,1)S(1)} %copy-done.10, bf16[512,2048]{1,0:T(8,128)(2,1)} %copy-done.94, bf16[512,512]{1,0:T(8,128)(2,1)S(1)} %get-tuple-element.144.dg_ref.dg_near, bf16[512,512]{1,0:T(8,128)(2,1)S(1)} %collective-permute-done.47.dg_come, bf16[512,512]{1,0:T(8,128)(2,1)S(1)} %copy-done.63, ...), custom_call_target="tpu_custom_call" | custom-call | flops 8000000000 | tf_op jit(solution)/shard_map/pallas_call | solution.py:884
  518.2 44.1 %shard_map.222 = (bf16[512,128]{1,0:T(8,128)(2,1)}, f32[512,1024]{1,0:T(8,128)}, bf16[640,128]{1,0:T(8,128)(2,1)}, f32[128,1024]{1,0:T(8,128)}, f32[8,1024]{1,0:T(8,128)}) custom-call(bf16[512,256]{1,0:T(8,128)(2,1)} %copy-done.46, bf16[512,256]{1,0:T(8,128)(2,1)} %copy-done.49, bf16[512,256]{1,0:T(8,128)(2,1)} %copy-done.48, bf16[512,256]{1,0:T(8,128)(2,1)} %copy-done.47, ...), custom_call_target="tpu_custom_call" | custom-call | flops 54999998464 | tf_op jit(solution)/shard_map/pallas_call | solution.py:440
  576.7 8.0 %shard_map.223 = (bf16[512,512]{1,0:T(8,128)(2,1)S(1)}, bf16[512,512]{1,0:T(8,128)(2,1)S(1)}, f32[256,1024]{1,0:T(8,128)S(1)}, f32[8,1024]{1,0:T(8,128)S(1)}) custom-call(bf16[640,128]{1,0:T(8,128)(2,1)S(1)} %copy-done.27, bf16[640,128]{1,0:T(8,128)(2,1)S(1)} %collective-permute-done.50.p1, bf16[640,128]{1,0:T(8,128)(2,1)S(1)} %collective-permute-done.51.p2, ...), custom_call_target="tpu_custom_call" | custom-call | tf_op jit(solution)/shard_map/pallas_call | solution.py:540
  609.5 7.2 shard_map.226
  620.1 20.2 %collective-permute-done.69.refs_3_ = bf16[2,1024,512]{2,1,0:T(8,128)(2,1)S(1)} collective-permute-done((bf16[2,1024,512]{2,1,0:T(8,128)(2,1)S(1)}, bf16[2,1024,512]{2,1,0:T(8,128)(2,1)S(1)}, u32[]{:S(2)}, u32[]{:S(2)}) %collective-permute-start.69) | collective-permute-done | bytes 2097184 | tf_op jit(solution)/shard_map/ppermute | solution.py:35
  640.8 21.8 %collective-permute-done.68.refs_2_ = bf16[2,1024,512]{2,1,0:T(8,128)(2,1)S(1)} collective-permute-done((bf16[2,1024,512]{2,1,0:T(8,128)(2,1)S(1)}, bf16[2,1024,512]{2,1,0:T(8,128)(2,1)S(1)}, u32[]{:S(2)}, u32[]{:S(2)}) %collective-permute-start.68) | collective-permute-done | bytes 2097184 | tf_op jit(solution)/shard_map/ppermute | solution.py:35
  688.0 13.1 %shard_map.227 = (f32[512,8192]{1,0:T(8,128)}, f32[512,128]{1,0:T(8,128)S(1)}, f32[1024,2048]{1,0:T(8,128)}) custom-call(s32[2]{0:T(128)S(1)} %copy-done.33, bf16[512,8192]{1,0:T(8,128)(2,1)} %bitcast.78, f32[512,1]{1,0:T(8,128)S(1)} %copy-done.6, bf16[2,1024,512]{2,1,0:T(8,128)(2,1)S(1)} %pad_maximum_fusion.4.refs_0_, bf16[2,1024,512]{2,1,0:T(8,128)(2,1)S(1)} %copy-done.35, ...), custom_call_target="tpu_custom_call" | custom-call | flops 8000000000 | tf_op jit(solution)/shard_map/pallas_call | solution.py:991
  702.8 9.7 %collective-permute-done.74.refs_2_ = bf16[2,624,512]{2,1,0:T(8,128)(2,1)S(1)} collective-permute-done((bf16[2,624,512]{2,1,0:T(8,128)(2,1)S(1)}, bf16[2,624,512]{2,1,0:T(8,128)(2,1)S(1)}, u32[]{:S(2)}, u32[]{:S(2)}) %collective-permute-start.74) | collective-permute-done | bytes 1277984 | tf_op jit(solution)/shard_map/ppermute | solution.py:35
  712.5 9.4 %shard_map.228 = (f32[512,8192]{1,0:T(8,128)}, f32[512,128]{1,0:T(8,128)S(1)}, f32[1024,128]{1,0:T(8,128)}, f32[32,1024]{1,0:T(8,128)}, f32[128,1024]{1,0:T(8,12...) custom-call(s32[2]{0:T(128)S(1)} %copy-done.33, ...), custom_call_target="tpu_custom_call", output_to_operand_aliasing={{0}: (11, {})} | custom-call | flops 8000000000 | tf_op jit(solution)/shard_map/pallas_call | solution.py:991
  (422 shorter events, 293.5 us)
Async XLA Ops:
  7.2 69.0 %all-gather.9.cloned.1.call-start = ((), (), s32[]{:S(2)}) async-start(), calls=%async_computation.8 | async-start | bytes 3194880 | tf_op jit(solution)/shard_map/all_gather | solution.py:1267
  19.6 139.5 %all-gather.11.cloned.1.call-start = ((), (), s32[]{:S(2)}) async-start(), calls=%async_computation.9 | async-start | bytes 5242880 | tf_op jit(solution)/shard_map/all_gather | solution.py:1267
  79.3 133.7 %all-gather.13.cloned.1.call-start = ((), (), s32[]{:S(2)}) async-start(), calls=%async_computation.10 | async-start | bytes 3194880 | tf_op jit(solution)/shard_map/all_gather | solution.py:1267
  123.1 24.9 %collective-permute-start.14 = (bf16[128,2048]{1,0:T(8,128)(2,1)S(1)}, bf16[128,2048]{1,0:T(8,128)(2,1)S(1)}, u32[]{:S(2)}, u32[]{:S(2)}) collective-permute-start(bf16[128,2048]{1,0:T(8,128)(2,1)S(1)} %copy-done.82), channel_id=1, source_target_pairs={{0,8},{4,12},{8,0},{12,4},{1,9},{5,13},{9,1},{13,5},{2,10},{6,14},... | collective-permute-start | bytes 1572872 | tf_op jit(solution)/shard_map/ppermute | solution.py:31
  123.9 24.9 %collective-permute-start.15 = (bf16[128,2048]{1,0:T(8,128)(2,1)S(1)}, bf16[128,2048]{1,0:T(8,128)(2,1)S(1)}, u32[]{:S(2)}, u32[]{:S(2)}) collective-permute-start(bf16[128,2048]{1,0:T(8,128)(2,1)S(1)} %copy-done.82), channel_id=1, source_target_pairs={{0,12},{4,8},{8,4},{12,0},{1,13},{5,9},{9,5},{13,1},{2,14},{6,10},... | collective-permute-start | bytes 1572872 | tf_op jit(solution)/shard_map/ppermute | solution.py:31
  159.1 135.4 %all-gather.15.cloned.1.call-start = ((), (), s32[]{:S(2)}) async-start(), calls=%async_computation.11 | async-start | bytes 5242880 | tf_op jit(solution)/shard_map/all_gather | solution.py:1267
  213.0 226.4 %reduce-scatter.5.cloned.1.call-start = ((), (), s32[]{:S(2)}) async-start(), calls=%async_computation.4 | async-start | bytes 5242880 | tf_op jit(solution)/shard_map/reduce_scatter | solution.py:1294
  213.1 28.4 %collective-permute-start.23 = (bf16[4,624,512]{2,1,0:T(8,128)(2,1)}, bf16[4,624,512]{2,1,0:T(8,128)(2,1)S(1)}, u32[]{:S(2)}, u32[]{:S(2)}) collective-permute-start(bf16[4,624,512]{2,1,0:T(8,128)(2,1)} %bitcast.111), channel_id=1, source_target_pairs={{0,16},{16,0},{1,17},{17,1},{2,18},{18,2},{3,19},{19,3},{4,20},{20... | collective-permute-start | bytes 7667720 | tf_op jit(solution)/shard_map/ppermute | solution.py:31
  294.6 37.0 %collective-permute-start.28 = (bf16[512,2048]{1,0:T(8,128)(2,1)S(1)}, bf16[512,2048]{1,0:T(8,128)(2,1)S(1)}, u32[]{:S(2)}, u32[]{:S(2)}) collective-permute-start(bf16[512,2048]{1,0:T(8,128)(2,1)S(1)} %copy-done.12), channel_id=1, source_target_pairs={{0,16},{16,0},{1,17},{17,1},{2,18},{18,2},{3,19},{19,3},{4,20},{20... | collective-permute-start | bytes 6291464 | tf_op jit(solution)/shard_map/ppermute | solution.py:31
  295.1 36.5 %collective-permute-start.31 = (bf16[512,2048]{1,0:T(8,128)(2,1)}, bf16[512,2048]{1,0:T(8,128)(2,1)}, u32[]{:S(2)}, u32[]{:S(2)}) collective-permute-start(bf16[512,2048]{1,0:T(8,128)(2,1)} %constant_dynamic-update-slice_fusion.d_ref.db_ref), channel_id=1, source_target_pairs={{0,16},{16,0},{1,17},{17,1},{2,18},{18,2},{3,19},{19,3},{4,20},{20... | collective-permute-start | bytes 6291464 | tf_op jit(solution)/shard_map/ppermute | solution.py:31
  341.8 161.8 %reduce-scatter.7.cloned.1.call-start = ((), (), s32[]{:S(2)}) async-start(), calls=%async_computation.5 | async-start | bytes 3194880 | tf_op jit(solution)/shard_map/reduce_scatter | solution.py:1294
  344.5 50.9 %collective-permute-start.35 = (bf16[128,2048]{1,0:T(8,128)(2,1)}, bf16[128,2048]{1,0:T(8,128)(2,1)S(1)}, u32[]{:S(2)}, u32[]{:S(2)}) collective-permute-start(bf16[128,2048]{1,0:T(8,128)(2,1)} %get-tuple-element.237), channel_id=1, source_target_pairs={{0,4},{4,0},{8,12},{12,8},{1,5},{5,1},{9,13},{13,9},{2,6},{6,2},{1... | collective-permute-start | bytes 1572872 | tf_op jit(solution)/shard_map/ppermute | solution.py:31
  346.0 49.9 %collective-permute-start.37 = (bf16[128,2048]{1,0:T(8,128)(2,1)}, bf16[128,2048]{1,0:T(8,128)(2,1)}, u32[]{:S(2)}, u32[]{:S(2)}) collective-permute-start(bf16[128,2048]{1,0:T(8,128)(2,1)} %get-tuple-element.238), channel_id=1, source_target_pairs={{0,12},{4,8},{8,4},{12,0},{1,13},{5,9},{9,5},{13,1},{2,14},{6,10},... | collective-permute-start | bytes 1572872 | tf_op jit(solution)/shard_map/ppermute | solution.py:31
  347.4 48.4 %collective-permute-start.36 = (bf16[128,2048]{1,0:T(8,128)(2,1)S(1)}, bf16[128,2048]{1,0:T(8,128)(2,1)}, u32[]{:S(2)}, u32[]{:S(2)}) collective-permute-start(bf16[128,2048]{1,0:T(8,128)(2,1)S(1)} %get-tuple-element.239), channel_id=1, source_target_pairs={{0,8},{4,12},{8,0},{12,4},{1,9},{5,13},{9,1},{13,5},{2,10},{6,14},... | collective-permute-start | bytes 1572872 | tf_op jit(solution)/shard_map/ppermute | solution.py:31
  422.4 25.5 %collective-permute-start.39 = (bf16[128,2048]{1,0:T(8,128)(2,1)}, bf16[128,2048]{1,0:T(8,128)(2,1)}, u32[]{:S(2)}, u32[]{:S(2)}) collective-permute-start(bf16[128,2048]{1,0:T(8,128)(2,1)} %get-tuple-element.236), channel_id=1, source_target_pairs={{0,8},{4,12},{8,0},{12,4},{1,9},{5,13},{9,1},{13,5},{2,10},{6,14},... | collective-permute-start | bytes 1572872 | tf_op jit(solution)/shard_map/ppermute | solution.py:31
  439.4 154.5 %reduce-scatter.9.cloned.1.call-start = ((), (), s32[]{:S(2)}) async-start(), calls=%async_computation.6 | async-start | bytes 5242880 | tf_op jit(solution)/shard_map/reduce_scatter | solution.py:1294
  456.2 36.6 %collective-permute-start.46 = (bf16[512,2048]{1,0:T(8,128)(2,1)S(1)}, bf16[512,2048]{1,0:T(8,128)(2,1)S(1)}, u32[]{:S(2)}, u32[]{:S(2)}) collective-permute-start(bf16[512,2048]{1,0:T(8,128)(2,1)S(1)} %copy-done.10), channel_id=1, source_target_pairs={{0,16},{16,0},{1,17},{17,1},{2,18},{18,2},{3,19},{19,3},{4,20},{20... | collective-permute-start | bytes 6291464 | tf_op jit(solution)/shard_map/ppermute | solution.py:31
  490.7 25.8 %collective-permute-start.56 = (bf16[2,1024,512]{2,1,0:T(8,128)(2,1)}, bf16[2,1024,512]{2,1,0:T(8,128)(2,1)}, u32[]{:S(2)}, u32[]{:S(2)}) collective-permute-start(bf16[2,1024,512]{2,1,0:T(8,128)(2,1)} %pad_maximum_fusion.3.refs_4_), channel_id=1, source_target_pairs={{16,28},{20,24},{24,20},{28,16},{17,29},{21,25},{25,21},{29,17},{1... | collective-permute-start | bytes 6291464 | tf_op jit(solution)/shard_map/ppermute | solution.py:35
  503.7 161.6 %reduce-scatter.11.cloned.1.call-start = ((), (), s32[]{:S(2)}) async-start(), calls=%async_computation.7 | async-start | bytes 3194880 | tf_op jit(solution)/shard_map/reduce_scatter | solution.py:1294
  507.7 54.6 %collective-permute-start.55 = (bf16[2,1024,512]{2,1,0:T(8,128)(2,1)}, bf16[2,1024,512]{2,1,0:T(8,128)(2,1)}, u32[]{:S(2)}, u32[]{:S(2)}) collective-permute-start(bf16[2,1024,512]{2,1,0:T(8,128)(2,1)} %pad_maximum_fusion.3.refs_4_), channel_id=1, source_target_pairs={{16,24},{20,28},{24,16},{28,20},{17,25},{21,29},{25,17},{29,21},{1... | collective-permute-start | bytes 6291464 | tf_op jit(solution)/shard_map/ppermute | solution.py:35
  509.7 54.4 %collective-permute-start.54 = (bf16[2,1024,512]{2,1,0:T(8,128)(2,1)}, bf16[2,1024,512]{2,1,0:T(8,128)(2,1)}, u32[]{:S(2)}, u32[]{:S(2)}) collective-permute-start(bf16[2,1024,512]{2,1,0:T(8,128)(2,1)} %pad_maximum_fusion.3.refs_4_), channel_id=1, source_target_pairs={{16,20},{20,16},{24,28},{28,24},{17,21},{21,17},{25,29},{29,25},{1... | collective-permute-start | bytes 6291464 | tf_op jit(solution)/shard_map/ppermute | solution.py:35
  512.9 51.7 %collective-permute-start.60 = (bf16[2,624,512]{2,1,0:T(8,128)(2,1)}, bf16[2,624,512]{2,1,0:T(8,128)(2,1)}, u32[]{:S(2)}, u32[]{:S(2)}) collective-permute-start(bf16[2,624,512]{2,1,0:T(8,128)(2,1)} %pad_maximum_fusion.5.refs_4_), channel_id=1, source_target_pairs={{16,28},{20,24},{24,20},{28,16},{17,29},{21,25},{25,21},{29,17},{1... | collective-permute-start | bytes 3833864 | tf_op jit(solution)/shard_map/ppermute | solution.py:35
  514.8 51.1 %collective-permute-start.59 = (bf16[2,624,512]{2,1,0:T(8,128)(2,1)}, bf16[2,624,512]{2,1,0:T(8,128)(2,1)}, u32[]{:S(2)}, u32[]{:S(2)}) collective-permute-start(bf16[2,624,512]{2,1,0:T(8,128)(2,1)} %pad_maximum_fusion.5.refs_4_), channel_id=1, source_target_pairs={{16,24},{20,28},{24,16},{28,20},{17,25},{21,29},{25,17},{29,21},{1... | collective-permute-start | bytes 3833864 | tf_op jit(solution)/shard_map/ppermute | solution.py:35
  516.5 49.4 %collective-permute-start.58 = (bf16[2,624,512]{2,1,0:T(8,128)(2,1)}, bf16[2,624,512]{2,1,0:T(8,128)(2,1)}, u32[]{:S(2)}, u32[]{:S(2)}) collective-permute-start(bf16[2,624,512]{2,1,0:T(8,128)(2,1)} %pad_maximum_fusion.5.refs_4_), channel_id=1, source_target_pairs={{16,20},{20,16},{24,28},{28,24},{17,21},{21,17},{25,29},{29,25},{1... | collective-permute-start | bytes 3833864 | tf_op jit(solution)/shard_map/ppermute | solution.py:35
  599.9 40.3 %collective-permute-start.69 = (bf16[2,1024,512]{2,1,0:T(8,128)(2,1)S(1)}, bf16[2,1024,512]{2,1,0:T(8,128)(2,1)S(1)}, u32[]{:S(2)}, u32[]{:S(2)}) collective-permute-start(bf16[2,1024,512]{2,1,0:T(8,128)(2,1)S(1)} %pad_maximum_fusion.4.refs_0_), channel_id=1, source_target_pairs={{0,12},{4,8},{8,4},{12,0},{1,13},{5,9},{9,5},{13,1},{2,14},{6,10},... | collective-permute-start | bytes 6291464 | tf_op jit(solution)/shard_map/ppermute | solution.py:35
  603.3 59.3 %collective-permute-start.68 = (bf16[2,1024,512]{2,1,0:T(8,128)(2,1)S(1)}, bf16[2,1024,512]{2,1,0:T(8,128)(2,1)S(1)}, u32[]{:S(2)}, u32[]{:S(2)}) collective-permute-start(bf16[2,1024,512]{2,1,0:T(8,128)(2,1)S(1)} %pad_maximum_fusion.4.refs_0_), channel_id=1, source_target_pairs={{0,8},{4,12},{8,0},{12,4},{1,9},{5,13},{9,1},{13,5},{2,10},{6,14},... | collective-permute-start | bytes 6291464 | tf_op jit(solution)/shard_map/ppermute | solution.py:35
  605.8 58.1 %collective-permute-start.67 = (bf16[2,1024,512]{2,1,0:T(8,128)(2,1)S(1)}, bf16[2,1024,512]{2,1,0:T(8,128)(2,1)S(1)}, u32[]{:S(2)}, u32[]{:S(2)}) collective-permute-start(bf16[2,1024,512]{2,1,0:T(8,128)(2,1)S(1)} %pad_maximum_fusion.4.refs_0_), channel_id=1, source_target_pairs={{0,4},{4,0},{8,12},{12,8},{1,5},{5,1},{9,13},{13,9},{2,6},{6,2},{1... | collective-permute-start | bytes 6291464 | tf_op jit(solution)/shard_map/ppermute | solution.py:35
  618.0 51.9 %collective-permute-start.63 = (bf16[128,2048]{1,0:T(8,128)(2,1)}, bf16[128,2048]{1,0:T(8,128)(2,1)}, u32[]{:S(2)}, u32[]{:S(2)}) collective-permute-start(bf16[128,2048]{1,0:T(8,128)(2,1)} %get-tuple-element.231), channel_id=1, source_target_pairs={{0,4},{4,0},{8,12},{12,8},{1,5},{5,1},{9,13},{13,9},{2,6},{6,2},{1... | collective-permute-start | bytes 1572872 | tf_op jit(solution)/shard_map/ppermute | solution.py:31
  618.5 55.5 %collective-permute-start.65 = (bf16[128,2048]{1,0:T(8,128)(2,1)}, bf16[128,2048]{1,0:T(8,128)(2,1)}, u32[]{:S(2)}, u32[]{:S(2)}) collective-permute-start(bf16[128,2048]{1,0:T(8,128)(2,1)} %get-tuple-element.232), channel_id=1, source_target_pairs={{0,12},{4,8},{8,4},{12,0},{1,13},{5,9},{9,5},{13,1},{2,14},{6,10},... | collective-permute-start | bytes 1572872 | tf_op jit(solution)/shard_map/ppermute | solution.py:31
  640.2 33.8 %collective-permute-start.64 = (bf16[128,2048]{1,0:T(8,128)(2,1)}, bf16[128,2048]{1,0:T(8,128)(2,1)}, u32[]{:S(2)}, u32[]{:S(2)}) collective-permute-start(bf16[128,2048]{1,0:T(8,128)(2,1)} %get-tuple-element.233), channel_id=1, source_target_pairs={{0,8},{4,12},{8,0},{12,4},{1,9},{5,13},{9,1},{13,5},{2,10},{6,14},... | collective-permute-start | bytes 1572872 | tf_op jit(solution)/shard_map/ppermute | solution.py:31
  682.0 30.5 %collective-permute-start.74 = (bf16[2,624,512]{2,1,0:T(8,128)(2,1)S(1)}, bf16[2,624,512]{2,1,0:T(8,128)(2,1)S(1)}, u32[]{:S(2)}, u32[]{:S(2)}) collective-permute-start(bf16[2,624,512]{2,1,0:T(8,128)(2,1)S(1)} %pad_maximum_fusion.6.refs_0_), channel_id=1, source_target_pairs={{0,8},{4,12},{8,0},{12,4},{1,9},{5,13},{9,1},{13,5},{2,10},{6,14},... | collective-permute-start | bytes 3833864 | tf_op jit(solution)/shard_map/ppermute | solution.py:35
  684.5 28.0 %collective-permute-start.73 = (bf16[2,624,512]{2,1,0:T(8,128)(2,1)S(1)}, bf16[2,624,512]{2,1,0:T(8,128)(2,1)S(1)}, u32[]{:S(2)}, u32[]{:S(2)}) collective-permute-start(bf16[2,624,512]{2,1,0:T(8,128)(2,1)S(1)} %pad_maximum_fusion.6.refs_0_), channel_id=1, source_target_pairs={{0,4},{4,0},{8,12},{12,8},{1,5},{5,1},{9,13},{13,9},{2,6},{6,2},{1... | collective-permute-start | bytes 3833864 | tf_op jit(solution)/shard_map/ppermute | solution.py:35
  (151 other events, 2133.4 us)
Sparse Core Ops, SparseCore 0:
  19.8 56.3 all-gather.8
  79.4 79.6 all-gather.10
  160.7 52.2 all-gather.12
  215.0 79.5 all-gather.14
  341.9 75.2 reduce-scatter.4
  439.5 49.5 reduce-scatter.6
  503.8 75.6 reduce-scatter.8
  594.1 49.1 reduce-scatter.10
